TPU v7x, 256 devices: a whole 4x4x8 slice. The times are simulated.
256 devices in a mesh: rows: 16 (over x_hi, y, core), cols: 16 (over z, x_lo).
Axes of the slice: x: 4 (x_hi: 2, x_lo: 2; x = x_hi * 2 + x_lo), y: 4, z: 8, core: 2. Of those that a mesh axis runs over, the one named last changes fastest.
Arguments:
- sky: float32 [512, 131072], P('rows', 'cols'), may hold values from -16 to 16
- thresholds: float32 [5], replicated, may hold values from 0.002 to 1.6
Outputs:
- denoised: float32 [512, 131072], P('rows', 'cols')
- coarse: float32 [512, 131072], P('rows', 'cols')
All inputs are finite; a program needn't handle non-finite values.
Results may differ from a plain program's by a relative error of at most 0.0003.
Values sent between devices are 32-bit elements; how exact they have to be, the bound alone decides.
No kernel may reach another device: no remote copies, remote signals or barrier semaphores. Data moves between devices by JAX's collectives and lax.ppermute only.
A program may use at most 64 MiB of HBM per device.

v0:
```python
import jax
import jax.numpy as jnp
from jax import lax
from jax.sharding import PartitionSpec as P

SCALES = 5


def extended_2(cells, sides, width):
    for axis, dim in sides:
        count = lax.axis_size(axis)
        ends = count - 1
        head = lax.slice_in_dim(cells, 0, width, axis=dim)
        tail = lax.slice_in_dim(cells, cells.shape[dim] - width, cells.shape[dim], axis=dim)
        cells = jnp.concatenate(
            [
                lax.ppermute(tail, axis, [(i, (i + 1) % count) for i in range(ends)]),
                cells,
                lax.ppermute(head, axis, [((i + 1) % count, i) for i in range(ends)]),
            ],
            axis=dim,
        )
    return cells


def five_taps(padded, dilation, count, axis):
    weights = (1.0, 4.0, 6.0, 4.0, 1.0)
    total = None
    for step in range(5):
        begin = step * dilation
        term = weights[step] * lax.slice_in_dim(padded, begin, begin + count, axis=axis)
        total = term if total is None else total + term
    return total / 16.0


def mirror_rims(values, extended, reach, axis, first, final):
    count = values.shape[axis]
    lower = jnp.where(
        first,
        jnp.flip(lax.slice_in_dim(values, 0, reach, axis=axis), axis),
        lax.slice_in_dim(extended, 0, reach, axis=axis),
    )
    upper = jnp.where(
        final,
        jnp.flip(lax.slice_in_dim(values, count - reach, count, axis=axis), axis),
        lax.slice_in_dim(extended, count + reach, count + 2 * reach, axis=axis),
    )
    return jnp.concatenate([lower, values, upper], axis=axis)


def across_columns(values, dilation):
    reach = 2 * dilation
    extended = extended_2(values, (("cols", 1),), reach)
    first = lax.axis_index("cols") == 0
    final = lax.axis_index("cols") == lax.axis_size("cols") - 1
    padded = mirror_rims(values, extended, reach, 1, first, final)
    return five_taps(padded, dilation, values.shape[1], 1)


def down_rows(values, dilation):
    reach = 2 * dilation
    extended = extended_2(values, (("rows", 0),), reach)
    first = lax.axis_index("rows") == 0
    final = lax.axis_index("rows") == lax.axis_size("rows") - 1
    padded = mirror_rims(values, extended, reach, 0, first, final)
    return five_taps(padded, dilation, values.shape[0], 0)


def soft_keep(detail, level):
    return jnp.sign(detail) * jnp.maximum(jnp.abs(detail) - level, 0.0)


def on_device(sky, thresholds):
    plane = sky
    summed = jnp.zeros_like(sky)
    start_scale = 0
    for scale in range(start_scale, SCALES):
        dilation = 2**scale
        across = across_columns(plane, dilation)
        following = down_rows(across, dilation)
        detail = plane - following
        summed = summed + soft_keep(detail, thresholds[scale])
        plane = following
    return (summed + plane, plane)


def solution(mesh):
    placed = (P("rows", "cols"), P())
    return jax.shard_map(
        on_device,
        mesh=mesh,
        in_specs=placed,
        out_specs=(P("rows", "cols"), P("rows", "cols")),
        check_vma=False,
    )
```

profile of v0, /device:TPU:102, one launch (start us, length us, event | category | flops | bytes accessed | tf_op | source)
XLA Modules:
  0.0 219.8 jit_solution(7646989624591875945)
XLA Ops:
  1.4 5.3 %collective-permute-start = (f32[32,2]{1,0:T(8,128)S(1)}, f32[32,2]{1,0:T(8,128)S(1)}, u32[]{:S(2)}, u32[]{:S(2)}) collective-permute-start(f32[32,2]{1,0:T(8,128)S(1)} %get-tuple-element.41), channel_id=1, source_target_pairs={{0,1},{1,2},{2,3},{3,4},{4,5},{5,6},{6,7},{7,8},{8,9},{9,10},{10,1... | collective-permute-start | bytes 776 | tf_op jit(solution)/shard_map/ppermute | solution.py:17
  6.7 1.9 collective-permute-start.1
  8.8 5.7 %collective-permute-done.1 = f32[32,2]{1,0:T(8,128)S(1)} collective-permute-done((f32[32,2]{1,0:T(8,128)S(1)}, f32[32,2]{1,0:T(8,128)S(1)}, u32[]{:S(2)}, u32[]{:S(2)}) %collective-permute-start.1) | collective-permute-done | bytes 288 | tf_op jit(solution)/shard_map/ppermute | solution.py:19
  14.5 4.5 %broadcast_multiply_fusion.8 = (f32[32,8192]{1,0:T(8,128)S(1)}, f32[32,8192]{1,0:T(8,128)S(1)}) fusion(f32[32,2]{1,0:T(8,128)S(1)} %broadcast_select_fusion.16, f32[32,8192]{1,0:T(8,128)} %param.2, f32[32,2]{1,0:T(8,128)S(1)} %broadcast_select_fusion.17), kind=kLoop, calls=%fused_computation.146 | loop fusion | flops 3145728 | bytes 3146240 | tf_op jit(solution)/shard_map/div | solution.py:33
  19.0 1.9 collective-permute-start.2
  21.0 1.6 rev.70
  22.5 7.3 %collective-permute-start.3 = (f32[2,8192]{1,0:T(2,128)S(1)}, f32[2,8192]{1,0:T(2,128)S(1)}, u32[]{:S(2)}, u32[]{:S(2)}) collective-permute-start(f32[2,8192]{1,0:T(2,128)S(1)} %get-tuple-element.38), channel_id=1, source_target_pairs={{16,0},{32,16},{48,32},{64,48},{80,64},{96,80},{112,96},{128,112},... | collective-permute-start | bytes 196616 | tf_op jit(solution)/shard_map/ppermute | solution.py:19
  29.8 1.6 rev.71
  33.4 1.9 collective-permute-start.4
  35.4 3.9 %collective-permute-start.5 = (f32[32,4]{1,0:T(8,128)S(1)}, f32[32,4]{1,0:T(8,128)S(1)}, u32[]{:S(2)}, u32[]{:S(2)}) collective-permute-start(f32[32,4]{1,0:T(8,128)S(1)} %get-tuple-element.36), channel_id=1, source_target_pairs={{1,0},{2,1},{3,2},{4,3},{5,4},{6,5},{7,6},{8,7},{9,8},{10,9},{11,1... | collective-permute-start | bytes 1544 | tf_op jit(solution)/shard_map/ppermute | solution.py:19
  39.4 3.7 %collective-permute-done.5 = f32[32,4]{1,0:T(8,128)S(1)} collective-permute-done((f32[32,4]{1,0:T(8,128)S(1)}, f32[32,4]{1,0:T(8,128)S(1)}, u32[]{:S(2)}, u32[]{:S(2)}) %collective-permute-start.5) | collective-permute-done | bytes 544 | tf_op jit(solution)/shard_map/ppermute | solution.py:19
  43.1 4.5 %broadcast_multiply_fusion.6 = (f32[32,8192]{1,0:T(8,128)S(1)}, f32[32,8192]{1,0:T(8,128)}) fusion(f32[32,4]{1,0:T(8,128)S(1)} %broadcast_select_fusion.14, f32[32,8192]{1,0:T(8,128)} %copy-done.6, f32[32,8192]{1,0:T(8,128)S(1)} %get-tuple-element.19, f32[32,4]{1,0:T(8,128)S(1)} %broadcast_select_fusion.15), kind=kLoop, calls=%fused_computation.144 | loop fusion | flops 3145728 | bytes 4195328 | tf_op jit(solution)/shard_map/div | solution.py:33
  47.7 1.9 collective-permute-start.6
  49.6 1.6 rev.74
  51.2 7.3 %collective-permute-start.7 = (f32[4,8192]{1,0:T(4,128)S(1)}, f32[4,8192]{1,0:T(4,128)S(1)}, u32[]{:S(2)}, u32[]{:S(2)}) collective-permute-start(f32[4,8192]{1,0:T(4,128)S(1)} %get-tuple-element.34), channel_id=1, source_target_pairs={{16,0},{32,16},{48,32},{64,48},{80,64},{96,80},{112,96},{128,112},... | collective-permute-start | bytes 393224 | tf_op jit(solution)/shard_map/ppermute | solution.py:19
  58.4 1.6 rev.75
  60.0 1.1 collective-permute-done.7
  61.1 1.8 broadcast_multiply_fusion.5
  63.0 1.9 collective-permute-start.8
  65.0 3.9 %collective-permute-start.9 = (f32[32,8]{1,0:T(8,128)S(1)}, f32[32,8]{1,0:T(8,128)S(1)}, u32[]{:S(2)}, u32[]{:S(2)}) collective-permute-start(f32[32,8]{1,0:T(8,128)S(1)} %get-tuple-element.32), channel_id=1, source_target_pairs={{1,0},{2,1},{3,2},{4,3},{5,4},{6,5},{7,6},{8,7},{9,8},{10,9},{11,1... | collective-permute-start | bytes 3080 | tf_op jit(solution)/shard_map/ppermute | solution.py:19
  69.0 3.7 %collective-permute-done.9 = f32[32,8]{1,0:T(8,128)S(1)} collective-permute-done((f32[32,8]{1,0:T(8,128)S(1)}, f32[32,8]{1,0:T(8,128)S(1)}, u32[]{:S(2)}, u32[]{:S(2)}) %collective-permute-start.9) | collective-permute-done | bytes 1056 | tf_op jit(solution)/shard_map/ppermute | solution.py:19
  72.8 2.1 broadcast_multiply_fusion.4
  74.9 1.9 collective-permute-start.10
  77.9 7.3 %collective-permute-start.11 = (f32[8,8192]{1,0:T(8,128)S(1)}, f32[8,8192]{1,0:T(8,128)S(1)}, u32[]{:S(2)}, u32[]{:S(2)}) collective-permute-start(f32[8,8192]{1,0:T(8,128)S(1)} %get-tuple-element.30), channel_id=1, source_target_pairs={{16,0},{32,16},{48,32},{64,48},{80,64},{96,80},{112,96},{128,112},... | collective-permute-start | bytes 786440 | tf_op jit(solution)/shard_map/ppermute | solution.py:19
  86.3 1.0 broadcast_select_fusion.3
  87.3 1.8 collective-permute-done.11
  89.2 1.6 broadcast_multiply_fusion.3
  91.9 1.9 collective-permute-start.12
  93.9 3.9 %collective-permute-start.13 = (f32[32,16]{1,0:T(8,128)S(1)}, f32[32,16]{1,0:T(8,128)S(1)}, u32[]{:S(2)}, u32[]{:S(2)}) collective-permute-start(f32[32,16]{1,0:T(8,128)S(1)} %get-tuple-element.28), channel_id=1, source_target_pairs={{1,0},{2,1},{3,2},{4,3},{5,4},{6,5},{7,6},{8,7},{9,8},{10,9},{11,1... | collective-permute-start | bytes 6152 | tf_op jit(solution)/shard_map/ppermute | solution.py:19
  97.9 3.7 %collective-permute-done.13 = f32[32,16]{1,0:T(8,128)S(1)} collective-permute-done((f32[32,16]{1,0:T(8,128)S(1)}, f32[32,16]{1,0:T(8,128)S(1)}, u32[]{:S(2)}, u32[]{:S(2)}) %collective-permute-start.13) | collective-permute-done | bytes 2080 | tf_op jit(solution)/shard_map/ppermute | solution.py:19
  101.6 4.7 %broadcast_multiply_fusion.2 = (f32[32,8192]{1,0:T(8,128)S(1)}, f32[32,8192]{1,0:T(8,128)}) fusion(f32[32,16]{1,0:T(8,128)S(1)} %broadcast_select_fusion.10, f32[32,8192]{1,0:T(8,128)} %copy-done.7, f32[32,8192]{1,0:T(8,128)S(1)} %get-tuple-element.11, f32[32,16]{1,0:T(8,128)S(1)} %broadcast_select_fusion.11), kind=kLoop, calls=%fused_computation.140 | loop fusion | flops 3145728 | bytes 4198400 | tf_op jit(solution)/shard_map/div | solution.py:33
  106.3 1.1 fusion.90
  107.4 1.9 collective-permute-start.14
  109.3 22.4 %rev.82 = f32[16,8192]{1,0:T(8,128)S(1)} reverse(f32[16,8192]{1,0:T(8,128)} %get-tuple-element.26), dimensions={0} | reverse | bytes 1048576 | tf_op jit(solution)/shard_map/jit(_flip)/rev | solution.py:40
  131.6 7.2 %collective-permute-start.15 = (f32[16,8192]{1,0:T(8,128)}, f32[16,8192]{1,0:T(8,128)}, u32[]{:S(2)}, u32[]{:S(2)}) collective-permute-start(f32[16,8192]{1,0:T(8,128)} %get-tuple-element.26), channel_id=1, source_target_pairs={{16,0},{32,16},{48,32},{64,48},{80,64},{96,80},{112,96},{128,112},... | collective-permute-start | bytes 1572872 | tf_op jit(solution)/shard_map/ppermute | solution.py:19
  138.9 22.3 %rev.83 = f32[16,8192]{1,0:T(8,128)S(1)} reverse(f32[16,8192]{1,0:T(8,128)} %get-tuple-element.27), dimensions={0} | reverse | bytes 1048576 | tf_op jit(solution)/shard_map/jit(_flip)/rev | solution.py:45
  161.2 1.1 broadcast_select_fusion.1
  162.3 1.2 broadcast_select_fusion
  164.0 1.0 copy-done.5
  165.0 1.9 collective-permute-start.16
  167.0 3.9 %collective-permute-start.17 = (f32[32,32]{1,0:T(8,128)S(1)}, f32[32,32]{1,0:T(8,128)S(1)}, u32[]{:S(2)}, u32[]{:S(2)}) collective-permute-start(f32[32,32]{1,0:T(8,128)S(1)} %get-tuple-element.24), channel_id=1, source_target_pairs={{1,0},{2,1},{3,2},{4,3},{5,4},{6,5},{7,6},{8,7},{9,8},{10,9},{11,1... | collective-permute-start | bytes 12296 | tf_op jit(solution)/shard_map/ppermute | solution.py:19
  171.0 3.7 %collective-permute-done.17 = f32[32,32]{1,0:T(8,128)S(1)} collective-permute-done((f32[32,32]{1,0:T(8,128)S(1)}, f32[32,32]{1,0:T(8,128)S(1)}, u32[]{:S(2)}, u32[]{:S(2)}) %collective-permute-start.17) | collective-permute-done | bytes 4128 | tf_op jit(solution)/shard_map/ppermute | solution.py:19
  174.8 4.7 %broadcast_multiply_fusion = (f32[32,8192]{1,0:T(8,128)}, f32[32,8192]{1,0:T(8,128)S(1)}) fusion(f32[32,32]{1,0:T(8,128)S(1)} %broadcast_select_fusion.8, f32[32,8192]{1,0:T(8,128)} %copy-done.5, f32[32,8192]{1,0:T(8,128)S(1)} %get-tuple-element.7, f32[32,32]{1,0:T(8,128)S(1)} %broadcast_select_fusion.9), kind=kLoop, calls=%fused_computation.138 | loop fusion | flops 3145728 | bytes 4202496 | tf_op jit(solution)/shard_map/div | solution.py:33
  179.4 1.9 collective-permute-start.18
  181.4 7.4 %collective-permute-start.19 = (f32[32,8192]{1,0:T(8,128)}, f32[32,8192]{1,0:T(8,128)}, u32[]{:S(2)}, u32[]{:S(2)}) collective-permute-start(f32[32,8192]{1,0:T(8,128)} %get-tuple-element.4), channel_id=1, source_target_pairs={{16,0},{32,16},{48,32},{64,48},{80,64},{96,80},{112,96},{128,112},... | collective-permute-start | bytes 3145736 | tf_op jit(solution)/shard_map/ppermute | solution.py:19
  189.5 19.4 %reverse.3 = f32[32,8192]{1,0:T(8,128)} reverse(f32[32,8192]{1,0:T(8,128)S(1)} %get-tuple-element.5), dimensions={0} | reverse | bytes 2097152 | tf_op jit(solution)/shard_map/reverse
  208.9 2.2 %multiply_select_fusion.1 = (f32[32,8192]{1,0:T(8,128)S(1)}, f32[32,8192]{1,0:T(8,128)S(1)}) fusion(f32[32,8192]{1,0:T(8,128)} %collective-permute-done.18, f32[32,8192]{1,0:T(8,128)} %reverse.3, pred[]{:T(512)S(6)} %eq.8, f32[32,8192]{1,0:T(8,128)} %collective-permute-done.19, pred[]{:T(512)S(6)} %eq.11), kind=kLoop, calls=%fused_computation.137 | loop fusion | flops 786432 | bytes 5242882 | tf_op jit(solution)/shard_map/jit(_where)/select_n | solution.py:38
  211.7 8.1 %add_add_fusion = (f32[32,8192]{1,0:T(8,128)}, f32[32,8192]{1,0:T(8,128)}) fusion(f32[32,8192]{1,0:T(8,128)S(1)} %copy-done.4, f32[]{:T(128)} %bitcast.4, f32[]{:T(128)} %bitcast.3, f32[]{:T(128)} %bitcast.2, f32[]{:T(128)} %bitcast.1, f32[]{:T(128)} %bitcast, f32[32,8192]{1,0:T(8,128)S(1)} %copy-done.1, f32[32,8192]{1,0:T(8,128)S(1)} %get-tuple-element.15, ...), kind=kLoop, calls=%fused_computation.135 | loop fusion | flops 12845056 | bytes 11534356 | tf_op jit(solution)/shard_map/add | solution.py:84
  (70 shorter events, 8.9 us)
Async XLA Ops:
  1.4 7.4 %collective-permute-start = (f32[32,2]{1,0:T(8,128)S(1)}, f32[32,2]{1,0:T(8,128)S(1)}, u32[]{:S(2)}, u32[]{:S(2)}) collective-permute-start(f32[32,2]{1,0:T(8,128)S(1)} %get-tuple-element.41), channel_id=1, source_target_pairs={{0,1},{1,2},{2,3},{3,4},{4,5},{5,6},{6,7},{7,8},{8,9},{9,10},{10,1... | collective-permute-start | bytes 776 | tf_op jit(solution)/shard_map/ppermute | solution.py:17
  6.7 7.7 %collective-permute-start.1 = (f32[32,2]{1,0:T(8,128)S(1)}, f32[32,2]{1,0:T(8,128)S(1)}, u32[]{:S(2)}, u32[]{:S(2)}) collective-permute-start(f32[32,2]{1,0:T(8,128)S(1)} %get-tuple-element.40), channel_id=1, source_target_pairs={{1,0},{2,1},{3,2},{4,3},{5,4},{6,5},{7,6},{8,7},{9,8},{10,9},{11,1... | collective-permute-start | bytes 776 | tf_op jit(solution)/shard_map/ppermute | solution.py:19
  19.0 12.3 %collective-permute-start.2 = (f32[2,8192]{1,0:T(2,128)S(1)}, f32[2,8192]{1,0:T(2,128)S(1)}, u32[]{:S(2)}, u32[]{:S(2)}) collective-permute-start(f32[2,8192]{1,0:T(2,128)S(1)} %get-tuple-element.39), channel_id=1, source_target_pairs={{0,16},{16,32},{32,48},{48,64},{64,80},{80,96},{96,112},{112,128},... | collective-permute-start | bytes 196616 | tf_op jit(solution)/shard_map/ppermute | solution.py:17
  22.5 9.1 %collective-permute-start.3 = (f32[2,8192]{1,0:T(2,128)S(1)}, f32[2,8192]{1,0:T(2,128)S(1)}, u32[]{:S(2)}, u32[]{:S(2)}) collective-permute-start(f32[2,8192]{1,0:T(2,128)S(1)} %get-tuple-element.38), channel_id=1, source_target_pairs={{16,0},{32,16},{48,32},{64,48},{80,64},{96,80},{112,96},{128,112},... | collective-permute-start | bytes 196616 | tf_op jit(solution)/shard_map/ppermute | solution.py:19
  32.4 1.0 copy-start.6
  32.4 15.2 %copy-start = (f32[32,8192]{1,0:T(8,128)}, f32[32,8192]{1,0:T(8,128)S(1)}, u32[]{:S(2)}) copy-start(f32[32,8192]{1,0:T(8,128)S(1)} %get-tuple-element.19) | copy-start | bytes 3145732
  33.4 6.0 %collective-permute-start.4 = (f32[32,4]{1,0:T(8,128)S(1)}, f32[32,4]{1,0:T(8,128)S(1)}, u32[]{:S(2)}, u32[]{:S(2)}) collective-permute-start(f32[32,4]{1,0:T(8,128)S(1)} %get-tuple-element.37), channel_id=1, source_target_pairs={{0,1},{1,2},{2,3},{3,4},{4,5},{5,6},{6,7},{7,8},{8,9},{9,10},{10,1... | collective-permute-start | bytes 1544 | tf_op jit(solution)/shard_map/ppermute | solution.py:17
  35.4 7.7 %collective-permute-start.5 = (f32[32,4]{1,0:T(8,128)S(1)}, f32[32,4]{1,0:T(8,128)S(1)}, u32[]{:S(2)}, u32[]{:S(2)}) collective-permute-start(f32[32,4]{1,0:T(8,128)S(1)} %get-tuple-element.36), channel_id=1, source_target_pairs={{1,0},{2,1},{3,2},{4,3},{5,4},{6,5},{7,6},{8,7},{9,8},{10,9},{11,1... | collective-permute-start | bytes 1544 | tf_op jit(solution)/shard_map/ppermute | solution.py:19
  47.7 12.3 %collective-permute-start.6 = (f32[4,8192]{1,0:T(4,128)S(1)}, f32[4,8192]{1,0:T(4,128)S(1)}, u32[]{:S(2)}, u32[]{:S(2)}) collective-permute-start(f32[4,8192]{1,0:T(4,128)S(1)} %get-tuple-element.35), channel_id=1, source_target_pairs={{0,16},{16,32},{32,48},{48,64},{64,80},{80,96},{96,112},{112,128},... | collective-permute-start | bytes 393224 | tf_op jit(solution)/shard_map/ppermute | solution.py:17
  51.2 9.9 %collective-permute-start.7 = (f32[4,8192]{1,0:T(4,128)S(1)}, f32[4,8192]{1,0:T(4,128)S(1)}, u32[]{:S(2)}, u32[]{:S(2)}) collective-permute-start(f32[4,8192]{1,0:T(4,128)S(1)} %get-tuple-element.34), channel_id=1, source_target_pairs={{16,0},{32,16},{48,32},{64,48},{80,64},{96,80},{112,96},{128,112},... | collective-permute-start | bytes 393224 | tf_op jit(solution)/shard_map/ppermute | solution.py:19
  63.0 6.0 %collective-permute-start.8 = (f32[32,8]{1,0:T(8,128)S(1)}, f32[32,8]{1,0:T(8,128)S(1)}, u32[]{:S(2)}, u32[]{:S(2)}) collective-permute-start(f32[32,8]{1,0:T(8,128)S(1)} %get-tuple-element.33), channel_id=1, source_target_pairs={{0,1},{1,2},{2,3},{3,4},{4,5},{5,6},{6,7},{7,8},{8,9},{9,10},{10,1... | collective-permute-start | bytes 3080 | tf_op jit(solution)/shard_map/ppermute | solution.py:17
  65.0 7.7 %collective-permute-start.9 = (f32[32,8]{1,0:T(8,128)S(1)}, f32[32,8]{1,0:T(8,128)S(1)}, u32[]{:S(2)}, u32[]{:S(2)}) collective-permute-start(f32[32,8]{1,0:T(8,128)S(1)} %get-tuple-element.32), channel_id=1, source_target_pairs={{1,0},{2,1},{3,2},{4,3},{5,4},{6,5},{7,6},{8,7},{9,8},{10,9},{11,1... | collective-permute-start | bytes 3080 | tf_op jit(solution)/shard_map/ppermute | solution.py:19
  74.9 11.4 %collective-permute-start.10 = (f32[8,8192]{1,0:T(8,128)S(1)}, f32[8,8192]{1,0:T(8,128)}, u32[]{:S(2)}, u32[]{:S(2)}) collective-permute-start(f32[8,8192]{1,0:T(8,128)S(1)} %get-tuple-element.31), channel_id=1, source_target_pairs={{0,16},{16,32},{32,48},{48,64},{64,80},{80,96},{96,112},{112,128},... | collective-permute-start | bytes 786440 | tf_op jit(solution)/shard_map/ppermute | solution.py:17
  77.9 11.3 %collective-permute-start.11 = (f32[8,8192]{1,0:T(8,128)S(1)}, f32[8,8192]{1,0:T(8,128)S(1)}, u32[]{:S(2)}, u32[]{:S(2)}) collective-permute-start(f32[8,8192]{1,0:T(8,128)S(1)} %get-tuple-element.30), channel_id=1, source_target_pairs={{16,0},{32,16},{48,32},{64,48},{80,64},{96,80},{112,96},{128,112},... | collective-permute-start | bytes 786440 | tf_op jit(solution)/shard_map/ppermute | solution.py:19
  90.8 1.0 copy-start.7
  90.8 15.5 %copy-start.2 = (f32[32,8192]{1,0:T(8,128)}, f32[32,8192]{1,0:T(8,128)S(1)}, u32[]{:S(2)}) copy-start(f32[32,8192]{1,0:T(8,128)S(1)} %get-tuple-element.11) | copy-start | bytes 3145732
  91.9 6.0 %collective-permute-start.12 = (f32[32,16]{1,0:T(8,128)S(1)}, f32[32,16]{1,0:T(8,128)S(1)}, u32[]{:S(2)}, u32[]{:S(2)}) collective-permute-start(f32[32,16]{1,0:T(8,128)S(1)} %get-tuple-element.29), channel_id=1, source_target_pairs={{0,1},{1,2},{2,3},{3,4},{4,5},{5,6},{6,7},{7,8},{8,9},{9,10},{10,1... | collective-permute-start | bytes 6152 | tf_op jit(solution)/shard_map/ppermute | solution.py:17
  93.9 7.7 %collective-permute-start.13 = (f32[32,16]{1,0:T(8,128)S(1)}, f32[32,16]{1,0:T(8,128)S(1)}, u32[]{:S(2)}, u32[]{:S(2)}) collective-permute-start(f32[32,16]{1,0:T(8,128)S(1)} %get-tuple-element.28), channel_id=1, source_target_pairs={{1,0},{2,1},{3,2},{4,3},{5,4},{6,5},{7,6},{8,7},{9,8},{10,9},{11,1... | collective-permute-start | bytes 6152 | tf_op jit(solution)/shard_map/ppermute | solution.py:19
  107.4 53.8 %collective-permute-start.14 = (f32[16,8192]{1,0:T(8,128)}, f32[16,8192]{1,0:T(8,128)}, u32[]{:S(2)}, u32[]{:S(2)}) collective-permute-start(f32[16,8192]{1,0:T(8,128)} %get-tuple-element.27), channel_id=1, source_target_pairs={{0,16},{16,32},{32,48},{48,64},{64,80},{80,96},{96,112},{112,128},... | collective-permute-start | bytes 1572872 | tf_op jit(solution)/shard_map/ppermute | solution.py:17
  131.6 30.7 %collective-permute-start.15 = (f32[16,8192]{1,0:T(8,128)}, f32[16,8192]{1,0:T(8,128)}, u32[]{:S(2)}, u32[]{:S(2)}) collective-permute-start(f32[16,8192]{1,0:T(8,128)} %get-tuple-element.26), channel_id=1, source_target_pairs={{16,0},{32,16},{48,32},{64,48},{80,64},{96,80},{112,96},{128,112},... | collective-permute-start | bytes 1572872 | tf_op jit(solution)/shard_map/ppermute | solution.py:19
  162.3 1.4 copy-start.8
  164.0 1.0 copy-start.5
  165.0 6.0 %collective-permute-start.16 = (f32[32,32]{1,0:T(8,128)S(1)}, f32[32,32]{1,0:T(8,128)S(1)}, u32[]{:S(2)}, u32[]{:S(2)}) collective-permute-start(f32[32,32]{1,0:T(8,128)S(1)} %get-tuple-element.25), channel_id=1, source_target_pairs={{0,1},{1,2},{2,3},{3,4},{4,5},{5,6},{6,7},{7,8},{8,9},{9,10},{10,1... | collective-permute-start | bytes 12296 | tf_op jit(solution)/shard_map/ppermute | solution.py:17
  167.0 7.7 %collective-permute-start.17 = (f32[32,32]{1,0:T(8,128)S(1)}, f32[32,32]{1,0:T(8,128)S(1)}, u32[]{:S(2)}, u32[]{:S(2)}) collective-permute-start(f32[32,32]{1,0:T(8,128)S(1)} %get-tuple-element.24), channel_id=1, source_target_pairs={{1,0},{2,1},{3,2},{4,3},{5,4},{6,5},{7,6},{8,7},{9,8},{10,9},{11,1... | collective-permute-start | bytes 12296 | tf_op jit(solution)/shard_map/ppermute | solution.py:19
  174.8 14.1 %copy-start.9 = (f32[5]{0:T(128)S(1)}, f32[5]{0:T(128)}, u32[]{:S(2)}) copy-start(f32[5]{0:T(128)} %param.3) | copy-start | bytes 64
  179.4 29.5 %collective-permute-start.18 = (f32[32,8192]{1,0:T(8,128)}, f32[32,8192]{1,0:T(8,128)}, u32[]{:S(2)}, u32[]{:S(2)}) collective-permute-start(f32[32,8192]{1,0:T(8,128)} %get-tuple-element.4), channel_id=1, source_target_pairs={{0,16},{16,32},{32,48},{48,64},{64,80},{80,96},{96,112},{112,128},... | collective-permute-start | bytes 3145736 | tf_op jit(solution)/shard_map/ppermute | solution.py:17
  181.4 27.6 %collective-permute-start.19 = (f32[32,8192]{1,0:T(8,128)}, f32[32,8192]{1,0:T(8,128)}, u32[]{:S(2)}, u32[]{:S(2)}) collective-permute-start(f32[32,8192]{1,0:T(8,128)} %get-tuple-element.4), channel_id=1, source_target_pairs={{16,0},{32,16},{48,32},{64,48},{80,64},{96,80},{112,96},{128,112},... | collective-permute-start | bytes 3145736 | tf_op jit(solution)/shard_map/ppermute | solution.py:19
  208.9 2.2 %copy-start.1 = (f32[32,8192]{1,0:T(8,128)S(1)}, f32[32,8192]{1,0:T(8,128)}, u32[]{:S(2)}) copy-start(f32[32,8192]{1,0:T(8,128)} %copy-done) | copy-start | bytes 3145732
  208.9 2.5 %copy-start.3 = (f32[32,8192]{1,0:T(8,128)S(1)}, f32[32,8192]{1,0:T(8,128)}, u32[]{:S(2)}) copy-start(f32[32,8192]{1,0:T(8,128)} %copy-done.2) | copy-start | bytes 3145732
  208.9 2.8 %copy-start.4 = (f32[32,8192]{1,0:T(8,128)S(1)}, f32[32,8192]{1,0:T(8,128)}, u32[]{:S(2)}) copy-start(f32[32,8192]{1,0:T(8,128)} %param.2) | copy-start | bytes 3145732
where the time goes:
time: 224 us; the launch traced here: 220 us
  local copies, waits for them, and re-layouts  79.7 us (36%)
  starting transfers between devices  76.5 us (34%)
  other arithmetic  38.6 us (17%)
  waiting for transfers between devices  24 us (11%)
    ppermute x10, starting transfers between devices, extended_2(): lax.ppermute(head, axis, [((i + 1) % count, i) for i in range(ends)])  54 us
    rev x9, local copies, waits for them, and re-layouts, mirror_rims(): jnp.flip(lax.slice_in_dim(values, 0, reach, axis=axis), axis)  26.8 us
    rev x9, local copies, waits for them, and re-layouts, mirror_rims(): jnp.flip(lax.slice_in_dim(values, count - reach, count, axis=axis), axis)  26.8 us
    div x9, other arithmetic, five_taps(): return total / 16.0  24.8 us
    ppermute x10, waiting for transfers between devices, extended_2(): lax.ppermute(head, axis, [((i + 1) % count, i) for i in range(ends)])  23.7 us
    ppermute x10, starting transfers between devices, extended_2(): lax.ppermute(tail, axis, [(i, (i + 1) % count) for i in range(ends)])  22.5 us
    another operation x1, local copies, waits for them, and re-layouts  19.4 us
    add x1, other arithmetic, on_device(): return (summed + plane, plane)  8.09 us
  transfers between devices with their start and end apart: 20, of which 9 were waited for; matrix products, arithmetic and copies ran while one was open for 35% of the time, Pallas kernels for 0%

commit v1 on v0

v1 whole, which is shorter than its diff:
```python
import functools

import jax
import jax.numpy as jnp
from jax import lax
from jax.experimental import pallas as pl
from jax.experimental.pallas import tpu as pltpu
from jax.sharding import PartitionSpec as P

LANES = 128
TILE = 8
VMEM_LIMIT = 48 * 1024 * 1024


def swaps(count, first):
    return [(i, j) for k in range(first, count - 1, 2) for i, j in ((k, k + 1), (k + 1, k))]


def smooth_blocks(src, dst, src_base, dst_base, begin, rows, dilation, blocks, emit):
    lane = lax.broadcasted_iota(jnp.int32, (rows, LANES), 1)
    far = 2 * dilation
    keep_left = lane < LANES - far
    keep_far = lane >= far
    keep_near = lane >= dilation

    def down(block):
        def tap(step):
            return src[block, pl.ds(begin - src_base + step * dilation, rows), :]

        return (tap(-2) + tap(2)) + 4.0 * (tap(-1) + tap(1)) + 6.0 * tap(0)

    def one(block, carry, last):
        here, here_left, near_before, far_before = carry
        if last:
            after, after_left = here, here_left
        else:
            after = down(block + 1)
            after_left = pltpu.roll(after, LANES - far, 1)
        pair = here + jnp.where(keep_left, here_left, after_left)
        near = pltpu.roll(pair, dilation, 1)
        distant = pltpu.roll(pair, far, 1)
        total = (pair + jnp.where(keep_far, distant, far_before)) + 4.0 * (
            jnp.where(keep_near, near, near_before) + here
        )
        total = total * (1.0 / 256.0)
        if dst is not None:
            dst[block, pl.ds(begin - dst_base, rows), :] = total
        emit(block, total)
        return after, after_left, near, distant

    start = down(0)
    zero = jnp.zeros((rows, LANES), jnp.float32)
    carry = (start, pltpu.roll(start, LANES - far, 1), zero, zero)
    carry = lax.fori_loop(0, blocks - 1, lambda b, c: one(b, c, False), carry, unroll=5)
    one(blocks - 1, carry, True)


def nothing(block, total):
    return None


def place_rows(ext, even_in, odd_in, work, sems, blocks, tile_rows):
    index = lax.axis_index("rows")
    last = lax.axis_size("rows") - 1
    parity = index % 2
    even_at = pl.multiple_of((1 - parity) * 2 * tile_rows, TILE)
    odd_at = pl.multiple_of(parity * 2 * tile_rows, TILE)
    own = pltpu.make_async_copy(ext, work.at[:, pl.ds(tile_rows, tile_rows), :], sems.at[0])
    one = pltpu.make_async_copy(even_in, work.at[:, pl.ds(even_at, tile_rows), :], sems.at[1])
    two = pltpu.make_async_copy(odd_in, work.at[:, pl.ds(odd_at, tile_rows), :], sems.at[2])
    own.start()
    one.start()
    two.start()
    own.wait()
    one.wait()
    two.wait()

    def flip(to):
        def body(block, carry):
            for k in range(tile_rows):
                work[block, pl.ds(to + tile_rows - 1 - k, 1), :] = work[block, pl.ds(tile_rows + k, 1), :]
            return carry

        lax.fori_loop(0, blocks, body, 0)

    @pl.when(index == 0)
    def _():
        flip(0)

    @pl.when(index == last)
    def _():
        flip(2 * tile_rows)


def fine_kernel(blocks, tile_rows, levels, ext, even_in, odd_in, plane_out, cut_out, work, other, sems):
    place_rows(ext, even_in, odd_in, work, sems, blocks, tile_rows)
    own = pl.ds(tile_rows, tile_rows)

    def clipped(source, scale):
        level = levels[scale]

        def emit(block, total, first=False):
            detail = source(block) - total
            cut = jnp.minimum(jnp.maximum(detail, -level), level)
            if scale == 0:
                cut_out[block] = cut
            else:
                cut_out[block] = cut_out[block] + cut

        return emit

    def run(src, dst, src_base, dst_base, dilation, spans, scale):
        for begin, rows in spans:
            if begin == tile_rows and rows == tile_rows:
                emit = clipped(lambda b: src[b, pl.ds(tile_rows - src_base, tile_rows), :], scale)
            else:
                emit = nothing
            smooth_blocks(src, dst, src_base, dst_base, begin, rows, dilation, blocks, emit)

    t = tile_rows
    run(work, other, 0, 4, 1, ((4, t - 4), (t, t), (2 * t, t - 4)), 0)
    run(other, work, 4, 0, 2, ((8, t - 8), (t, t), (2 * t, t - 8)), 1)
    run(work, other, 0, 4, 4, ((16, t - 16), (t, t), (2 * t, t - 16)), 2)
    run(other, plane_out, 4, t, 8, ((t, t),), 3)


def coarse_kernel(blocks, tile_rows, levels, plane, even_in, odd_in, cut, sky, denoised, coarse, work, sems):
    place_rows(plane, even_in, odd_in, work, sems, blocks, tile_rows)
    level = levels[4]

    def emit(block, total):
        detail = work[block, pl.ds(tile_rows, tile_rows), :] - total
        all_cut = cut[block] + jnp.minimum(jnp.maximum(detail, -level), level)

        @pl.when(jnp.logical_and(block >= 1, block <= blocks - 2))
        def _():
            columns = pl.ds(pl.multiple_of((block - 1) * LANES, LANES), LANES)
            coarse[:, columns] = total
            denoised[:, columns] = sky[:, columns] - all_cut

    smooth_blocks(work, None, 0, 0, tile_rows, tile_rows, 16, blocks, emit)


def on_device(sky, thresholds):
    rows, columns = sky.shape
    row_count, col_count = lax.axis_size("rows"), lax.axis_size("cols")
    col = lax.axis_index("cols")
    blocks = columns // LANES + 2
    even_col = col % 2 == 0
    left_edge, right_edge = sky[:, :LANES], sky[:, columns - LANES :]
    first = lax.ppermute(jnp.where(even_col, right_edge, left_edge), "cols", swaps(col_count, 0))
    second = lax.ppermute(jnp.where(even_col, left_edge, right_edge), "cols", swaps(col_count, 1))
    left = jnp.where(even_col, second, first)
    right = jnp.where(even_col, first, second)
    left = jnp.where(col == 0, jnp.flip(left_edge, 1), left)
    right = jnp.where(col == col_count - 1, jnp.flip(right_edge, 1), right)
    inner = sky.reshape(rows, columns // LANES, LANES).transpose(1, 0, 2)
    ext = jnp.concatenate([left[None], inner, right[None]], axis=0)

    def exchange(values):
        return (
            lax.ppermute(values, "rows", swaps(row_count, 0)),
            lax.ppermute(values, "rows", swaps(row_count, 1)),
        )

    any_space = pl.BlockSpec(memory_space=pl.ANY)
    in_vmem = pl.BlockSpec(memory_space=pltpu.VMEM)
    in_smem = pl.BlockSpec(memory_space=pltpu.SMEM)
    block_shape = jax.ShapeDtypeStruct((blocks, rows, LANES), jnp.float32)
    work = pltpu.VMEM((blocks, 3 * rows, LANES), jnp.float32)
    params = pltpu.CompilerParams(vmem_limit_bytes=VMEM_LIMIT)

    plane, cut = pl.pallas_call(
        functools.partial(fine_kernel, blocks, rows),
        out_shape=(block_shape, block_shape),
        in_specs=[in_smem, any_space, any_space, any_space],
        out_specs=(in_vmem, in_vmem),
        scratch_shapes=[work, work, pltpu.SemaphoreType.DMA((3,))],
        compiler_params=params,
        name="fine",
    )(thresholds, ext, *exchange(ext))

    flat = jax.ShapeDtypeStruct((rows, columns), jnp.float32)
    return pl.pallas_call(
        functools.partial(coarse_kernel, blocks, rows),
        out_shape=(flat, flat),
        in_specs=[in_smem, any_space, any_space, any_space, in_vmem, in_vmem],
        out_specs=(in_vmem, in_vmem),
        scratch_shapes=[work, pltpu.SemaphoreType.DMA((3,))],
        compiler_params=params,
        name="coarse",
    )(thresholds, plane, *exchange(plane), cut, sky)


def solution(mesh):
    return jax.shard_map(
        on_device,
        mesh=mesh,
        in_specs=(P("rows", "cols"), P()),
        out_specs=(P("rows", "cols"), P("rows", "cols")),
        check_vma=False,
    )
```

time: 224 us -> 90 us (0.40); the launches traced: 220 us -> 89.8 us
  local copies, waits for them, and re-layouts: 79.7 us -> 1.51 us
  starting transfers between devices: 76.5 us -> 13.2 us
  Pallas kernels: 0 us -> 38.8 us
  other arithmetic: 38.6 us -> 0.82 us
  waiting for transfers between devices: 24 us -> 34.6 us
    ppermute x20 -> x6, starting transfers between devices: 76.5 us -> 13.2 us  [the longest x2 7.68 us: exchange(): lax.ppermute(values, 'rows', swaps(row_count, 1))]
    rev x18 -> x2, local copies, waits for them, and re-layouts: 53.6 us -> 0.14 us  [the longest x1 0.07 us: on_device(): left = jnp.where(col == 0, jnp.flip(left_edge, 1), left)]
    pallas_call x0 -> x2, Pallas kernels: none -> 38.8 us  [the longest x1 26 us: on_device(): pl.pallas_call(functools.partial(fine_kernel, blocks, rows), out_shape=(b...]
    div x9 -> x0, other arithmetic: 24.8 us -> none  [five_taps(): return total / 16.0]
    another operation x1 -> x0, local copies, waits for them, and re-layouts: 19.4 us -> none
    ppermute x20 -> x6, waiting for transfers between devices: 24 us -> 34.6 us  [the longest x2 32.4 us: exchange(): lax.ppermute(values, 'rows', swaps(row_count, 1))]
    add x1 -> x0, other arithmetic: 8.09 us -> none  [on_device(): return (summed + plane, plane)]
    select_n x19 -> x0, other arithmetic: 5.68 us -> none  [the longest x10 4.37 us: mirror_rims(): jnp.where(first, jnp.flip(lax.slice_in_dim(values, 0, reach, axis=axis),...]
  transfers between devices with their start and end apart: 20 -> 6, of which waited for: 9 -> 4; matrix products, arithmetic and copies ran while one was open for 35% -> 2% of each run, Pallas kernels for 0% -> 0%
where the time goes in v1:
time: 90 us; the launch traced here: 89.8 us
  Pallas kernels  38.8 us (43%)
  waiting for transfers between devices  34.6 us (38%)
  starting transfers between devices  13.2 us (15%)
  local copies, waits for them, and re-layouts  1.51 us (2%)
    ppermute x2, waiting for transfers between devices, exchange(): lax.ppermute(values, 'rows', swaps(row_count, 1))  32.4 us
    pallas_call x1, Pallas kernels, on_device(): pl.pallas_call(functools.partial(fine_kernel, blocks, rows), out_shape=(b...  26 us
    pallas_call x1, Pallas kernels, on_device(): pl.pallas_call(functools.partial(coarse_kernel, blocks, rows), out_shape=...  12.8 us
    ppermute x2, starting transfers between devices, exchange(): lax.ppermute(values, 'rows', swaps(row_count, 1))  7.68 us
    ppermute x1, starting transfers between devices, on_device(): lax.ppermute(jnp.where(even_col, left_edge, right_edge), 'cols', swaps(co...  5.29 us
  transfers between devices with their start and end apart: 6, of which 4 were waited for; matrix products, arithmetic and copies ran while one was open for 2% of the time, Pallas kernels for 0%

profile of v1, /device:TPU:102, one launch (start us, length us, event | category | flops | bytes accessed | tf_op | source)
XLA Modules:
  0.0 89.8 jit_solution(16071043607223147485)
XLA Ops:
  0.6 0.7 fusion
  1.4 5.3 %collective-permute-start = (f32[32,128]{1,0:T(8,128)S(1)}, f32[32,128]{1,0:T(8,128)S(1)}, u32[]{:S(2)}, u32[]{:S(2)}) collective-permute-start(f32[32,128]{1,0:T(8,128)S(1)} %get-tuple-element.7), channel_id=1, source_target_pairs={{1,2},{2,1},{3,4},{4,3},{5,6},{6,5},{7,8},{8,7},{9,10},{10,9},{11,... | collective-permute-start | bytes 49160 | tf_op jit(solution)/shard_map/ppermute | solution.py:152
  6.7 0.1 collective-permute-start.1
  6.8 1.4 %bitcast_bitcast_fusion = f32[64,32,128]{2,1,0:T(8,128)S(1)} fusion(f32[32,8192]{1,0:T(8,128)} %sky.1), kind=kLoop, calls=%fused_computation.1 | loop fusion | bytes 2097152 | tf_op jit(solution)/shard_map/transpose | solution.py:157
  8.2 0.1 rev.7
  8.2 0.1 rev.8
  8.3 0.9 %collective-permute-done = f32[32,128]{1,0:T(8,128)S(1)} collective-permute-done((f32[32,128]{1,0:T(8,128)S(1)}, f32[32,128]{1,0:T(8,128)S(1)}, u32[]{:S(2)}, u32[]{:S(2)}) %collective-permute-start) | collective-permute-done | bytes 16416 | tf_op jit(solution)/shard_map/ppermute | solution.py:152
  9.2 1.3 %collective-permute-done.1 = f32[32,128]{1,0:T(8,128)S(1)} collective-permute-done((f32[32,128]{1,0:T(8,128)S(1)}, f32[32,128]{1,0:T(8,128)S(1)}, u32[]{:S(2)}, u32[]{:S(2)}) %collective-permute-start.1) | collective-permute-done | bytes 16416 | tf_op jit(solution)/shard_map/ppermute | solution.py:151
  10.5 0.0 copy-start.1
  10.5 0.1 pad_maximum_fusion.ext
  10.6 0.0 copy-start
  10.6 3.9 %collective-permute-start.3 = (f32[66,32,128]{2,1,0:T(8,128)S(1)}, f32[66,32,128]{2,1,0:T(8,128)S(1)}, u32[]{:S(2)}, u32[]{:S(2)}) collective-permute-start(f32[66,32,128]{2,1,0:T(8,128)S(1)} %pad_maximum_fusion.ext), channel_id=1, source_target_pairs={{16,32},{32,16},{48,64},{64,48},{80,96},{96,80},{112,128},{128,112... | collective-permute-start | bytes 3244040 | tf_op jit(solution)/shard_map/ppermute | solution.py:163
  14.5 0.1 collective-permute-start.2
  14.6 16.2 %collective-permute-done.3.odd_in = f32[66,32,128]{2,1,0:T(8,128)S(1)} collective-permute-done((f32[66,32,128]{2,1,0:T(8,128)S(1)}, f32[66,32,128]{2,1,0:T(8,128)S(1)}, u32[]{:S(2)}, u32[]{:S(2)}) %collective-permute-start.3) | collective-permute-done | bytes 1081376 | tf_op jit(solution)/shard_map/ppermute | solution.py:163
  30.8 0.0 collective-permute-done.2.even_in
  30.8 0.0 copy-done.1
  30.8 26.0 %fine.1 = (f32[66,32,128]{2,1,0:T(8,128)S(1)}, f32[66,32,128]{2,1,0:T(8,128)S(1)}) custom-call(f32[5]{0:T(128)S(1)} %copy-done.1, f32[66,32,128]{2,1,0:T(8,128)S(1)} %pad_maximum_fusion.ext, f32[66,32,128]{2,1,0:T(8,128)S(1)} %collective-permute-done.2.even_in, f32[66,32,128]{2,1,0:T(8,128)S(1)} %collective-permute-done.3.odd_in), custom_call_target="tpu_custom_call" | custom-call | tf_op jit(solution)/shard_map/fine/pallas_call | solution.py:173
  56.9 3.8 %collective-permute-start.5 = (f32[66,32,128]{2,1,0:T(8,128)S(1)}, f32[66,32,128]{2,1,0:T(8,128)S(1)}, u32[]{:S(2)}, u32[]{:S(2)}) collective-permute-start(f32[66,32,128]{2,1,0:T(8,128)S(1)} %get-tuple-element.4.plane), channel_id=1, source_target_pairs={{16,32},{32,16},{48,64},{64,48},{80,96},{96,80},{112,128},{128,112... | collective-permute-start | bytes 3244040 | tf_op jit(solution)/shard_map/ppermute | solution.py:163
  60.7 0.1 collective-permute-start.4
  60.8 16.2 %collective-permute-done.5.odd_in = f32[66,32,128]{2,1,0:T(8,128)S(1)} collective-permute-done((f32[66,32,128]{2,1,0:T(8,128)S(1)}, f32[66,32,128]{2,1,0:T(8,128)S(1)}, u32[]{:S(2)}, u32[]{:S(2)}) %collective-permute-start.5) | collective-permute-done | bytes 1081376 | tf_op jit(solution)/shard_map/ppermute | solution.py:163
  77.0 0.0 collective-permute-done.4.even_in
  77.0 0.0 copy-done
  77.0 12.8 %coarse.1 = (f32[32,8192]{1,0:T(8,128)}, f32[32,8192]{1,0:T(8,128)}) custom-call(f32[5]{0:T(128)S(1)} %copy-done.1, f32[66,32,128]{2,1,0:T(8,128)S(1)} %get-tuple-element.4.plane, f32[66,32,128]{2,1,0:T(8,128)S(1)} %collective-permute-done.4.even_in, f32[66,32,128]{2,1,0:T(8,128)S(1)} %collective-permute-done.5.odd_in, ...), custom_call_target="tpu_custom_call" | custom-call | tf_op jit(solution)/shard_map/coarse/pallas_call | solution.py:184
  (1 shorter events, 0.0 us)
Async XLA Ops:
  1.4 7.8 %collective-permute-start = (f32[32,128]{1,0:T(8,128)S(1)}, f32[32,128]{1,0:T(8,128)S(1)}, u32[]{:S(2)}, u32[]{:S(2)}) collective-permute-start(f32[32,128]{1,0:T(8,128)S(1)} %get-tuple-element.7), channel_id=1, source_target_pairs={{1,2},{2,1},{3,4},{4,3},{5,6},{6,5},{7,8},{8,7},{9,10},{10,9},{11,... | collective-permute-start | bytes 49160 | tf_op jit(solution)/shard_map/ppermute | solution.py:152
  6.7 3.8 %collective-permute-start.1 = (f32[32,128]{1,0:T(8,128)S(1)}, f32[32,128]{1,0:T(8,128)S(1)}, u32[]{:S(2)}, u32[]{:S(2)}) collective-permute-start(f32[32,128]{1,0:T(8,128)S(1)} %get-tuple-element.8), channel_id=1, source_target_pairs={{0,1},{1,0},{2,3},{3,2},{4,5},{5,4},{6,7},{7,6},{8,9},{9,8},{10,11... | collective-permute-start | bytes 49160 | tf_op jit(solution)/shard_map/ppermute | solution.py:151
  10.5 20.3 %copy-start.1 = (f32[5]{0:T(128)S(1)}, f32[5]{0:T(128)}, u32[]{:S(2)}) copy-start(f32[5]{0:T(128)} %levels.3) | copy-start | bytes 64
  10.6 66.4 %copy-start = (f32[32,8192]{1,0:T(8,128)S(1)}, f32[32,8192]{1,0:T(8,128)}, u32[]{:S(2)}) copy-start(f32[32,8192]{1,0:T(8,128)} %sky.1) | copy-start | bytes 3145732
  10.6 20.2 %collective-permute-start.3 = (f32[66,32,128]{2,1,0:T(8,128)S(1)}, f32[66,32,128]{2,1,0:T(8,128)S(1)}, u32[]{:S(2)}, u32[]{:S(2)}) collective-permute-start(f32[66,32,128]{2,1,0:T(8,128)S(1)} %pad_maximum_fusion.ext), channel_id=1, source_target_pairs={{16,32},{32,16},{48,64},{64,48},{80,96},{96,80},{112,128},{128,112... | collective-permute-start | bytes 3244040 | tf_op jit(solution)/shard_map/ppermute | solution.py:163
  14.5 16.3 %collective-permute-start.2 = (f32[66,32,128]{2,1,0:T(8,128)S(1)}, f32[66,32,128]{2,1,0:T(8,128)S(1)}, u32[]{:S(2)}, u32[]{:S(2)}) collective-permute-start(f32[66,32,128]{2,1,0:T(8,128)S(1)} %pad_maximum_fusion.ext), channel_id=1, source_target_pairs={{0,16},{16,0},{32,48},{48,32},{64,80},{80,64},{96,112},{112,96},{1... | collective-permute-start | bytes 3244040 | tf_op jit(solution)/shard_map/ppermute | solution.py:162
  56.9 20.1 %collective-permute-start.5 = (f32[66,32,128]{2,1,0:T(8,128)S(1)}, f32[66,32,128]{2,1,0:T(8,128)S(1)}, u32[]{:S(2)}, u32[]{:S(2)}) collective-permute-start(f32[66,32,128]{2,1,0:T(8,128)S(1)} %get-tuple-element.4.plane), channel_id=1, source_target_pairs={{16,32},{32,16},{48,64},{64,48},{80,96},{96,80},{112,128},{128,112... | collective-permute-start | bytes 3244040 | tf_op jit(solution)/shard_map/ppermute | solution.py:163
  60.7 16.3 %collective-permute-start.4 = (f32[66,32,128]{2,1,0:T(8,128)S(1)}, f32[66,32,128]{2,1,0:T(8,128)S(1)}, u32[]{:S(2)}, u32[]{:S(2)}) collective-permute-start(f32[66,32,128]{2,1,0:T(8,128)S(1)} %get-tuple-element.4.plane), channel_id=1, source_target_pairs={{0,16},{16,0},{32,48},{48,32},{64,80},{80,64},{96,112},{112,96},{1... | collective-permute-start | bytes 3244040 | tf_op jit(solution)/shard_map/ppermute | solution.py:162

commit v2 on v0

v2 whole, which is shorter than its diff:
```python
import functools

import jax
import jax.numpy as jnp
import ml_dtypes
import numpy as np
from jax import lax
from jax.experimental import pallas as pl
from jax.experimental.pallas import tpu as pltpu
from jax.sharding import PartitionSpec as P

LANES = 128
HALF = LANES // 2
PAIR = 2 * LANES
SPAN = PAIR + LANES
TILE = 8
SCALES = 5
MEBI = 1024 * 1024
BATCH = 16
F32, BF16 = jnp.float32, jnp.bfloat16


def swaps(count, first):
    return [(i, j) for k in range(first, count - 1, 2) for i, j in ((k, k + 1), (k + 1, k))]


def column_weights(scales):
    taps = np.ones(1)
    for scale in range(scales):
        step = np.zeros(4 * 2**scale + 1)
        step[:: 2**scale] = (1.0, 4.0, 6.0, 4.0, 1.0)
        taps = np.convolve(taps, step)
    reach = len(taps) // 2
    source = np.concatenate([np.arange(PAIR + HALF), np.arange(-HALF, 0)])
    offset = source[:, None] - np.arange(PAIR)[None, :]
    exact = np.where(np.abs(offset) <= reach, taps[np.clip(offset + reach, 0, 2 * reach)], 0.0) * 2.0 ** (-8 * scales)
    high = exact.astype(ml_dtypes.bfloat16)
    low = (exact - high.astype(np.float64)).astype(ml_dtypes.bfloat16)
    return [high, low] if np.any(low.astype(np.float32)) else [high]


def binomial(a, b, c, d, e):
    return (a + e) + 4.0 * (b + d) + 6.0 * c


def columns_of(block, width=LANES):
    if isinstance(block, int):
        return slice(block * width, (block + 1) * width)
    return pl.ds(pl.multiple_of(block * width, width), width)


def loop(begin, end, body, group=1):
    def step(k, carry):
        for slot in range(group):
            body(begin + k * group + slot, slot)
        return carry

    whole = (end - begin) // group
    lax.fori_loop(0, whole, step, 0)
    for index in range(begin + whole * group, end):
        body(index, index - begin - whole * group)


def with_neighbours(own, odd_in, flipped, run):
    rows = own[0].shape[0]
    index, last = lax.axis_index("rows"), lax.axis_size("rows") - 1
    outer = jnp.logical_or(index == 0, index == last)

    @pl.when(outer)
    def _():
        for source, target in zip(own, flipped):
            for k in range(rows):
                target[k : k + 1, :] = source[rows - 1 - k : rows - k, :]
        run(flipped)

    @pl.when(jnp.logical_not(outer))
    def _():
        run(odd_in)


def load_block(own, even, odd, buffer):
    rows = own.shape[0]
    parity = lax.axis_index("rows") % 2
    buffer[rows : 2 * rows, :] = own
    buffer[pl.ds(pl.multiple_of((1 - parity) * 2 * rows, TILE), rows), :] = even
    buffer[pl.ds(pl.multiple_of(parity * 2 * rows, TILE), rows), :] = odd


def taps(buffer, begin, step, count):
    return [buffer[begin + k * step : begin + k * step + count, :] for k in (-2, -1, 0, 1, 2)]


def take_kernel(sky, part, first, second):
    columns = sky.shape[1]
    part[...] = sky[:, 0 : part.shape[1]]
    left, right = sky[:, 0:LANES], sky[:, columns - LANES : columns]
    even = lax.axis_index("cols") % 2 == 0
    first[...] = jnp.where(even, right, left)
    second[...] = jnp.where(even, left, right)


def join_kernel(sky, first, second, rest):
    width, columns = rest.shape[1] - LANES, sky.shape[1]
    rest[:, 0:width] = sky[:, columns - width : columns]
    rows = sky.shape[0]
    index, last = lax.axis_index("cols"), lax.axis_size("cols") - 1
    in_first = lax.broadcasted_iota(jnp.int32, (rows, LANES), 1) < HALF
    even = index % 2 == 0
    left = jnp.where(even, second[...], first[...])
    right = jnp.where(even, first[...], second[...])
    halo = slice(width, width + LANES)
    rest[:, halo] = jnp.where(in_first, right, left)

    def flip(value):
        row = lax.broadcasted_iota(jnp.int32, (LANES, LANES), 0)
        lane = lax.broadcasted_iota(jnp.int32, (LANES, LANES), 1)
        turn = (row + lane == LANES - 1).astype(F32)
        return jnp.dot(value, turn, preferred_element_type=F32, precision=lax.Precision.HIGHEST)

    @pl.when(index == 0)
    def _():
        rest[:, halo] = jnp.where(in_first, right, flip(sky[:, 0:LANES]))

    @pl.when(index == last)
    def _():
        rest[:, halo] = jnp.where(in_first, flip(sky[:, columns - LANES : columns]), left)


def rows_kernel(group, own, even_in, odd_in, out, flipped, *buffers):
    rows = own.shape[0]

    def run(odd):
        def one(block, slot):
            zero, ones, twos = buffers[3 * slot : 3 * slot + 3]
            columns = columns_of(block)
            load_block(own[:, columns], even_in[:, columns], odd[0][:, columns], zero)
            ones[...] = binomial(*taps(zero, 4, 1, 3 * rows - 8))
            two = binomial(*taps(ones, 4, 2, 3 * rows - 16))
            twos[...] = two
            n = 3 * rows - 32
            three = binomial(two[0:n], twos[4 : n + 4, :], two[8 : n + 8], twos[12 : n + 12, :], two[16 : n + 16])
            out[:, columns] = binomial(*[three[8 * k : 8 * k + rows] for k in range(5)])

        loop(0, own.shape[1] // LANES, one, group)

    with_neighbours((own,), (odd_in,), (flipped,), run)


def put(value, operand, rows, main=None, after=None, before=None):
    high = value.astype(BF16)
    low = (value - high.astype(F32)).astype(BF16)

    def at(slot):
        return slice(slot * rows, (slot + 1) * rows) if isinstance(slot, int) else pl.ds(pl.multiple_of(slot * rows, 16), rows)

    for base, piece in ((0, high), (SPAN, low)):
        if main is not None:
            operand[at(main[0]), base + main[1] * LANES : base + (main[1] + 1) * LANES] = piece
        if after is not None:
            operand[at(after), base + PAIR : base + PAIR + HALF] = piece[:, :HALF]
        if before is not None:
            operand[at(before), base + PAIR + HALF : base + SPAN] = piece[:, HALF:]


def clip(detail, level):
    return jnp.minimum(jnp.maximum(detail, -level), level)


def filter_columns(operand, weights, rows, start, count, emit):
    value = operand[start * rows : (start + count) * rows, :]
    total = None
    for weight in weights:
        term = jnp.dot(value[:, : weight.shape[0]], weight[...], preferred_element_type=F32)
        total = term if total is None else total + term
    for k in range(count):
        emit(start + k, total[k * rows : (k + 1) * rows])


def details_kernel(pairs, weight_counts, levels, *refs):
    own, even_in, odd_in, four, refs = refs[:2], refs[2:4], refs[4:6], refs[6:8], refs[8:]
    weights, refs = refs[: sum(weight_counts)], refs[sum(weight_counts) :]
    out, plane, refs = refs[0], refs[1], refs[2:]
    flipped, operands, buffers = refs[:2], refs[2:6], refs[6:]
    rows = own[0].shape[0]
    first = own[0].shape[1] // PAIR

    def run(odd):
        def one(span, block, slot):
            zero, ones, twos = buffers[3 * slot : 3 * slot + 3]
            columns = columns_of(block)
            load_block(own[span][:, columns], even_in[span][:, columns], odd[span][:, columns], zero)
            ones[...] = binomial(*taps(zero, rows - 12, 1, rows + 24))
            two = binomial(*taps(ones, 4, 2, rows + 16))
            twos[...] = two
            three = binomial(two[0:rows], twos[4 : rows + 4, :], two[8 : rows + 8], twos[12 : rows + 12, :], two[16 : rows + 16])
            return ones[12 : rows + 12, :], two[8 : rows + 8], three, four[span][:, columns]

        for span, begin, end in ((0, 0, first), (1, first, pairs)):

            def body(pair, _):
                block = 2 * (pair - begin)
                left, right = one(span, block, 0), one(span, block + 1, 1)
                for k in range(4):
                    put(left[k], operands[k], rows, main=(pair + 1, 0), after=pair)
                    put(right[k], operands[k], rows, main=(pair + 1, 1), before=pair + 2)

            loop(begin, end, body)
        for k, value in enumerate(one(1, 2 * (pairs - first), 0)):
            put(value, operands[k], rows, after=pairs, before=1)

    with_neighbours(own, odd_in, flipped, run)

    at = 0
    for scale in range(4):
        use = weights[at : at + weight_counts[scale]]
        at += weight_counts[scale]
        level = levels[scale]

        def emit(slot, total):
            pair = slot - 1
            columns = columns_of(pair, PAIR)
            if scale == 0:
                sky = own[0][:, columns] if pair < first else own[1][:, columns_of(pair - first, PAIR)]
                out[:, columns] = sky - clip(sky - total, level)
            else:
                out[:, columns] = out[:, columns] - clip(plane[:, columns] - total, level)
            plane[:, columns] = total

        for start in range(0, pairs, BATCH):
            filter_columns(operands[scale], use, rows, start + 1, BATCH, emit)


def last_rows(own, even_in, odd, then):
    half = own[0].shape[0] // 2

    def with_sides(above, below):
        def one(span, block):
            columns = columns_of(block)
            a, b = above[span][0:half, columns], above[span][half : 2 * half, columns]
            c, d = own[span][0:half, columns], own[span][half : 2 * half, columns]
            e, f = below[span][0:half, columns], below[span][half : 2 * half, columns]
            return jnp.concatenate([binomial(a, b, c, d, e), binomial(b, c, d, e, f)], axis=0)

        then(one)

    parity = lax.axis_index("rows") % 2
    pl.when(parity == 0)(lambda: with_sides(odd, even_in))
    pl.when(parity == 1)(lambda: with_sides(even_in, odd))


def finish(operand, weights, rows, start, count, level, pair_of, part_sum, plane, denoised, coarse):
    def emit(slot, total):
        columns, place = columns_of(pair_of(slot), PAIR), columns_of(slot - start, PAIR)
        coarse[:, place] = total
        denoised[:, place] = part_sum[:, columns] - clip(plane[:, columns] - total, level)

    filter_columns(operand, weights, rows, start, count, emit)


def row_copies(source, target, begin, sems):
    columns = slice(begin, begin + source.shape[1])
    return [
        pltpu.make_async_copy(source.at[row : row + TILE, :], target.at[row : row + TILE, columns], sems.at[k])
        for k, row in enumerate(range(0, source.shape[0], TILE))
    ]


def coarse_one_kernel(levels, own, even_in, odd_in, part_sum, plane, high, low, denoised, coarse, flipped, operand):
    rows = own.shape[0]
    pairs = own.shape[1] // PAIR

    def blocks(one):
        def body(pair, _):
            put(one(0, 2 * pair), operand, rows, main=(pair, 0), after=pair - 1)
            put(one(0, 2 * pair + 1), operand, rows, main=(pair, 1), before=pair + 1)

        put(one(0, 1), operand, rows, before=1)
        loop(1, pairs - 1, body)
        put(one(0, 2 * pairs - 2), operand, rows, after=pairs - 2)

    with_neighbours((own,), (odd_in,), (flipped,), lambda odd: last_rows((own,), (even_in,), odd, blocks))
    finish(operand, (high, low), rows, 1, pairs - 2, levels[4], lambda slot: slot, part_sum, plane, denoised, coarse)


def coarse_two_kernel(levels, *refs):
    own, even_in, odd_in, refs = refs[:2], refs[2:4], refs[4:6], refs[6:]
    part_sum, plane, high, low, den_one, coa_one, denoised, coarse, *refs = refs
    flipped, (operand, den_two, coa_two, den_three, coa_three, sems) = refs[:2], refs[2:]
    rows, columns = part_sum.shape
    first, pairs = own[0].shape[1] // PAIR, columns // PAIR
    begin = first - 1
    copies = row_copies(den_one, denoised, PAIR, sems.at[0]) + row_copies(coa_one, coarse, PAIR, sems.at[1])
    for copy in copies:
        copy.start()

    def blocks(one):
        def body(pair, _):
            block = 2 * (pair - first)
            put(one(1, block), operand, rows, main=(pair - begin + 1, 0), after=pair - begin)
            put(one(1, block + 1), operand, rows, main=(pair - begin + 1, 1), before=pair - begin + 2)

        loop(first, pairs, body)
        put(one(0, 2 * begin), operand, rows, main=(1, 0))
        put(one(0, 2 * begin + 1), operand, rows, main=(1, 1), before=2)
        put(one(0, 2 * begin - 1), operand, rows, before=1)
        put(one(1, 2 * (pairs - first)), operand, rows, after=pairs - begin, before=0)
        put(one(0, 0), operand, rows, main=(0, 0))
        put(one(0, 1), operand, rows, main=(0, 1))
        put(one(0, 2), operand, rows, after=0)

    with_neighbours(own, odd_in, flipped, lambda odd: last_rows(own, even_in, odd, blocks))
    count = pairs - begin + 1
    half = count // 2
    pair_of = lambda slot: slot + begin - 1 if slot else 0
    for start, size, den, coa, at in ((0, half, den_two, coa_two, 2), (half, count - half, den_three, coa_three, 6)):
        finish(operand, (high, low), rows, start, size, levels[4], pair_of, part_sum, plane, den, coa)
        for source, target, k in ((den, denoised, at), (coa, coarse, at + 1)):
            if start == 0:
                more = row_copies(source.at[:, 0:PAIR], target, 0, sems.at[k])
                more += row_copies(source.at[:, PAIR : half * PAIR], target, begin * PAIR, sems.at[k + 2])
            else:
                more = row_copies(source, target, (begin + half - 1) * PAIR, sems.at[k])
            for copy in more:
                copy.start()
            copies += more
    for copy in copies:
        copy.wait()


def on_device(sky, thresholds):
    rows, columns = sky.shape
    row_count, col_count = lax.axis_size("rows"), lax.axis_size("cols")
    blocks, pairs = columns // LANES, columns // PAIR
    first = blocks // 2 + 2
    weights = [
        [jnp.asarray(w if k else np.concatenate([w, w])) for k, w in enumerate(column_weights(scale + 1))]
        for scale in range(SCALES)
    ]

    any_space = pl.BlockSpec(memory_space=pl.ANY)
    in_vmem = pl.BlockSpec(memory_space=pltpu.VMEM)
    in_smem = pl.BlockSpec(memory_space=pltpu.SMEM)
    dma = pltpu.SemaphoreType.DMA

    def room(mebibytes):
        return pltpu.CompilerParams(vmem_limit_bytes=mebibytes * MEBI)

    def array(width):
        return jax.ShapeDtypeStruct((rows, width), F32)

    def vmem(width):
        return pltpu.VMEM((rows, width), F32)

    def operand(slots):
        return pltpu.VMEM((slots * rows, 2 * SPAN), BF16)

    def exchange(values):
        return (
            lax.ppermute(values, "rows", swaps(row_count, 0)),
            lax.ppermute(values, "rows", swaps(row_count, 1)),
        )

    widths = (first * LANES, (blocks - first + 1) * LANES)
    part, one, two = pl.pallas_call(
        take_kernel,
        out_shape=(array(widths[0]), array(LANES), array(LANES)),
        in_specs=[in_vmem],
        out_specs=(in_vmem,) * 3,
        compiler_params=room(8),
        name="take",
    )(sky)
    near = [exchange(part)]
    one = lax.ppermute(one, "cols", swaps(col_count, 0))
    two = lax.ppermute(two, "cols", swaps(col_count, 1))
    rest = pl.pallas_call(
        join_kernel,
        out_shape=array(widths[1]),
        in_specs=[in_vmem] * 3,
        out_specs=in_vmem,
        compiler_params=room(8),
        cost_estimate=pl.CostEstimate(flops=3 * 10**10, bytes_accessed=10**6, transcendentals=0),
        name="join",
    )(sky, one, two)
    near.append(exchange(rest))
    own = (part, rest)
    group = 4

    def smooth_rows(which, name):
        width = widths[which]
        return pl.pallas_call(
            functools.partial(rows_kernel, group),
            out_shape=array(width),
            in_specs=[in_vmem] * 3,
            out_specs=in_vmem,
            scratch_shapes=[vmem(width)]
            + [pltpu.VMEM((3 * rows - cut, LANES), F32) for _ in range(group) for cut in (0, 8, 16)],
            compiler_params=room(10),
            name=name,
        )(own[which], *near[which])

    four = [smooth_rows(0, "rows_one")]
    near_four = [exchange(four[0])]
    four.append(smooth_rows(1, "rows_two"))
    near_four.append(exchange(four[1]))

    def columnwise(pairs_of_inputs):
        return [x[0] for x in pairs_of_inputs] + [x[1] for x in pairs_of_inputs]

    fine = [w for scale in range(4) for w in weights[scale]]
    part_sum, plane = pl.pallas_call(
        functools.partial(details_kernel, pairs, tuple(len(weights[scale]) for scale in range(4))),
        out_shape=(array(columns), array(columns)),
        in_specs=[in_smem] + [in_vmem] * (8 + len(fine)),
        out_specs=(in_vmem, in_vmem),
        scratch_shapes=[vmem(w) for w in widths]
        + [operand(pairs + 2)] * 4
        + [pltpu.VMEM((n, LANES), F32) for _ in range(2) for n in (3 * rows, rows + 24, rows + 16)],
        compiler_params=room(28),
        name="details",
    )(thresholds, *own, *columnwise(near), *four, *fine)

    inner = first // 2 - 2
    outs = pl.pallas_call(
        coarse_one_kernel,
        out_shape=(array(inner * PAIR),) * 2,
        in_specs=[in_smem] + [in_vmem] * 7,
        out_specs=(in_vmem,) * 2,
        scratch_shapes=[vmem(widths[0]), operand(inner + 2)],
        compiler_params=room(16),
        name="coarse_one",
    )(thresholds, four[0], *near_four[0], part_sum, plane, *weights[4])
    count = pairs - inner
    return pl.pallas_call(
        coarse_two_kernel,
        out_shape=(array(columns), array(columns)),
        in_specs=[in_smem] + [in_vmem] * 12,
        out_specs=(pl.BlockSpec(memory_space=pltpu.HBM),) * 2,
        scratch_shapes=[vmem(w) for w in widths]
        + [operand(count + 2)]
        + [vmem(n * PAIR) for n in (count // 2, count // 2, count - count // 2, count - count // 2)]
        + [dma((8, rows // TILE))],
        compiler_params=room(16),
        name="coarse_two",
    )(thresholds, *four, *columnwise(near_four), part_sum, plane, *weights[4], *outs)


def solution(mesh):
    return jax.shard_map(
        on_device,
        mesh=mesh,
        in_specs=(P("rows", "cols"), P()),
        out_specs=(P("rows", "cols"), P("rows", "cols")),
        check_vma=False,
    )
```

time: 224 us -> 47.8 us (0.21); the launches traced: 220 us -> 47.5 us
  local copies, waits for them, and re-layouts: 79.7 us -> 1.28 us
  starting transfers between devices: 76.5 us -> 25.5 us
  other arithmetic: 38.6 us -> 0 us
  waiting for transfers between devices: 24 us -> 7.01 us
  Pallas kernels: 0 us -> 12.7 us
    rev x18 -> x0, local copies, waits for them, and re-layouts: 53.6 us -> none  [the longest x9 26.8 us: mirror_rims(): jnp.flip(lax.slice_in_dim(values, 0, reach, axis=axis), axis)]
    ppermute x20 -> x10, starting transfers between devices: 76.5 us -> 25.5 us  [the longest x4 18.6 us: exchange(): lax.ppermute(values, 'rows', swaps(row_count, 1))]
    div x9 -> x0, other arithmetic: 24.8 us -> none  [five_taps(): return total / 16.0]
    another operation x1 -> x0, local copies, waits for them, and re-layouts: 19.4 us -> none
    ppermute x20 -> x10, waiting for transfers between devices: 24 us -> 7.01 us  [the longest x4 7 us: exchange(): lax.ppermute(values, 'rows', swaps(row_count, 1))]
    pallas_call x0 -> x7, Pallas kernels: none -> 12.7 us  [the longest x1 5.8 us: on_device(): pl.pallas_call(functools.partial(details_kernel, pairs, tuple((len(weight...]
    add x1 -> x0, other arithmetic: 8.09 us -> none  [on_device(): return (summed + plane, plane)]
    select_n x19 -> x0, other arithmetic: 5.68 us -> none  [the longest x10 4.37 us: mirror_rims(): jnp.where(first, jnp.flip(lax.slice_in_dim(values, 0, reach, axis=axis),...]
  transfers between devices with their start and end apart: 20 -> 10, of which waited for: 9 -> 2; matrix products, arithmetic and copies ran while one was open for 35% -> 0% of each run, Pallas kernels for 0% -> 21%
where the time goes in v2:
time: 47.8 us; the launch traced here: 47.5 us
  starting transfers between devices  25.5 us (53%)
  Pallas kernels  12.7 us (27%)
  waiting for transfers between devices  7.01 us (15%)
  local copies, waits for them, and re-layouts  1.28 us (3%)
  between operations  0.94 us (2%)
    ppermute x4, starting transfers between devices, exchange(): lax.ppermute(values, 'rows', swaps(row_count, 1))  18.6 us
    ppermute x4, waiting for transfers between devices, exchange(): lax.ppermute(values, 'rows', swaps(row_count, 1))  7 us
    pallas_call x1, Pallas kernels, on_device(): pl.pallas_call(functools.partial(details_kernel, pairs, tuple((len(weight...  5.8 us
    ppermute x1, starting transfers between devices, on_device(): two = lax.ppermute(two, 'cols', swaps(col_count, 1))  5.66 us
    pallas_call x2, Pallas kernels, smooth_rows(): pl.pallas_call(functools.partial(rows_kernel, group), out_shape=array(wid...  2.75 us
    pallas_call x1, Pallas kernels, on_device(): pl.pallas_call(coarse_two_kernel, out_shape=(array(columns), array(column...  2.7 us
    pallas_call x1, Pallas kernels, on_device(): pl.pallas_call(coarse_one_kernel, out_shape=(array(inner * PAIR),) * 2, i...  1.38 us
    unnamed x20, local copies, waits for them, and re-layouts  1.28 us
  transfers between devices with their start and end apart: 10, of which 2 were waited for; matrix products, arithmetic and copies ran while one was open for 0% of the time, Pallas kernels for 21%

profile of v2, /device:TPU:102, one launch (start us, length us, event | category | flops | bytes accessed | tf_op | source)
XLA Modules:
  0.0 47.5 jit_solution(15364763063105989151)
XLA Ops:
  0.6 0.0 copy-start.1
  0.6 1.2 %copy-done.1 = f32[32,8192]{1,0:T(8,128)S(1)} copy-done((f32[32,8192]{1,0:T(8,128)S(1)}, f32[32,8192]{1,0:T(8,128)}, u32[]{:S(2)}) %copy-start.1) | copy-done | bytes 1048600
  1.9 0.9 %collective-permute-start.2 = (f32[32,128]{1,0:T(8,128)S(1)}, f32[32,128]{1,0:T(8,128)S(1)}, u32[]{:S(2)}, u32[]{:S(2)}) collective-permute-start(f32[32,128]{1,0:T(8,128)S(1)} %get-tuple-element.10), channel_id=1, source_target_pairs={{0,1},{1,0},{2,3},{3,2},{4,5},{5,4},{6,7},{7,6},{8,9},{9,8},{10,11... | collective-permute-start | bytes 49160 | tf_op jit(solution)/shard_map/ppermute | solution.py:373
  2.8 5.7 %collective-permute-start.3 = (f32[32,128]{1,0:T(8,128)S(1)}, f32[32,128]{1,0:T(8,128)S(1)}, u32[]{:S(2)}, u32[]{:S(2)}) collective-permute-start(f32[32,128]{1,0:T(8,128)S(1)} %get-tuple-element.11), channel_id=1, source_target_pairs={{1,2},{2,1},{3,4},{4,3},{5,6},{6,5},{7,8},{8,7},{9,10},{10,9},{11,... | collective-permute-start | bytes 49160 | tf_op jit(solution)/shard_map/ppermute | solution.py:374
  8.5 4.6 %collective-permute-start.1 = (f32[32,4352]{1,0:T(8,128)S(1)}, f32[32,4352]{1,0:T(8,128)S(1)}, u32[]{:S(2)}, u32[]{:S(2)}) collective-permute-start(f32[32,4352]{1,0:T(8,128)S(1)} %get-tuple-element.9.own.refs_0_), channel_id=1, source_target_pairs={{16,32},{32,16},{48,64},{64,48},{80,96},{96,80},{112,128},{128,112... | collective-permute-start | bytes 1671176 | tf_op jit(solution)/shard_map/ppermute | solution.py:360
  13.1 0.1 collective-permute-start
  13.2 0.0 collective-permute-done.2.first
  13.2 0.0 collective-permute-done.3.second
  13.3 4.5 %collective-permute-start.5 = (f32[32,3968]{1,0:T(8,128)S(1)}, f32[32,3968]{1,0:T(8,128)S(1)}, u32[]{:S(2)}, u32[]{:S(2)}) collective-permute-start(f32[32,3968]{1,0:T(8,128)S(1)} %join.1.own.refs_1_), channel_id=1, source_target_pairs={{16,32},{32,16},{48,64},{64,48},{80,96},{96,80},{112,128},{128,112... | collective-permute-start | bytes 1523720 | tf_op jit(solution)/shard_map/ppermute | solution.py:360
  17.8 0.1 collective-permute-start.4
  17.9 5.0 %collective-permute-done.1.odd_in.refs_4_ = f32[32,4352]{1,0:T(8,128)S(1)} collective-permute-done((f32[32,4352]{1,0:T(8,128)S(1)}, f32[32,4352]{1,0:T(8,128)S(1)}, u32[]{:S(2)}, u32[]{:S(2)}) %collective-permute-start.1) | collective-permute-done | bytes 557088 | tf_op jit(solution)/shard_map/ppermute | solution.py:360
  22.9 0.0 collective-permute-done.even_in.refs_2_
  22.9 1.4 %rows_one.1.refs_6_.own.refs_0_ = f32[32,4352]{1,0:T(8,128)S(1)} custom-call(f32[32,4352]{1,0:T(8,128)S(1)} %get-tuple-element.9.own.refs_0_, f32[32,4352]{1,0:T(8,128)S(1)} %collective-permute-done.even_in.refs_2_, f32[32,4352]{1,0:T(8,128)S(1)} %collective-permute-done.1.odd_in.refs_4_), custom_call_target="tpu_custom_call" | custom-call | tf_op jit(solution)/shard_map/rows_one/pallas_call | solution.py:390
  24.4 0.0 copy-start.3
  24.4 0.0 copy-start.4
  24.4 0.0 copy-start.5
  24.4 0.0 copy-start.6
  24.5 0.0 copy-start.7
  24.5 0.0 copy-start.8
  24.5 0.0 copy-start.9
  24.5 4.8 %collective-permute-start.8 = (f32[32,4352]{1,0:T(8,128)S(1)}, f32[32,4352]{1,0:T(8,128)S(1)}, u32[]{:S(2)}, u32[]{:S(2)}) collective-permute-start(f32[32,4352]{1,0:T(8,128)S(1)} %rows_one.1.refs_6_.own.refs_0_), channel_id=1, source_target_pairs={{16,32},{32,16},{48,64},{64,48},{80,96},{96,80},{112,128},{128,112... | collective-permute-start | bytes 1671176 | tf_op jit(solution)/shard_map/ppermute | solution.py:360
  29.3 0.1 collective-permute-start.6
  29.4 0.0 collective-permute-done.5.odd_in.refs_5_
  29.4 0.0 collective-permute-done.4.even_in.refs_3_
  29.4 1.3 %rows_two.1.refs_7_.refs_1_ = f32[32,3968]{1,0:T(8,128)S(1)} custom-call(f32[32,3968]{1,0:T(8,128)S(1)} %join.1.own.refs_1_, f32[32,3968]{1,0:T(8,128)S(1)} %collective-permute-done.4.even_in.refs_3_, f32[32,3968]{1,0:T(8,128)S(1)} %collective-permute-done.5.odd_in.refs_5_), custom_call_target="tpu_custom_call" | custom-call | tf_op jit(solution)/shard_map/rows_two/pallas_call | solution.py:390
  30.7 0.0 copy-start
  30.7 0.0 copy-start.2
  30.7 4.7 %collective-permute-start.9 = (f32[32,3968]{1,0:T(8,128)S(1)}, f32[32,3968]{1,0:T(8,128)S(1)}, u32[]{:S(2)}, u32[]{:S(2)}) collective-permute-start(f32[32,3968]{1,0:T(8,128)S(1)} %rows_two.1.refs_7_.refs_1_), channel_id=1, source_target_pairs={{16,32},{32,16},{48,64},{64,48},{80,96},{96,80},{112,128},{128,112... | collective-permute-start | bytes 1523720 | tf_op jit(solution)/shard_map/ppermute | solution.py:360
  35.4 0.1 collective-permute-start.7
  35.5 0.0 copy-done.3
  35.5 0.0 copy-done.4
  35.5 0.0 copy-done.5
  35.5 0.0 copy-done.6
  35.5 0.0 copy-done.7
  35.5 0.0 copy-done.8
  35.6 0.0 copy-done.9
  35.6 5.8 %details.1 = (f32[32,8192]{1,0:T(8,128)S(1)}, f32[32,8192]{1,0:T(8,128)S(1)}) custom-call(f32[5]{0:T(128)S(1)} %copy-done.9, f32[32,4352]{1,0:T(8,128)S(1)} %get-tuple-element.9.own.refs_0_, f32[32,3968]{1,0:T(8,128)S(1)} %join.1.own.refs_1_, f32[32,4352]{1,0:T(8,128)S(1)} %collective-permute-done.even_in.refs_2_, ...), custom_call_target="tpu_custom_call" | custom-call | tf_op jit(solution)/shard_map/details/pallas_call | solution.py:410
  41.4 0.0 collective-permute-done.8.odd_in.refs_4_
  41.4 0.0 collective-permute-done.6.even_in.refs_2_
  41.4 0.0 copy-done
  41.4 0.0 copy-done.2
  41.4 1.4 %coarse_one.1 = (f32[32,3840]{1,0:T(8,128)S(1)}, f32[32,3840]{1,0:T(8,128)S(1)}) custom-call(f32[5]{0:T(128)S(1)} %copy-done.9, f32[32,4352]{1,0:T(8,128)S(1)} %rows_one.1.refs_6_.own.refs_0_, f32[32,4352]{1,0:T(8,128)S(1)} %collective-permute-done.6.even_in.refs_2_, f32[32,4352]{1,0:T(8,128)S(1)} %collective-permute-done.8.odd_in.refs_4_, ...), custom_call_target="tpu_custom_call" | custom-call | tf_op jit(solution)/shard_map/coarse_one/pallas_call | solution.py:423
  42.8 2.0 %collective-permute-done.9.refs_5_ = f32[32,3968]{1,0:T(8,128)S(1)} collective-permute-done((f32[32,3968]{1,0:T(8,128)S(1)}, f32[32,3968]{1,0:T(8,128)S(1)}, u32[]{:S(2)}, u32[]{:S(2)}) %collective-permute-start.9) | collective-permute-done | bytes 507936 | tf_op jit(solution)/shard_map/ppermute | solution.py:360
  44.8 0.0 collective-permute-done.7.refs_3_
  44.8 2.7 %coarse_two.1 = (f32[32,8192]{1,0:T(8,128)}, f32[32,8192]{1,0:T(8,128)}) custom-call(f32[5]{0:T(128)S(1)} %copy-done.9, f32[32,4352]{1,0:T(8,128)S(1)} %rows_one.1.refs_6_.own.refs_0_, f32[32,3968]{1,0:T(8,128)S(1)} %rows_two.1.refs_7_.refs_1_, f32[32,4352]{1,0:T(8,128)S(1)} %collective-permute-done.6.even_in.refs_2_, ...), custom_call_target="tpu_custom_call" | custom-call | tf_op jit(solution)/shard_map/coarse_two/pallas_call | solution.py:433
  (2 shorter events, 0.1 us)
Async XLA Ops:
  0.6 1.2 %copy-start.1 = (f32[32,8192]{1,0:T(8,128)S(1)}, f32[32,8192]{1,0:T(8,128)}, u32[]{:S(2)}) copy-start(f32[32,8192]{1,0:T(8,128)} %sky.3) | copy-start | bytes 3145732
  1.9 11.3 %collective-permute-start.2 = (f32[32,128]{1,0:T(8,128)S(1)}, f32[32,128]{1,0:T(8,128)S(1)}, u32[]{:S(2)}, u32[]{:S(2)}) collective-permute-start(f32[32,128]{1,0:T(8,128)S(1)} %get-tuple-element.10), channel_id=1, source_target_pairs={{0,1},{1,0},{2,3},{3,2},{4,5},{5,4},{6,7},{7,6},{8,9},{9,8},{10,11... | collective-permute-start | bytes 49160 | tf_op jit(solution)/shard_map/ppermute | solution.py:373
  2.8 10.4 %collective-permute-start.3 = (f32[32,128]{1,0:T(8,128)S(1)}, f32[32,128]{1,0:T(8,128)S(1)}, u32[]{:S(2)}, u32[]{:S(2)}) collective-permute-start(f32[32,128]{1,0:T(8,128)S(1)} %get-tuple-element.11), channel_id=1, source_target_pairs={{1,2},{2,1},{3,4},{4,3},{5,6},{6,5},{7,8},{8,7},{9,10},{10,9},{11,... | collective-permute-start | bytes 49160 | tf_op jit(solution)/shard_map/ppermute | solution.py:374
  8.5 14.5 %collective-permute-start.1 = (f32[32,4352]{1,0:T(8,128)S(1)}, f32[32,4352]{1,0:T(8,128)S(1)}, u32[]{:S(2)}, u32[]{:S(2)}) collective-permute-start(f32[32,4352]{1,0:T(8,128)S(1)} %get-tuple-element.9.own.refs_0_), channel_id=1, source_target_pairs={{16,32},{32,16},{48,64},{64,48},{80,96},{96,80},{112,128},{128,112... | collective-permute-start | bytes 1671176 | tf_op jit(solution)/shard_map/ppermute | solution.py:360
  13.1 9.8 %collective-permute-start = (f32[32,4352]{1,0:T(8,128)S(1)}, f32[32,4352]{1,0:T(8,128)S(1)}, u32[]{:S(2)}, u32[]{:S(2)}) collective-permute-start(f32[32,4352]{1,0:T(8,128)S(1)} %get-tuple-element.9.own.refs_0_), channel_id=1, source_target_pairs={{0,16},{16,0},{32,48},{48,32},{64,80},{80,64},{96,112},{112,96},{1... | collective-permute-start | bytes 1671176 | tf_op jit(solution)/shard_map/ppermute | solution.py:359
  13.3 16.1 %collective-permute-start.5 = (f32[32,3968]{1,0:T(8,128)S(1)}, f32[32,3968]{1,0:T(8,128)S(1)}, u32[]{:S(2)}, u32[]{:S(2)}) collective-permute-start(f32[32,3968]{1,0:T(8,128)S(1)} %join.1.own.refs_1_), channel_id=1, source_target_pairs={{16,32},{32,16},{48,64},{64,48},{80,96},{96,80},{112,128},{128,112... | collective-permute-start | bytes 1523720 | tf_op jit(solution)/shard_map/ppermute | solution.py:360
  17.8 11.5 %collective-permute-start.4 = (f32[32,3968]{1,0:T(8,128)S(1)}, f32[32,3968]{1,0:T(8,128)S(1)}, u32[]{:S(2)}, u32[]{:S(2)}) collective-permute-start(f32[32,3968]{1,0:T(8,128)S(1)} %join.1.own.refs_1_), channel_id=1, source_target_pairs={{0,16},{16,0},{32,48},{48,32},{64,80},{80,64},{96,112},{112,96},{1... | collective-permute-start | bytes 1523720 | tf_op jit(solution)/shard_map/ppermute | solution.py:359
  24.4 11.1 %copy-start.3 = (bf16[768,256]{1,0:T(8,128)(2,1)S(1)}, bf16[768,256]{1,0:T(8,128)(2,1)}, u32[]{:S(2)}) copy-start(bf16[768,256]{1,0:T(8,128)(2,1)} %constant.20.clone.refs_12_) | copy-start | bytes 1179652
  24.4 11.1 %copy-start.4 = (bf16[768,256]{1,0:T(8,128)(2,1)S(1)}, bf16[768,256]{1,0:T(8,128)(2,1)}, u32[]{:S(2)}) copy-start(bf16[768,256]{1,0:T(8,128)(2,1)} %constant.18.clone.refs_10_) | copy-start | bytes 1179652
  24.4 11.1 %copy-start.5 = (bf16[768,256]{1,0:T(8,128)(2,1)S(1)}, bf16[768,256]{1,0:T(8,128)(2,1)}, u32[]{:S(2)}) copy-start(bf16[768,256]{1,0:T(8,128)(2,1)} %constant.17.clone.refs_9_) | copy-start | bytes 1179652
  24.4 11.1 %copy-start.6 = (bf16[768,256]{1,0:T(8,128)(2,1)S(1)}, bf16[768,256]{1,0:T(8,128)(2,1)}, u32[]{:S(2)}) copy-start(bf16[768,256]{1,0:T(8,128)(2,1)} %constant.16.clone.refs_8_) | copy-start | bytes 1179652
  24.5 11.1 %copy-start.7 = (bf16[384,256]{1,0:T(8,128)(2,1)S(1)}, bf16[384,256]{1,0:T(8,128)(2,1)}, u32[]{:S(2)}) copy-start(bf16[384,256]{1,0:T(8,128)(2,1)} %constant.21.clone.refs_13_) | copy-start | bytes 589828
  24.5 11.1 %copy-start.8 = (bf16[384,256]{1,0:T(8,128)(2,1)S(1)}, bf16[384,256]{1,0:T(8,128)(2,1)}, u32[]{:S(2)}) copy-start(bf16[384,256]{1,0:T(8,128)(2,1)} %constant.19.clone.refs_11_) | copy-start | bytes 589828
  24.5 11.1 %copy-start.9 = (f32[5]{0:T(128)S(1)}, f32[5]{0:T(128)}, u32[]{:S(2)}) copy-start(f32[5]{0:T(128)} %levels.5) | copy-start | bytes 64
  24.5 16.9 %collective-permute-start.8 = (f32[32,4352]{1,0:T(8,128)S(1)}, f32[32,4352]{1,0:T(8,128)S(1)}, u32[]{:S(2)}, u32[]{:S(2)}) collective-permute-start(f32[32,4352]{1,0:T(8,128)S(1)} %rows_one.1.refs_6_.own.refs_0_), channel_id=1, source_target_pairs={{16,32},{32,16},{48,64},{64,48},{80,96},{96,80},{112,128},{128,112... | collective-permute-start | bytes 1671176 | tf_op jit(solution)/shard_map/ppermute | solution.py:360
  29.3 12.1 %collective-permute-start.6 = (f32[32,4352]{1,0:T(8,128)S(1)}, f32[32,4352]{1,0:T(8,128)S(1)}, u32[]{:S(2)}, u32[]{:S(2)}) collective-permute-start(f32[32,4352]{1,0:T(8,128)S(1)} %rows_one.1.refs_6_.own.refs_0_), channel_id=1, source_target_pairs={{0,16},{16,0},{32,48},{48,32},{64,80},{80,64},{96,112},{112,96},{1... | collective-permute-start | bytes 1671176 | tf_op jit(solution)/shard_map/ppermute | solution.py:359
  30.7 10.7 %copy-start = (bf16[768,256]{1,0:T(8,128)(2,1)S(1)}, bf16[768,256]{1,0:T(8,128)(2,1)}, u32[]{:S(2)}) copy-start(bf16[768,256]{1,0:T(8,128)(2,1)} %constant.22.clone.high.refs_8_) | copy-start | bytes 1179652
  30.7 10.7 %copy-start.2 = (bf16[384,256]{1,0:T(8,128)(2,1)S(1)}, bf16[384,256]{1,0:T(8,128)(2,1)}, u32[]{:S(2)}) copy-start(bf16[384,256]{1,0:T(8,128)(2,1)} %constant.23.clone.low.refs_9_) | copy-start | bytes 589828
  30.7 14.1 %collective-permute-start.9 = (f32[32,3968]{1,0:T(8,128)S(1)}, f32[32,3968]{1,0:T(8,128)S(1)}, u32[]{:S(2)}, u32[]{:S(2)}) collective-permute-start(f32[32,3968]{1,0:T(8,128)S(1)} %rows_two.1.refs_7_.refs_1_), channel_id=1, source_target_pairs={{16,32},{32,16},{48,64},{64,48},{80,96},{96,80},{112,128},{128,112... | collective-permute-start | bytes 1523720 | tf_op jit(solution)/shard_map/ppermute | solution.py:360
  35.4 9.4 %collective-permute-start.7 = (f32[32,3968]{1,0:T(8,128)S(1)}, f32[32,3968]{1,0:T(8,128)S(1)}, u32[]{:S(2)}, u32[]{:S(2)}) collective-permute-start(f32[32,3968]{1,0:T(8,128)S(1)} %rows_two.1.refs_7_.refs_1_), channel_id=1, source_target_pairs={{0,16},{16,0},{32,48},{48,32},{64,80},{80,64},{96,112},{112,96},{1... | collective-permute-start | bytes 1523720 | tf_op jit(solution)/shard_map/ppermute | solution.py:359

commit v3 on v2

--- a/solution.py
+++ b/solution.py
@@ -61,7 +61,7 @@
         body(index, index - begin - whole * group)
 
 
-def with_neighbours(own, odd_in, flipped, run):
+def with_neighbours(own, odd_in, flipped, run, prepare=None):
     rows = own[0].shape[0]
     index, last = lax.axis_index("rows"), lax.axis_size("rows") - 1
     outer = jnp.logical_or(index == 0, index == last)
@@ -75,6 +75,8 @@
 
     @pl.when(jnp.logical_not(outer))
     def _():
+        if prepare is not None:
+            prepare()
         run(odd_in)
 
 
@@ -126,24 +128,33 @@
         rest[:, halo] = jnp.where(in_first, flip(sky[:, columns - LANES : columns]), left)
 
 
+def smooth_tile(group, own, even_in, odd_in, out, buffers):
+    rows = own.shape[0]
+
+    def one(block, slot):
+        zero, ones, twos = buffers[3 * slot : 3 * slot + 3]
+        columns = columns_of(block)
+        load_block(own[:, columns], even_in[:, columns], odd_in[:, columns], zero)
+        ones[...] = binomial(*taps(zero, 4, 1, 3 * rows - 8))
+        two = binomial(*taps(ones, 4, 2, 3 * rows - 16))
+        twos[...] = two
+        n = 3 * rows - 32
+        three = binomial(two[0:n], twos[4 : n + 4, :], two[8 : n + 8], twos[12 : n + 12, :], two[16 : n + 16])
+        out[:, columns] = binomial(*[three[8 * k : 8 * k + rows] for k in range(5)])
+
+    loop(0, own.shape[1] // LANES, one, group)
+
+
 def rows_kernel(group, own, even_in, odd_in, out, flipped, *buffers):
-    rows = own.shape[0]
-
     def run(odd):
-        def one(block, slot):
-            zero, ones, twos = buffers[3 * slot : 3 * slot + 3]
-            columns = columns_of(block)
-            load_block(own[:, columns], even_in[:, columns], odd[0][:, columns], zero)
-            ones[...] = binomial(*taps(zero, 4, 1, 3 * rows - 8))
-            two = binomial(*taps(ones, 4, 2, 3 * rows - 16))
-            twos[...] = two
-            n = 3 * rows - 32
-            three = binomial(two[0:n], twos[4 : n + 4, :], two[8 : n + 8], twos[12 : n + 12, :], two[16 : n + 16])
-            out[:, columns] = binomial(*[three[8 * k : 8 * k + rows] for k in range(5)])
-
-        loop(0, own.shape[1] // LANES, one, group)
+        smooth_tile(group, own, even_in, odd[0], out, buffers)
 
     with_neighbours((own,), (odd_in,), (flipped,), run)
+
+
+def far_kernel(group, after, own, even_in, odd_in, *refs):
+    out, *buffers = refs[after:]
+    smooth_tile(group, own, even_in, odd_in, out, buffers)
 
 
 def put(value, operand, rows, main=None, after=None, before=None):
@@ -283,13 +294,13 @@
 
 
 def coarse_two_kernel(levels, *refs):
-    own, even_in, odd_in, refs = refs[:2], refs[2:4], refs[4:6], refs[6:]
-    part_sum, plane, high, low, den_one, coa_one, denoised, coarse, *refs = refs
+    own, even_in, refs = refs[:2], refs[2:4], refs[4:]
+    far, part_sum, plane, high, low, den_one, coa_one, denoised, coarse, *refs = refs[:2], *refs[2:]
     flipped, (operand, den_two, coa_two, den_three, coa_three, sems) = refs[:2], refs[2:]
     rows, columns = part_sum.shape
     first, pairs = own[0].shape[1] // PAIR, columns // PAIR
     begin = first - 1
-    copies = row_copies(den_one, denoised, PAIR, sems.at[0]) + row_copies(coa_one, coarse, PAIR, sems.at[1])
+    copies = row_copies(den_one, denoised, PAIR, sems.at[6]) + row_copies(coa_one, coarse, PAIR, sems.at[7])
     for copy in copies:
         copy.start()
 
@@ -308,11 +319,11 @@
         put(one(0, 1), operand, rows, main=(0, 1))
         put(one(0, 2), operand, rows, after=0)
 
-    with_neighbours(own, odd_in, flipped, lambda odd: last_rows(own, even_in, odd, blocks))
+    with_neighbours(own, far, flipped, lambda odd: last_rows(own, even_in, odd, blocks))
     count = pairs - begin + 1
     half = count // 2
     pair_of = lambda slot: slot + begin - 1 if slot else 0
-    for start, size, den, coa, at in ((0, half, den_two, coa_two, 2), (half, count - half, den_three, coa_three, 6)):
+    for start, size, den, coa, at in ((0, half, den_two, coa_two, 0), (half, count - half, den_three, coa_three, 4)):
         finish(operand, (high, low), rows, start, size, levels[4], pair_of, part_sum, plane, den, coa)
         for source, target, k in ((den, denoised, at), (coa, coarse, at + 1)):
             if start == 0:
@@ -337,9 +348,10 @@
         for scale in range(SCALES)
     ]
 
-    any_space = pl.BlockSpec(memory_space=pl.ANY)
     in_vmem = pl.BlockSpec(memory_space=pltpu.VMEM)
     in_smem = pl.BlockSpec(memory_space=pltpu.SMEM)
+    any_space = pl.BlockSpec(memory_space=pl.ANY)
+    in_hbm = pl.BlockSpec(memory_space=pltpu.HBM)
     dma = pltpu.SemaphoreType.DMA
 
     def room(mebibytes):
@@ -354,11 +366,14 @@
     def operand(slots):
         return pltpu.VMEM((slots * rows, 2 * SPAN), BF16)
 
+    def even_swap(values):
+        return lax.ppermute(values, "rows", swaps(row_count, 0))
+
+    def odd_swap(values):
+        return lax.ppermute(values, "rows", swaps(row_count, 1))
+
     def exchange(values):
-        return (
-            lax.ppermute(values, "rows", swaps(row_count, 0)),
-            lax.ppermute(values, "rows", swaps(row_count, 1)),
-        )
+        return even_swap(values), odd_swap(values)
 
     widths = (first * LANES, (blocks - first + 1) * LANES)
     part, one, two = pl.pallas_call(
@@ -382,8 +397,11 @@
         name="join",
     )(sky, one, two)
     near.append(exchange(rest))
+    beyond = [odd_swap(even) for even, _ in near]
     own = (part, rest)
-    group = 4
+    group = 8
+
+    row_buffers = [pltpu.VMEM((3 * rows - cut, LANES), F32) for _ in range(group) for cut in (0, 8, 16)]
 
     def smooth_rows(which, name):
         width = widths[which]
@@ -392,16 +410,13 @@
             out_shape=array(width),
             in_specs=[in_vmem] * 3,
             out_specs=in_vmem,
-            scratch_shapes=[vmem(width)]
-            + [pltpu.VMEM((3 * rows - cut, LANES), F32) for _ in range(group) for cut in (0, 8, 16)],
+            scratch_shapes=[vmem(width)] + row_buffers,
             compiler_params=room(10),
             name=name,
         )(own[which], *near[which])
 
-    four = [smooth_rows(0, "rows_one")]
-    near_four = [exchange(four[0])]
-    four.append(smooth_rows(1, "rows_two"))
-    near_four.append(exchange(four[1]))
+    four = [smooth_rows(0, "rows_one"), smooth_rows(1, "rows_two")]
+    even_four = [even_swap(values) for values in four]
 
     def columnwise(pairs_of_inputs):
         return [x[0] for x in pairs_of_inputs] + [x[1] for x in pairs_of_inputs]
@@ -419,7 +434,19 @@
         name="details",
     )(thresholds, *own, *columnwise(near), *four, *fine)
 
+    def smooth_far(which, name, *after):
+        return pl.pallas_call(
+            functools.partial(far_kernel, group, len(after)),
+            out_shape=array(widths[which]),
+            in_specs=[in_vmem] * 3 + [any_space] * len(after),
+            out_specs=in_vmem,
+            scratch_shapes=row_buffers,
+            compiler_params=room(10),
+            name=name,
+        )(near[which][1], own[which], beyond[which], *after)
+
     inner = first // 2 - 2
+    far_one = smooth_far(0, "far_one")
     outs = pl.pallas_call(
         coarse_one_kernel,
         out_shape=(array(inner * PAIR),) * 2,
@@ -428,20 +455,21 @@
         scratch_shapes=[vmem(widths[0]), operand(inner + 2)],
         compiler_params=room(16),
         name="coarse_one",
-    )(thresholds, four[0], *near_four[0], part_sum, plane, *weights[4])
+    )(thresholds, four[0], even_four[0], far_one, part_sum, plane, *weights[4])
     count = pairs - inner
+    far_two = smooth_far(1, "far_two", outs[0])
     return pl.pallas_call(
         coarse_two_kernel,
         out_shape=(array(columns), array(columns)),
         in_specs=[in_smem] + [in_vmem] * 12,
-        out_specs=(pl.BlockSpec(memory_space=pltpu.HBM),) * 2,
+        out_specs=(in_hbm,) * 2,
         scratch_shapes=[vmem(w) for w in widths]
         + [operand(count + 2)]
         + [vmem(n * PAIR) for n in (count // 2, count // 2, count - count // 2, count - count // 2)]
         + [dma((8, rows // TILE))],
         compiler_params=room(16),
         name="coarse_two",
-    )(thresholds, *four, *columnwise(near_four), part_sum, plane, *weights[4], *outs)
+    )(thresholds, *four, *even_four, far_one, far_two, part_sum, plane, *weights[4], *outs)
 
 
 def solution(mesh):

time: 47.8 us -> 45.2 us (0.946); the launches traced: 47.5 us -> 44.4 us
  waiting for transfers between devices: 7.01 us -> 0.03 us
  Pallas kernels: 12.7 us -> 14.9 us
  starting transfers between devices: 25.5 us -> 27.2 us
    ppermute x8, waiting for transfers between devices: 7.01 us -> 0.02 us  [the longest x4 0.01 us: even_swap(): return lax.ppermute(values, 'rows', swaps(row_count, 0))]
    pallas_call x0 -> x2, Pallas kernels: none -> 2.43 us  [smooth_far(): pl.pallas_call(functools.partial(far_kernel, group, len(after)), out_shap...]
    ppermute x8, starting transfers between devices: 19 us -> 20.6 us  [the longest x4 20.2 us: odd_swap(): return lax.ppermute(values, 'rows', swaps(row_count, 1))]
  transfers between devices with their start and end apart: 10 -> 10, of which waited for: 2 -> 0; matrix products, arithmetic and copies ran while one was open for 0% -> 0% of each run, Pallas kernels for 21% -> 27%
where the time goes in v3:
time: 45.2 us; the launch traced here: 44.4 us
  starting transfers between devices  27.2 us (60%)
  Pallas kernels  14.9 us (33%)
  local copies, waits for them, and re-layouts  1.28 us (3%)
  between operations  0.99 us (2%)
    ppermute x4, starting transfers between devices, odd_swap(): return lax.ppermute(values, 'rows', swaps(row_count, 1))  20.2 us
    pallas_call x1, Pallas kernels, on_device(): pl.pallas_call(functools.partial(details_kernel, pairs, tuple((len(weight...  5.8 us
    ppermute x1, starting transfers between devices, on_device(): two = lax.ppermute(two, 'cols', swaps(col_count, 1))  5.66 us
    pallas_call x1, Pallas kernels, on_device(): pl.pallas_call(coarse_two_kernel, out_shape=(array(columns), array(column...  2.7 us
    pallas_call x2, Pallas kernels, smooth_rows(): pl.pallas_call(functools.partial(rows_kernel, group), out_shape=array(wid...  2.52 us
    pallas_call x2, Pallas kernels, smooth_far(): pl.pallas_call(functools.partial(far_kernel, group, len(after)), out_shap...  2.43 us
    pallas_call x1, Pallas kernels, on_device(): pl.pallas_call(coarse_one_kernel, out_shape=(array(inner * PAIR),) * 2, i...  1.38 us
    unnamed x20, local copies, waits for them, and re-layouts  1.28 us
  transfers between devices with their start and end apart: 10, of which 0 were waited for; matrix products, arithmetic and copies ran while one was open for 0% of the time, Pallas kernels for 27%

profile of v3, /device:TPU:102, one launch (start us, length us, event | category | flops | bytes accessed | tf_op | source)
XLA Modules:
  0.0 44.4 jit_solution(8512044586223767530)
XLA Ops:
  0.6 0.0 copy-start.1
  0.6 1.2 %copy-done.1 = f32[32,8192]{1,0:T(8,128)S(1)} copy-done((f32[32,8192]{1,0:T(8,128)S(1)}, f32[32,8192]{1,0:T(8,128)}, u32[]{:S(2)}) %copy-start.1) | copy-done | bytes 1048600
  1.9 0.9 %collective-permute-start.2 = (f32[32,128]{1,0:T(8,128)S(1)}, f32[32,128]{1,0:T(8,128)S(1)}, u32[]{:S(2)}, u32[]{:S(2)}) collective-permute-start(f32[32,128]{1,0:T(8,128)S(1)} %get-tuple-element.10), channel_id=1, source_target_pairs={{0,1},{1,0},{2,3},{3,2},{4,5},{5,4},{6,7},{7,6},{8,9},{9,8},{10,11... | collective-permute-start | bytes 49160 | tf_op jit(solution)/shard_map/ppermute | solution.py:388
  2.8 5.7 %collective-permute-start.3 = (f32[32,128]{1,0:T(8,128)S(1)}, f32[32,128]{1,0:T(8,128)S(1)}, u32[]{:S(2)}, u32[]{:S(2)}) collective-permute-start(f32[32,128]{1,0:T(8,128)S(1)} %get-tuple-element.11), channel_id=1, source_target_pairs={{1,2},{2,1},{3,4},{4,3},{5,6},{6,5},{7,8},{8,7},{9,10},{10,9},{11,... | collective-permute-start | bytes 49160 | tf_op jit(solution)/shard_map/ppermute | solution.py:389
  8.5 0.1 collective-permute-start
  8.6 5.9 %collective-permute-start.1 = (f32[32,4352]{1,0:T(8,128)S(1)}, f32[32,4352]{1,0:T(8,128)S(1)}, u32[]{:S(2)}, u32[]{:S(2)}) collective-permute-start(f32[32,4352]{1,0:T(8,128)S(1)} %get-tuple-element.9.own.even_in.refs_0_), channel_id=1, source_target_pairs={{16,32},{32,16},{48,64},{64,48},{80,96},{96,80},{112,128},{128,112... | collective-permute-start | bytes 1671176 | tf_op jit(solution)/shard_map/ppermute | solution.py:373
  14.4 0.0 collective-permute-done.2.first
  14.5 0.0 collective-permute-done.3.second
  14.5 0.1 collective-permute-start.4
  14.6 3.3 %collective-permute-start.5 = (f32[32,3968]{1,0:T(8,128)S(1)}, f32[32,3968]{1,0:T(8,128)S(1)}, u32[]{:S(2)}, u32[]{:S(2)}) collective-permute-start(f32[32,3968]{1,0:T(8,128)S(1)} %join.1.own.refs_1_.even_in), channel_id=1, source_target_pairs={{16,32},{32,16},{48,64},{64,48},{80,96},{96,80},{112,128},{128,112... | collective-permute-start | bytes 1523720 | tf_op jit(solution)/shard_map/ppermute | solution.py:373
  17.9 0.0 collective-permute-done.even_in.refs_2_
  18.0 5.9 %collective-permute-start.8 = (f32[32,4352]{1,0:T(8,128)S(1)}, f32[32,4352]{1,0:T(8,128)S(1)}, u32[]{:S(2)}, u32[]{:S(2)}) collective-permute-start(f32[32,4352]{1,0:T(8,128)S(1)} %collective-permute-done.even_in.refs_2_), channel_id=1, source_target_pairs={{16,32},{32,16},{48,64},{64,48},{80,96},{96,80},{112,128},{128,112... | collective-permute-start | bytes 1671176 | tf_op jit(solution)/shard_map/ppermute | solution.py:373
  23.8 0.0 collective-permute-done.1.odd_in.own.refs_4_
  23.8 1.3 %rows_one.1.refs_6_.own.refs_0_ = f32[32,4352]{1,0:T(8,128)S(1)} custom-call(f32[32,4352]{1,0:T(8,128)S(1)} %get-tuple-element.9.own.even_in.refs_0_, f32[32,4352]{1,0:T(8,128)S(1)} %collective-permute-done.even_in.refs_2_, f32[32,4352]{1,0:T(8,128)S(1)} %collective-permute-done.1.odd_in.own.refs_4_), custom_call_target="tpu_custom_call" | custom-call | tf_op jit(solution)/shard_map/rows_one/pallas_call | solution.py:408
  25.2 0.0 copy-start.3
  25.2 0.0 copy-start.4
  25.2 0.0 copy-start.5
  25.2 0.0 copy-start.6
  25.2 0.0 copy-start.7
  25.2 0.0 copy-start.8
  25.2 0.0 copy-start.9
  25.3 0.1 collective-permute-start.6
  25.4 0.0 collective-permute-done.4.even_in.refs_3_
  25.4 5.2 %collective-permute-start.9 = (f32[32,3968]{1,0:T(8,128)S(1)}, f32[32,3968]{1,0:T(8,128)S(1)}, u32[]{:S(2)}, u32[]{:S(2)}) collective-permute-start(f32[32,3968]{1,0:T(8,128)S(1)} %collective-permute-done.4.even_in.refs_3_), channel_id=1, source_target_pairs={{16,32},{32,16},{48,64},{64,48},{80,96},{96,80},{112,128},{128,112... | collective-permute-start | bytes 1523720 | tf_op jit(solution)/shard_map/ppermute | solution.py:373
  30.6 0.0 collective-permute-done.5.odd_in.refs_5_.own
  30.6 1.2 %rows_two.1.refs_7_.refs_1_ = f32[32,3968]{1,0:T(8,128)S(1)} custom-call(f32[32,3968]{1,0:T(8,128)S(1)} %join.1.own.refs_1_.even_in, f32[32,3968]{1,0:T(8,128)S(1)} %collective-permute-done.4.even_in.refs_3_, f32[32,3968]{1,0:T(8,128)S(1)} %collective-permute-done.5.odd_in.refs_5_.own), custom_call_target="tpu_custom_call" | custom-call | tf_op jit(solution)/shard_map/rows_two/pallas_call | solution.py:408
  31.8 0.1 collective-permute-start.7
  31.9 0.0 copy-done.3
  31.9 0.0 copy-done.4
  31.9 0.0 copy-done.5
  31.9 0.0 copy-done.6
  31.9 0.0 copy-done.7
  31.9 0.0 copy-done.8
  31.9 0.0 copy-done.9
  31.9 5.8 %details.1 = (f32[32,8192]{1,0:T(8,128)S(1)}, f32[32,8192]{1,0:T(8,128)S(1)}) custom-call(f32[5]{0:T(128)S(1)} %copy-done.9, f32[32,4352]{1,0:T(8,128)S(1)} %get-tuple-element.9.own.even_in.refs_0_, f32[32,3968]{1,0:T(8,128)S(1)} %join.1.own.refs_1_.even_in, f32[32,4352]{1,0:T(8,128)S(1)} %collective-permute-done.even_in.refs_2_, ...), custom_call_target="tpu_custom_call" | custom-call | tf_op jit(solution)/shard_map/details/pallas_call | solution.py:425
  37.7 0.0 copy-start
  37.7 0.0 copy-start.2
  37.8 0.0 collective-permute-done.8.odd_in
  37.8 1.3 %far_one.1.odd_in.refs_4_ = f32[32,4352]{1,0:T(8,128)S(1)} custom-call(f32[32,4352]{1,0:T(8,128)S(1)} %collective-permute-done.1.odd_in.own.refs_4_, f32[32,4352]{1,0:T(8,128)S(1)} %get-tuple-element.9.own.even_in.refs_0_, f32[32,4352]{1,0:T(8,128)S(1)} %collective-permute-done.8.odd_in), custom_call_target="tpu_custom_call" | custom-call | tf_op jit(solution)/shard_map/far_one/pallas_call | solution.py:438
  39.1 0.0 collective-permute-done.6.even_in.refs_2_
  39.1 0.0 copy-done
  39.1 0.0 copy-done.2
  39.1 1.4 %coarse_one.1 = (f32[32,3840]{1,0:T(8,128)S(1)}, f32[32,3840]{1,0:T(8,128)S(1)}) custom-call(f32[5]{0:T(128)S(1)} %copy-done.9, f32[32,4352]{1,0:T(8,128)S(1)} %rows_one.1.refs_6_.own.refs_0_, f32[32,4352]{1,0:T(8,128)S(1)} %collective-permute-done.6.even_in.refs_2_, f32[32,4352]{1,0:T(8,128)S(1)} %far_one.1.odd_in.refs_4_, ...), custom_call_target="tpu_custom_call" | custom-call | tf_op jit(solution)/shard_map/coarse_one/pallas_call | solution.py:450
  40.5 0.0 collective-permute-done.9.odd_in
  40.5 1.2 %far_two.1.refs_5_ = f32[32,3968]{1,0:T(8,128)S(1)} custom-call(f32[32,3968]{1,0:T(8,128)S(1)} %collective-permute-done.5.odd_in.refs_5_.own, f32[32,3968]{1,0:T(8,128)S(1)} %join.1.own.refs_1_.even_in, f32[32,3968]{1,0:T(8,128)S(1)} %collective-permute-done.9.odd_in, f32[32,3840]{1,0:T(8,128)S(1)} %get-tuple-element.14.refs_0_.refs_10_), custom_call_target="tpu_custom_call" | custom-call | tf_op jit(solution)/shard_map/far_two/pallas_call | solution.py:438
  41.6 0.0 collective-permute-done.7.refs_3_
  41.7 2.7 %coarse_two.1 = (f32[32,8192]{1,0:T(8,128)}, f32[32,8192]{1,0:T(8,128)}) custom-call(f32[5]{0:T(128)S(1)} %copy-done.9, f32[32,4352]{1,0:T(8,128)S(1)} %rows_one.1.refs_6_.own.refs_0_, f32[32,3968]{1,0:T(8,128)S(1)} %rows_two.1.refs_7_.refs_1_, f32[32,4352]{1,0:T(8,128)S(1)} %collective-permute-done.6.even_in.refs_2_, ...), custom_call_target="tpu_custom_call" | custom-call | tf_op jit(solution)/shard_map/coarse_two/pallas_call | solution.py:461
  (2 shorter events, 0.1 us)
Async XLA Ops:
  0.6 1.2 %copy-start.1 = (f32[32,8192]{1,0:T(8,128)S(1)}, f32[32,8192]{1,0:T(8,128)}, u32[]{:S(2)}) copy-start(f32[32,8192]{1,0:T(8,128)} %sky.3) | copy-start | bytes 3145732
  1.9 12.5 %collective-permute-start.2 = (f32[32,128]{1,0:T(8,128)S(1)}, f32[32,128]{1,0:T(8,128)S(1)}, u32[]{:S(2)}, u32[]{:S(2)}) collective-permute-start(f32[32,128]{1,0:T(8,128)S(1)} %get-tuple-element.10), channel_id=1, source_target_pairs={{0,1},{1,0},{2,3},{3,2},{4,5},{5,4},{6,7},{7,6},{8,9},{9,8},{10,11... | collective-permute-start | bytes 49160 | tf_op jit(solution)/shard_map/ppermute | solution.py:388
  2.8 11.6 %collective-permute-start.3 = (f32[32,128]{1,0:T(8,128)S(1)}, f32[32,128]{1,0:T(8,128)S(1)}, u32[]{:S(2)}, u32[]{:S(2)}) collective-permute-start(f32[32,128]{1,0:T(8,128)S(1)} %get-tuple-element.11), channel_id=1, source_target_pairs={{1,2},{2,1},{3,4},{4,3},{5,6},{6,5},{7,8},{8,7},{9,10},{10,9},{11,... | collective-permute-start | bytes 49160 | tf_op jit(solution)/shard_map/ppermute | solution.py:389
  8.5 9.5 %collective-permute-start = (f32[32,4352]{1,0:T(8,128)S(1)}, f32[32,4352]{1,0:T(8,128)S(1)}, u32[]{:S(2)}, u32[]{:S(2)}) collective-permute-start(f32[32,4352]{1,0:T(8,128)S(1)} %get-tuple-element.9.own.even_in.refs_0_), channel_id=1, source_target_pairs={{0,16},{16,0},{32,48},{48,32},{64,80},{80,64},{96,112},{112,96},{1... | collective-permute-start | bytes 1671176 | tf_op jit(solution)/shard_map/ppermute | solution.py:370
  8.6 15.2 %collective-permute-start.1 = (f32[32,4352]{1,0:T(8,128)S(1)}, f32[32,4352]{1,0:T(8,128)S(1)}, u32[]{:S(2)}, u32[]{:S(2)}) collective-permute-start(f32[32,4352]{1,0:T(8,128)S(1)} %get-tuple-element.9.own.even_in.refs_0_), channel_id=1, source_target_pairs={{16,32},{32,16},{48,64},{64,48},{80,96},{96,80},{112,128},{128,112... | collective-permute-start | bytes 1671176 | tf_op jit(solution)/shard_map/ppermute | solution.py:373
  14.5 10.8 %collective-permute-start.4 = (f32[32,3968]{1,0:T(8,128)S(1)}, f32[32,3968]{1,0:T(8,128)S(1)}, u32[]{:S(2)}, u32[]{:S(2)}) collective-permute-start(f32[32,3968]{1,0:T(8,128)S(1)} %join.1.own.refs_1_.even_in), channel_id=1, source_target_pairs={{0,16},{16,0},{32,48},{48,32},{64,80},{80,64},{96,112},{112,96},{1... | collective-permute-start | bytes 1523720 | tf_op jit(solution)/shard_map/ppermute | solution.py:370
  14.6 15.9 %collective-permute-start.5 = (f32[32,3968]{1,0:T(8,128)S(1)}, f32[32,3968]{1,0:T(8,128)S(1)}, u32[]{:S(2)}, u32[]{:S(2)}) collective-permute-start(f32[32,3968]{1,0:T(8,128)S(1)} %join.1.own.refs_1_.even_in), channel_id=1, source_target_pairs={{16,32},{32,16},{48,64},{64,48},{80,96},{96,80},{112,128},{128,112... | collective-permute-start | bytes 1523720 | tf_op jit(solution)/shard_map/ppermute | solution.py:373
  18.0 19.8 %collective-permute-start.8 = (f32[32,4352]{1,0:T(8,128)S(1)}, f32[32,4352]{1,0:T(8,128)S(1)}, u32[]{:S(2)}, u32[]{:S(2)}) collective-permute-start(f32[32,4352]{1,0:T(8,128)S(1)} %collective-permute-done.even_in.refs_2_), channel_id=1, source_target_pairs={{16,32},{32,16},{48,64},{64,48},{80,96},{96,80},{112,128},{128,112... | collective-permute-start | bytes 1671176 | tf_op jit(solution)/shard_map/ppermute | solution.py:373
  25.2 6.7 %copy-start.3 = (bf16[768,256]{1,0:T(8,128)(2,1)S(1)}, bf16[768,256]{1,0:T(8,128)(2,1)}, u32[]{:S(2)}) copy-start(bf16[768,256]{1,0:T(8,128)(2,1)} %constant.16.clone.refs_8_) | copy-start | bytes 1179652
  25.2 6.7 %copy-start.4 = (bf16[768,256]{1,0:T(8,128)(2,1)S(1)}, bf16[768,256]{1,0:T(8,128)(2,1)}, u32[]{:S(2)}) copy-start(bf16[768,256]{1,0:T(8,128)(2,1)} %constant.17.clone.refs_9_) | copy-start | bytes 1179652
  25.2 6.7 %copy-start.5 = (bf16[768,256]{1,0:T(8,128)(2,1)S(1)}, bf16[768,256]{1,0:T(8,128)(2,1)}, u32[]{:S(2)}) copy-start(bf16[768,256]{1,0:T(8,128)(2,1)} %constant.18.clone.refs_10_) | copy-start | bytes 1179652
  25.2 6.7 %copy-start.6 = (bf16[768,256]{1,0:T(8,128)(2,1)S(1)}, bf16[768,256]{1,0:T(8,128)(2,1)}, u32[]{:S(2)}) copy-start(bf16[768,256]{1,0:T(8,128)(2,1)} %constant.20.clone.refs_12_) | copy-start | bytes 1179652
  25.2 6.7 %copy-start.7 = (bf16[384,256]{1,0:T(8,128)(2,1)S(1)}, bf16[384,256]{1,0:T(8,128)(2,1)}, u32[]{:S(2)}) copy-start(bf16[384,256]{1,0:T(8,128)(2,1)} %constant.19.clone.refs_11_) | copy-start | bytes 589828
  25.2 6.7 %copy-start.8 = (bf16[384,256]{1,0:T(8,128)(2,1)S(1)}, bf16[384,256]{1,0:T(8,128)(2,1)}, u32[]{:S(2)}) copy-start(bf16[384,256]{1,0:T(8,128)(2,1)} %constant.21.clone.refs_13_) | copy-start | bytes 589828
  25.2 6.7 %copy-start.9 = (f32[5]{0:T(128)S(1)}, f32[5]{0:T(128)}, u32[]{:S(2)}) copy-start(f32[5]{0:T(128)} %levels.5) | copy-start | bytes 64
  25.3 13.8 %collective-permute-start.6 = (f32[32,4352]{1,0:T(8,128)S(1)}, f32[32,4352]{1,0:T(8,128)S(1)}, u32[]{:S(2)}, u32[]{:S(2)}) collective-permute-start(f32[32,4352]{1,0:T(8,128)S(1)} %rows_one.1.refs_6_.own.refs_0_), channel_id=1, source_target_pairs={{0,16},{16,0},{32,48},{48,32},{64,80},{80,64},{96,112},{112,96},{1... | collective-permute-start | bytes 1671176 | tf_op jit(solution)/shard_map/ppermute | solution.py:370
  25.4 15.1 %collective-permute-start.9 = (f32[32,3968]{1,0:T(8,128)S(1)}, f32[32,3968]{1,0:T(8,128)S(1)}, u32[]{:S(2)}, u32[]{:S(2)}) collective-permute-start(f32[32,3968]{1,0:T(8,128)S(1)} %collective-permute-done.4.even_in.refs_3_), channel_id=1, source_target_pairs={{16,32},{32,16},{48,64},{64,48},{80,96},{96,80},{112,128},{128,112... | collective-permute-start | bytes 1523720 | tf_op jit(solution)/shard_map/ppermute | solution.py:373
  31.8 9.9 %collective-permute-start.7 = (f32[32,3968]{1,0:T(8,128)S(1)}, f32[32,3968]{1,0:T(8,128)S(1)}, u32[]{:S(2)}, u32[]{:S(2)}) collective-permute-start(f32[32,3968]{1,0:T(8,128)S(1)} %rows_two.1.refs_7_.refs_1_), channel_id=1, source_target_pairs={{0,16},{16,0},{32,48},{48,32},{64,80},{80,64},{96,112},{112,96},{1... | collective-permute-start | bytes 1523720 | tf_op jit(solution)/shard_map/ppermute | solution.py:370
  37.7 1.3 %copy-start = (bf16[768,256]{1,0:T(8,128)(2,1)S(1)}, bf16[768,256]{1,0:T(8,128)(2,1)}, u32[]{:S(2)}) copy-start(bf16[768,256]{1,0:T(8,128)(2,1)} %constant.22.clone.high.refs_8_) | copy-start | bytes 1179652
  37.7 1.3 %copy-start.2 = (bf16[384,256]{1,0:T(8,128)(2,1)S(1)}, bf16[384,256]{1,0:T(8,128)(2,1)}, u32[]{:S(2)}) copy-start(bf16[384,256]{1,0:T(8,128)(2,1)} %constant.23.clone.low.refs_9_) | copy-start | bytes 589828

commit v4 on v3

--- a/solution.py
+++ b/solution.py
@@ -17,6 +17,7 @@
 SCALES = 5
 MEBI = 1024 * 1024
 BATCH = 16
+STEPS = 4
 F32, BF16 = jnp.float32, jnp.bfloat16
 
 
@@ -195,50 +196,60 @@
     rows = own[0].shape[0]
     first = own[0].shape[1] // PAIR
 
-    def run(odd):
-        def one(span, block, slot):
-            zero, ones, twos = buffers[3 * slot : 3 * slot + 3]
-            columns = columns_of(block)
-            load_block(own[span][:, columns], even_in[span][:, columns], odd[span][:, columns], zero)
-            ones[...] = binomial(*taps(zero, rows - 12, 1, rows + 24))
-            two = binomial(*taps(ones, 4, 2, rows + 16))
-            twos[...] = two
-            three = binomial(two[0:rows], twos[4 : rows + 4, :], two[8 : rows + 8], twos[12 : rows + 12, :], two[16 : rows + 16])
-            return ones[12 : rows + 12, :], two[8 : rows + 8], three, four[span][:, columns]
-
-        for span, begin, end in ((0, 0, first), (1, first, pairs)):
-
-            def body(pair, _):
-                block = 2 * (pair - begin)
-                left, right = one(span, block, 0), one(span, block + 1, 1)
-                for k in range(4):
-                    put(left[k], operands[k], rows, main=(pair + 1, 0), after=pair)
-                    put(right[k], operands[k], rows, main=(pair + 1, 1), before=pair + 2)
-
-            loop(begin, end, body)
-        for k, value in enumerate(one(1, 2 * (pairs - first), 0)):
-            put(value, operands[k], rows, after=pairs, before=1)
-
-    with_neighbours(own, odd_in, flipped, run)
-
-    at = 0
-    for scale in range(4):
-        use = weights[at : at + weight_counts[scale]]
-        at += weight_counts[scale]
-        level = levels[scale]
-
+    def keep(odd):
+        for source, target in zip(odd, flipped):
+            if source is not target:
+                target[...] = source[...]
+
+    with_neighbours(own, odd_in, flipped, keep)
+
+    def one(span, block, slot):
+        zero, ones, twos = buffers[3 * slot : 3 * slot + 3]
+        columns = columns_of(block)
+        load_block(own[span][:, columns], even_in[span][:, columns], flipped[span][:, columns], zero)
+        ones[...] = binomial(*taps(zero, rows - 12, 1, rows + 24))
+        two = binomial(*taps(ones, 4, 2, rows + 16))
+        twos[...] = two
+        three = binomial(two[0:rows], twos[4 : rows + 4, :], two[8 : rows + 8], twos[12 : rows + 12, :], two[16 : rows + 16])
+        return ones[12 : rows + 12, :], two[8 : rows + 8], three, four[span][:, columns]
+
+    def one_pair(span, begin, pair, slot):
+        block = 2 * (pair - begin)
+        left, right = one(span, block, 2 * slot), one(span, block + 1, 2 * slot + 1)
+        for k in range(4):
+            put(left[k], operands[k], rows, main=(pair + 1, 0), after=pair)
+            put(right[k], operands[k], rows, main=(pair + 1, 1), before=pair + 2)
+
+    for k, value in enumerate(one(1, 2 * (pairs - first), 0)):
+        put(value, operands[k], rows, after=pairs, before=1)
+    loop(0, first, lambda pair, slot: one_pair(0, 0, pair, slot), 2)
+    def columns_step(scale, start, count):
         def emit(slot, total):
             pair = slot - 1
             columns = columns_of(pair, PAIR)
             if scale == 0:
                 sky = own[0][:, columns] if pair < first else own[1][:, columns_of(pair - first, PAIR)]
-                out[:, columns] = sky - clip(sky - total, level)
+                out[:, columns] = sky - clip(sky - total, levels[scale : scale + 1, :])
             else:
-                out[:, columns] = out[:, columns] - clip(plane[:, columns] - total, level)
+                out[:, columns] = out[:, columns] - clip(plane[:, columns] - total, levels[scale : scale + 1, :])
             plane[:, columns] = total
 
-        for start in range(0, pairs, BATCH):
-            filter_columns(operands[scale], use, rows, start + 1, BATCH, emit)
+        use = weights[sum(weight_counts[:scale]) : sum(weight_counts[: scale + 1])]
+        filter_columns(operands[scale], use, rows, start + 1, count, emit)
+
+    waiting = list(range(first, pairs))
+    share = -(-len(waiting) // STEPS)
+    for scale in range(4):
+        for start in range(0, first - 1, BATCH):
+            count = min(BATCH, first - 1 - start)
+            columns_step(scale, start, count)
+            for pair in waiting[:share]:
+                one_pair(1, first, pair, pair % 4)
+            waiting = waiting[share:]
+    for pair in waiting:
+        one_pair(1, first, pair, pair % 4)
+    for scale in range(4):
+        columns_step(scale, first - 1, pairs - first + 1)
 
 
 def last_rows(own, even_in, odd, then):
@@ -290,7 +301,7 @@
         put(one(0, 2 * pairs - 2), operand, rows, after=pairs - 2)
 
     with_neighbours((own,), (odd_in,), (flipped,), lambda odd: last_rows((own,), (even_in,), odd, blocks))
-    finish(operand, (high, low), rows, 1, pairs - 2, levels[4], lambda slot: slot, part_sum, plane, denoised, coarse)
+    finish(operand, (high, low), rows, 1, pairs - 2, levels[4:5, :], lambda slot: slot, part_sum, plane, denoised, coarse)
 
 
 def coarse_two_kernel(levels, *refs):
@@ -324,7 +335,7 @@
     half = count // 2
     pair_of = lambda slot: slot + begin - 1 if slot else 0
     for start, size, den, coa, at in ((0, half, den_two, coa_two, 0), (half, count - half, den_three, coa_three, 4)):
-        finish(operand, (high, low), rows, start, size, levels[4], pair_of, part_sum, plane, den, coa)
+        finish(operand, (high, low), rows, start, size, levels[4:5, :], pair_of, part_sum, plane, den, coa)
         for source, target, k in ((den, denoised, at), (coa, coarse, at + 1)):
             if start == 0:
                 more = row_copies(source.at[:, 0:PAIR], target, 0, sems.at[k])
@@ -349,7 +360,6 @@
     ]
 
     in_vmem = pl.BlockSpec(memory_space=pltpu.VMEM)
-    in_smem = pl.BlockSpec(memory_space=pltpu.SMEM)
     any_space = pl.BlockSpec(memory_space=pl.ANY)
     in_hbm = pl.BlockSpec(memory_space=pltpu.HBM)
     dma = pltpu.SemaphoreType.DMA
@@ -375,6 +385,7 @@
     def exchange(values):
         return even_swap(values), odd_swap(values)
 
+    levels = jnp.broadcast_to(thresholds[:, None], (SCALES, PAIR))
     widths = (first * LANES, (blocks - first + 1) * LANES)
     part, one, two = pl.pallas_call(
         take_kernel,
@@ -425,14 +436,14 @@
     part_sum, plane = pl.pallas_call(
         functools.partial(details_kernel, pairs, tuple(len(weights[scale]) for scale in range(4))),
         out_shape=(array(columns), array(columns)),
-        in_specs=[in_smem] + [in_vmem] * (8 + len(fine)),
+        in_specs=[in_vmem] * (9 + len(fine)),
         out_specs=(in_vmem, in_vmem),
         scratch_shapes=[vmem(w) for w in widths]
         + [operand(pairs + 2)] * 4
-        + [pltpu.VMEM((n, LANES), F32) for _ in range(2) for n in (3 * rows, rows + 24, rows + 16)],
+        + [pltpu.VMEM((n, LANES), F32) for _ in range(8) for n in (3 * rows, rows + 24, rows + 16)],
         compiler_params=room(28),
         name="details",
-    )(thresholds, *own, *columnwise(near), *four, *fine)
+    )(levels, *own, *columnwise(near), *four, *fine)
 
     def smooth_far(which, name, *after):
         return pl.pallas_call(
@@ -450,18 +461,18 @@
     outs = pl.pallas_call(
         coarse_one_kernel,
         out_shape=(array(inner * PAIR),) * 2,
-        in_specs=[in_smem] + [in_vmem] * 7,
+        in_specs=[in_vmem] * 8,
         out_specs=(in_vmem,) * 2,
         scratch_shapes=[vmem(widths[0]), operand(inner + 2)],
         compiler_params=room(16),
         name="coarse_one",
-    )(thresholds, four[0], even_four[0], far_one, part_sum, plane, *weights[4])
+    )(levels, four[0], even_four[0], far_one, part_sum, plane, *weights[4])
     count = pairs - inner
     far_two = smooth_far(1, "far_two", outs[0])
     return pl.pallas_call(
         coarse_two_kernel,
         out_shape=(array(columns), array(columns)),
-        in_specs=[in_smem] + [in_vmem] * 12,
+        in_specs=[in_vmem] * 13,
         out_specs=(in_hbm,) * 2,
         scratch_shapes=[vmem(w) for w in widths]
         + [operand(count + 2)]
@@ -469,7 +480,7 @@
         + [dma((8, rows // TILE))],
         compiler_params=room(16),
         name="coarse_two",
-    )(thresholds, *four, *even_four, far_one, far_two, part_sum, plane, *weights[4], *outs)
+    )(levels, *four, *even_four, far_one, far_two, part_sum, plane, *weights[4], *outs)
 
 
 def solution(mesh):

time: 45.2 us -> 44.1 us (0.976)
  Pallas kernels: 14.9 us -> 12.9 us
  waiting for transfers between devices: 0.03 us -> 0.91 us
    pallas_call x1, Pallas kernels: 5.8 us -> 4.87 us  [on_device(): pl.pallas_call(functools.partial(details_kernel, pairs, tuple((len(weight...]
    ppermute x4, waiting for transfers between devices: 0.01 us -> 0.9 us  [odd_swap(): return lax.ppermute(values, 'rows', swaps(row_count, 1))]
    pallas_call x1, Pallas kernels: 1.38 us -> 0.84 us  [on_device(): pl.pallas_call(coarse_one_kernel, out_shape=(array(inner * PAIR),) * 2, i...]
    pallas_call x1, Pallas kernels: 2.7 us -> 2.17 us  [on_device(): pl.pallas_call(coarse_two_kernel, out_shape=(array(columns), array(column...]
  transfers between devices with their start and end apart: 10 -> 10, of which waited for: 0 -> 1; matrix products, arithmetic and copies ran while one was open for 0% -> 0% of each run, Pallas kernels for 27% -> 25%
where the time goes in v4:
time: 44.1 us; the launch traced here: 43.3 us
  starting transfers between devices  27.2 us (62%)
  Pallas kernels  12.9 us (29%)
  local copies, waits for them, and re-layouts  1.35 us (3%)
  between operations  0.96 us (2%)
  waiting for transfers between devices  0.91 us (2%)
    ppermute x4, starting transfers between devices, odd_swap(): return lax.ppermute(values, 'rows', swaps(row_count, 1))  20.2 us
    ppermute x1, starting transfers between devices, on_device(): two = lax.ppermute(two, 'cols', swaps(col_count, 1))  5.66 us
    pallas_call x1, Pallas kernels, on_device(): pl.pallas_call(functools.partial(details_kernel, pairs, tuple((len(weight...  4.87 us
    pallas_call x2, Pallas kernels, smooth_rows(): pl.pallas_call(functools.partial(rows_kernel, group), out_shape=array(wid...  2.54 us
    pallas_call x2, Pallas kernels, smooth_far(): pl.pallas_call(functools.partial(far_kernel, group, len(after)), out_shap...  2.43 us
    pallas_call x1, Pallas kernels, on_device(): pl.pallas_call(coarse_two_kernel, out_shape=(array(columns), array(column...  2.17 us
    unnamed x20, local copies, waits for them, and re-layouts  1.28 us
    ppermute x1, starting transfers between devices, on_device(): one = lax.ppermute(one, 'cols', swaps(col_count, 0))  0.91 us
  transfers between devices with their start and end apart: 10, of which 1 were waited for; matrix products, arithmetic and copies ran while one was open for 0% of the time, Pallas kernels for 25%

profile of v4, /device:TPU:102, one launch (start us, length us, event | category | flops | bytes accessed | tf_op | source)
XLA Modules:
  0.0 43.3 jit_solution(1763386255577015588)
XLA Ops:
  0.6 0.0 copy-start.1
  0.6 1.2 %copy-done.1 = f32[32,8192]{1,0:T(8,128)S(1)} copy-done((f32[32,8192]{1,0:T(8,128)S(1)}, f32[32,8192]{1,0:T(8,128)}, u32[]{:S(2)}) %copy-start.1) | copy-done | bytes 1048600
  1.9 0.9 %collective-permute-start.2 = (f32[32,128]{1,0:T(8,128)S(1)}, f32[32,128]{1,0:T(8,128)S(1)}, u32[]{:S(2)}, u32[]{:S(2)}) collective-permute-start(f32[32,128]{1,0:T(8,128)S(1)} %get-tuple-element.10), channel_id=1, source_target_pairs={{0,1},{1,0},{2,3},{3,2},{4,5},{5,4},{6,7},{7,6},{8,9},{9,8},{10,11... | collective-permute-start | bytes 49160 | tf_op jit(solution)/shard_map/ppermute | solution.py:399
  2.8 5.7 %collective-permute-start.3 = (f32[32,128]{1,0:T(8,128)S(1)}, f32[32,128]{1,0:T(8,128)S(1)}, u32[]{:S(2)}, u32[]{:S(2)}) collective-permute-start(f32[32,128]{1,0:T(8,128)S(1)} %get-tuple-element.11), channel_id=1, source_target_pairs={{1,2},{2,1},{3,4},{4,3},{5,6},{6,5},{7,8},{8,7},{9,10},{10,9},{11,... | collective-permute-start | bytes 49160 | tf_op jit(solution)/shard_map/ppermute | solution.py:400
  8.5 0.1 collective-permute-start
  8.6 5.9 %collective-permute-start.1 = (f32[32,4352]{1,0:T(8,128)S(1)}, f32[32,4352]{1,0:T(8,128)S(1)}, u32[]{:S(2)}, u32[]{:S(2)}) collective-permute-start(f32[32,4352]{1,0:T(8,128)S(1)} %get-tuple-element.9.own.even_in.refs_0_), channel_id=1, source_target_pairs={{16,32},{32,16},{48,64},{64,48},{80,96},{96,80},{112,128},{128,112... | collective-permute-start | bytes 1671176 | tf_op jit(solution)/shard_map/ppermute | solution.py:383
  14.4 0.0 collective-permute-done.2.first
  14.5 0.0 collective-permute-done.3.second
  14.5 0.1 collective-permute-start.4
  14.6 3.3 %collective-permute-start.5 = (f32[32,3968]{1,0:T(8,128)S(1)}, f32[32,3968]{1,0:T(8,128)S(1)}, u32[]{:S(2)}, u32[]{:S(2)}) collective-permute-start(f32[32,3968]{1,0:T(8,128)S(1)} %join.1.own.refs_1_.even_in), channel_id=1, source_target_pairs={{16,32},{32,16},{48,64},{64,48},{80,96},{96,80},{112,128},{128,112... | collective-permute-start | bytes 1523720 | tf_op jit(solution)/shard_map/ppermute | solution.py:383
  17.9 0.0 collective-permute-done.even_in.refs_2_
  18.0 5.9 %collective-permute-start.8 = (f32[32,4352]{1,0:T(8,128)S(1)}, f32[32,4352]{1,0:T(8,128)S(1)}, u32[]{:S(2)}, u32[]{:S(2)}) collective-permute-start(f32[32,4352]{1,0:T(8,128)S(1)} %collective-permute-done.even_in.refs_2_), channel_id=1, source_target_pairs={{16,32},{32,16},{48,64},{64,48},{80,96},{96,80},{112,128},{128,112... | collective-permute-start | bytes 1671176 | tf_op jit(solution)/shard_map/ppermute | solution.py:383
  23.8 0.0 collective-permute-done.1.odd_in.own.refs_4_
  23.8 1.4 %rows_one.1.refs_6_.own.refs_0_ = f32[32,4352]{1,0:T(8,128)S(1)} custom-call(f32[32,4352]{1,0:T(8,128)S(1)} %get-tuple-element.9.own.even_in.refs_0_, f32[32,4352]{1,0:T(8,128)S(1)} %collective-permute-done.even_in.refs_2_, f32[32,4352]{1,0:T(8,128)S(1)} %collective-permute-done.1.odd_in.own.refs_4_), custom_call_target="tpu_custom_call" | custom-call | tf_op jit(solution)/shard_map/rows_one/pallas_call | solution.py:419
  25.2 0.0 copy-start.9
  25.2 0.0 copy-start.3
  25.2 0.0 copy-start.4
  25.2 0.0 copy-start.5
  25.2 0.0 copy-start.6
  25.2 0.0 copy-start.7
  25.3 0.0 copy-start.8
  25.3 0.1 collective-permute-start.6
  25.4 0.0 collective-permute-done.4.even_in.refs_3_
  25.4 5.2 %collective-permute-start.9 = (f32[32,3968]{1,0:T(8,128)S(1)}, f32[32,3968]{1,0:T(8,128)S(1)}, u32[]{:S(2)}, u32[]{:S(2)}) collective-permute-start(f32[32,3968]{1,0:T(8,128)S(1)} %collective-permute-done.4.even_in.refs_3_), channel_id=1, source_target_pairs={{16,32},{32,16},{48,64},{64,48},{80,96},{96,80},{112,128},{128,112... | collective-permute-start | bytes 1523720 | tf_op jit(solution)/shard_map/ppermute | solution.py:383
  30.6 0.0 collective-permute-done.5.odd_in.refs_5_.own
  30.6 1.2 %rows_two.1.refs_7_.refs_1_ = f32[32,3968]{1,0:T(8,128)S(1)} custom-call(f32[32,3968]{1,0:T(8,128)S(1)} %join.1.own.refs_1_.even_in, f32[32,3968]{1,0:T(8,128)S(1)} %collective-permute-done.4.even_in.refs_3_, f32[32,3968]{1,0:T(8,128)S(1)} %collective-permute-done.5.odd_in.refs_5_.own), custom_call_target="tpu_custom_call" | custom-call | tf_op jit(solution)/shard_map/rows_two/pallas_call | solution.py:419
  31.8 0.1 collective-permute-start.7
  31.9 0.0 copy-done.9
  31.9 0.1 broadcast_in_dim.2.levels
  32.0 0.0 copy-done.3
  32.0 0.0 copy-done.4
  32.0 0.0 copy-done.5
  32.0 0.0 copy-done.6
  32.0 0.0 copy-done.7
  32.0 0.0 copy-done.8
  32.0 4.9 %details.1 = (f32[32,8192]{1,0:T(8,128)S(1)}, f32[32,8192]{1,0:T(8,128)S(1)}) custom-call(f32[5,256]{1,0:T(8,128)S(1)} %broadcast_in_dim.2.levels, f32[32,4352]{1,0:T(8,128)S(1)} %get-tuple-element.9.own.even_in.refs_0_, f32[32,3968]{1,0:T(8,128)S(1)} %join.1.own.refs_1_.even_in, f32[32,4352]{1,0:T(8,128)S(1)} %collective-permute-done.even_in.refs_2_, ...), custom_call_target="tpu_custom_call" | custom-call | tf_op jit(solution)/shard_map/details/pallas_call | solution.py:436
  36.9 0.0 copy-start
  36.9 0.0 copy-start.2
  36.9 0.0 collective-permute-done.8.odd_in
  36.9 1.3 %far_one.1.odd_in.refs_4_ = f32[32,4352]{1,0:T(8,128)S(1)} custom-call(f32[32,4352]{1,0:T(8,128)S(1)} %collective-permute-done.1.odd_in.own.refs_4_, f32[32,4352]{1,0:T(8,128)S(1)} %get-tuple-element.9.own.even_in.refs_0_, f32[32,4352]{1,0:T(8,128)S(1)} %collective-permute-done.8.odd_in), custom_call_target="tpu_custom_call" | custom-call | tf_op jit(solution)/shard_map/far_one/pallas_call | solution.py:449
  38.2 0.0 collective-permute-done.6.even_in.refs_2_
  38.2 0.0 copy-done
  38.2 0.0 copy-done.2
  38.2 0.8 %coarse_one.1 = (f32[32,3840]{1,0:T(8,128)S(1)}, f32[32,3840]{1,0:T(8,128)S(1)}) custom-call(f32[5,256]{1,0:T(8,128)S(1)} %broadcast_in_dim.2.levels, f32[32,4352]{1,0:T(8,128)S(1)} %rows_one.1.refs_6_.own.refs_0_, f32[32,4352]{1,0:T(8,128)S(1)} %collective-permute-done.6.even_in.refs_2_, f32[32,4352]{1,0:T(8,128)S(1)} %far_one.1.odd_in.refs_4_, ...), custom_call_target="tpu_custom_call" | custom-call | tf_op jit(solution)/shard_map/coarse_one/pallas_call | solution.py:461
  39.1 0.9 %collective-permute-done.9.odd_in = f32[32,3968]{1,0:T(8,128)S(1)} collective-permute-done((f32[32,3968]{1,0:T(8,128)S(1)}, f32[32,3968]{1,0:T(8,128)S(1)}, u32[]{:S(2)}, u32[]{:S(2)}) %collective-permute-start.9) | collective-permute-done | bytes 507936 | tf_op jit(solution)/shard_map/ppermute | solution.py:383
  40.0 1.1 %far_two.1.refs_5_ = f32[32,3968]{1,0:T(8,128)S(1)} custom-call(f32[32,3968]{1,0:T(8,128)S(1)} %collective-permute-done.5.odd_in.refs_5_.own, f32[32,3968]{1,0:T(8,128)S(1)} %join.1.own.refs_1_.even_in, f32[32,3968]{1,0:T(8,128)S(1)} %collective-permute-done.9.odd_in, f32[32,3840]{1,0:T(8,128)S(1)} %get-tuple-element.14.refs_0_.refs_10_), custom_call_target="tpu_custom_call" | custom-call | tf_op jit(solution)/shard_map/far_two/pallas_call | solution.py:449
  41.1 0.0 collective-permute-done.7.refs_3_
  41.1 2.2 %coarse_two.1 = (f32[32,8192]{1,0:T(8,128)}, f32[32,8192]{1,0:T(8,128)}) custom-call(f32[5,256]{1,0:T(8,128)S(1)} %broadcast_in_dim.2.levels, f32[32,4352]{1,0:T(8,128)S(1)} %rows_one.1.refs_6_.own.refs_0_, f32[32,3968]{1,0:T(8,128)S(1)} %rows_two.1.refs_7_.refs_1_, f32[32,4352]{1,0:T(8,128)S(1)} %collective-permute-done.6.even_in.refs_2_, ...), custom_call_target="tpu_custom_call" | custom-call | tf_op jit(solution)/shard_map/coarse_two/pallas_call | solution.py:472
  (2 shorter events, 0.1 us)
Async XLA Ops:
  0.6 1.2 %copy-start.1 = (f32[32,8192]{1,0:T(8,128)S(1)}, f32[32,8192]{1,0:T(8,128)}, u32[]{:S(2)}) copy-start(f32[32,8192]{1,0:T(8,128)} %sky.3) | copy-start | bytes 3145732
  1.9 12.5 %collective-permute-start.2 = (f32[32,128]{1,0:T(8,128)S(1)}, f32[32,128]{1,0:T(8,128)S(1)}, u32[]{:S(2)}, u32[]{:S(2)}) collective-permute-start(f32[32,128]{1,0:T(8,128)S(1)} %get-tuple-element.10), channel_id=1, source_target_pairs={{0,1},{1,0},{2,3},{3,2},{4,5},{5,4},{6,7},{7,6},{8,9},{9,8},{10,11... | collective-permute-start | bytes 49160 | tf_op jit(solution)/shard_map/ppermute | solution.py:399
  2.8 11.6 %collective-permute-start.3 = (f32[32,128]{1,0:T(8,128)S(1)}, f32[32,128]{1,0:T(8,128)S(1)}, u32[]{:S(2)}, u32[]{:S(2)}) collective-permute-start(f32[32,128]{1,0:T(8,128)S(1)} %get-tuple-element.11), channel_id=1, source_target_pairs={{1,2},{2,1},{3,4},{4,3},{5,6},{6,5},{7,8},{8,7},{9,10},{10,9},{11,... | collective-permute-start | bytes 49160 | tf_op jit(solution)/shard_map/ppermute | solution.py:400
  8.5 9.5 %collective-permute-start = (f32[32,4352]{1,0:T(8,128)S(1)}, f32[32,4352]{1,0:T(8,128)S(1)}, u32[]{:S(2)}, u32[]{:S(2)}) collective-permute-start(f32[32,4352]{1,0:T(8,128)S(1)} %get-tuple-element.9.own.even_in.refs_0_), channel_id=1, source_target_pairs={{0,16},{16,0},{32,48},{48,32},{64,80},{80,64},{96,112},{112,96},{1... | collective-permute-start | bytes 1671176 | tf_op jit(solution)/shard_map/ppermute | solution.py:380
  8.6 15.2 %collective-permute-start.1 = (f32[32,4352]{1,0:T(8,128)S(1)}, f32[32,4352]{1,0:T(8,128)S(1)}, u32[]{:S(2)}, u32[]{:S(2)}) collective-permute-start(f32[32,4352]{1,0:T(8,128)S(1)} %get-tuple-element.9.own.even_in.refs_0_), channel_id=1, source_target_pairs={{16,32},{32,16},{48,64},{64,48},{80,96},{96,80},{112,128},{128,112... | collective-permute-start | bytes 1671176 | tf_op jit(solution)/shard_map/ppermute | solution.py:383
  14.5 10.9 %collective-permute-start.4 = (f32[32,3968]{1,0:T(8,128)S(1)}, f32[32,3968]{1,0:T(8,128)S(1)}, u32[]{:S(2)}, u32[]{:S(2)}) collective-permute-start(f32[32,3968]{1,0:T(8,128)S(1)} %join.1.own.refs_1_.even_in), channel_id=1, source_target_pairs={{0,16},{16,0},{32,48},{48,32},{64,80},{80,64},{96,112},{112,96},{1... | collective-permute-start | bytes 1523720 | tf_op jit(solution)/shard_map/ppermute | solution.py:380
  14.6 16.0 %collective-permute-start.5 = (f32[32,3968]{1,0:T(8,128)S(1)}, f32[32,3968]{1,0:T(8,128)S(1)}, u32[]{:S(2)}, u32[]{:S(2)}) collective-permute-start(f32[32,3968]{1,0:T(8,128)S(1)} %join.1.own.refs_1_.even_in), channel_id=1, source_target_pairs={{16,32},{32,16},{48,64},{64,48},{80,96},{96,80},{112,128},{128,112... | collective-permute-start | bytes 1523720 | tf_op jit(solution)/shard_map/ppermute | solution.py:383
  18.0 18.9 %collective-permute-start.8 = (f32[32,4352]{1,0:T(8,128)S(1)}, f32[32,4352]{1,0:T(8,128)S(1)}, u32[]{:S(2)}, u32[]{:S(2)}) collective-permute-start(f32[32,4352]{1,0:T(8,128)S(1)} %collective-permute-done.even_in.refs_2_), channel_id=1, source_target_pairs={{16,32},{32,16},{48,64},{64,48},{80,96},{96,80},{112,128},{128,112... | collective-permute-start | bytes 1671176 | tf_op jit(solution)/shard_map/ppermute | solution.py:383
  25.2 6.7 %copy-start.9 = (f32[5]{0:T(128)S(1)}, f32[5]{0:T(128)}, u32[]{:S(2)}) copy-start(f32[5]{0:T(128)} %param.11) | copy-start | bytes 64
  25.2 6.8 %copy-start.3 = (bf16[768,256]{1,0:T(8,128)(2,1)S(1)}, bf16[768,256]{1,0:T(8,128)(2,1)}, u32[]{:S(2)}) copy-start(bf16[768,256]{1,0:T(8,128)(2,1)} %constant.16.clone.refs_8_) | copy-start | bytes 1179652
  25.2 6.8 %copy-start.4 = (bf16[768,256]{1,0:T(8,128)(2,1)S(1)}, bf16[768,256]{1,0:T(8,128)(2,1)}, u32[]{:S(2)}) copy-start(bf16[768,256]{1,0:T(8,128)(2,1)} %constant.17.clone.refs_9_) | copy-start | bytes 1179652
  25.2 6.7 %copy-start.5 = (bf16[768,256]{1,0:T(8,128)(2,1)S(1)}, bf16[768,256]{1,0:T(8,128)(2,1)}, u32[]{:S(2)}) copy-start(bf16[768,256]{1,0:T(8,128)(2,1)} %constant.18.clone.refs_10_) | copy-start | bytes 1179652
  25.2 6.7 %copy-start.6 = (bf16[768,256]{1,0:T(8,128)(2,1)S(1)}, bf16[768,256]{1,0:T(8,128)(2,1)}, u32[]{:S(2)}) copy-start(bf16[768,256]{1,0:T(8,128)(2,1)} %constant.20.clone.refs_12_) | copy-start | bytes 1179652
  25.2 6.7 %copy-start.7 = (bf16[384,256]{1,0:T(8,128)(2,1)S(1)}, bf16[384,256]{1,0:T(8,128)(2,1)}, u32[]{:S(2)}) copy-start(bf16[384,256]{1,0:T(8,128)(2,1)} %constant.19.clone.refs_11_) | copy-start | bytes 589828
  25.3 6.7 %copy-start.8 = (bf16[384,256]{1,0:T(8,128)(2,1)S(1)}, bf16[384,256]{1,0:T(8,128)(2,1)}, u32[]{:S(2)}) copy-start(bf16[384,256]{1,0:T(8,128)(2,1)} %constant.21.clone.refs_13_) | copy-start | bytes 589828
  25.3 12.9 %collective-permute-start.6 = (f32[32,4352]{1,0:T(8,128)S(1)}, f32[32,4352]{1,0:T(8,128)S(1)}, u32[]{:S(2)}, u32[]{:S(2)}) collective-permute-start(f32[32,4352]{1,0:T(8,128)S(1)} %rows_one.1.refs_6_.own.refs_0_), channel_id=1, source_target_pairs={{0,16},{16,0},{32,48},{48,32},{64,80},{80,64},{96,112},{112,96},{1... | collective-permute-start | bytes 1671176 | tf_op jit(solution)/shard_map/ppermute | solution.py:380
  25.4 14.6 %collective-permute-start.9 = (f32[32,3968]{1,0:T(8,128)S(1)}, f32[32,3968]{1,0:T(8,128)S(1)}, u32[]{:S(2)}, u32[]{:S(2)}) collective-permute-start(f32[32,3968]{1,0:T(8,128)S(1)} %collective-permute-done.4.even_in.refs_3_), channel_id=1, source_target_pairs={{16,32},{32,16},{48,64},{64,48},{80,96},{96,80},{112,128},{128,112... | collective-permute-start | bytes 1523720 | tf_op jit(solution)/shard_map/ppermute | solution.py:383
  31.8 9.3 %collective-permute-start.7 = (f32[32,3968]{1,0:T(8,128)S(1)}, f32[32,3968]{1,0:T(8,128)S(1)}, u32[]{:S(2)}, u32[]{:S(2)}) collective-permute-start(f32[32,3968]{1,0:T(8,128)S(1)} %rows_two.1.refs_7_.refs_1_), channel_id=1, source_target_pairs={{0,16},{16,0},{32,48},{48,32},{64,80},{80,64},{96,112},{112,96},{1... | collective-permute-start | bytes 1523720 | tf_op jit(solution)/shard_map/ppermute | solution.py:380
  36.9 1.3 %copy-start = (bf16[768,256]{1,0:T(8,128)(2,1)S(1)}, bf16[768,256]{1,0:T(8,128)(2,1)}, u32[]{:S(2)}) copy-start(bf16[768,256]{1,0:T(8,128)(2,1)} %constant.22.clone.high.refs_8_) | copy-start | bytes 1179652
  36.9 1.3 %copy-start.2 = (bf16[384,256]{1,0:T(8,128)(2,1)S(1)}, bf16[384,256]{1,0:T(8,128)(2,1)}, u32[]{:S(2)}) copy-start(bf16[384,256]{1,0:T(8,128)(2,1)} %constant.23.clone.low.refs_9_) | copy-start | bytes 589828

commit v5 on v4

--- a/solution.py
+++ b/solution.py
@@ -16,7 +16,7 @@
 TILE = 8
 SCALES = 5
 MEBI = 1024 * 1024
-BATCH = 16
+BATCH = 18
 STEPS = 4
 F32, BF16 = jnp.float32, jnp.bfloat16
 
@@ -353,7 +353,7 @@
     rows, columns = sky.shape
     row_count, col_count = lax.axis_size("rows"), lax.axis_size("cols")
     blocks, pairs = columns // LANES, columns // PAIR
-    first = blocks // 2 + 2
+    first = blocks // 2 + 6
     weights = [
         [jnp.asarray(w if k else np.concatenate([w, w])) for k, w in enumerate(column_weights(scale + 1))]
         for scale in range(SCALES)

time: 44.1 us -> 43.1 us (0.977); the launches traced: 43.3 us -> 42.9 us
  starting transfers between devices: 27.2 us -> 26 us
  waiting for transfers between devices: 0.91 us -> 1.67 us
    ppermute x4, starting transfers between devices: 20.2 us -> 18.6 us  [odd_swap(): return lax.ppermute(values, 'rows', swaps(row_count, 1))]
    ppermute x4, waiting for transfers between devices: 0.9 us -> 1.65 us  [odd_swap(): return lax.ppermute(values, 'rows', swaps(row_count, 1))]
    ppermute x4, starting transfers between devices: 0.37 us -> 0.84 us  [even_swap(): return lax.ppermute(values, 'rows', swaps(row_count, 0))]
  transfers between devices with their start and end apart: 10 -> 10, of which waited for: 1 -> 2; matrix products, arithmetic and copies ran while one was open for 0% -> 0% of each run, Pallas kernels for 25% -> 25%
where the time goes in v5:
time: 43.1 us; the launch traced here: 42.9 us
  starting transfers between devices  26 us (60%)
  Pallas kernels  12.9 us (30%)
  waiting for transfers between devices  1.67 us (4%)
  local copies, waits for them, and re-layouts  1.34 us (3%)
  between operations  0.92 us (2%)
    ppermute x4, starting transfers between devices, odd_swap(): return lax.ppermute(values, 'rows', swaps(row_count, 1))  18.6 us
    ppermute x1, starting transfers between devices, on_device(): two = lax.ppermute(two, 'cols', swaps(col_count, 1))  5.66 us
    pallas_call x1, Pallas kernels, on_device(): pl.pallas_call(functools.partial(details_kernel, pairs, tuple((len(weight...  4.93 us
    pallas_call x2, Pallas kernels, smooth_rows(): pl.pallas_call(functools.partial(rows_kernel, group), out_shape=array(wid...  2.53 us
    pallas_call x2, Pallas kernels, smooth_far(): pl.pallas_call(functools.partial(far_kernel, group, len(after)), out_shap...  2.43 us
    pallas_call x1, Pallas kernels, on_device(): pl.pallas_call(coarse_two_kernel, out_shape=(array(columns), array(column...  2.03 us
    ppermute x4, waiting for transfers between devices, odd_swap(): return lax.ppermute(values, 'rows', swaps(row_count, 1))  1.65 us
    unnamed x20, local copies, waits for them, and re-layouts  1.27 us
  transfers between devices with their start and end apart: 10, of which 2 were waited for; matrix products, arithmetic and copies ran while one was open for 0% of the time, Pallas kernels for 25%

profile of v5, /device:TPU:102, one launch (start us, length us, event | category | flops | bytes accessed | tf_op | source)
XLA Modules:
  0.0 42.9 jit_solution(5345560429605495894)
XLA Ops:
  0.6 0.0 copy-start.1
  0.6 1.2 %copy-done.1 = f32[32,8192]{1,0:T(8,128)S(1)} copy-done((f32[32,8192]{1,0:T(8,128)S(1)}, f32[32,8192]{1,0:T(8,128)}, u32[]{:S(2)}) %copy-start.1) | copy-done | bytes 1048600
  1.9 0.9 %collective-permute-start.2 = (f32[32,128]{1,0:T(8,128)S(1)}, f32[32,128]{1,0:T(8,128)S(1)}, u32[]{:S(2)}, u32[]{:S(2)}) collective-permute-start(f32[32,128]{1,0:T(8,128)S(1)} %get-tuple-element.10), channel_id=1, source_target_pairs={{0,1},{1,0},{2,3},{3,2},{4,5},{5,4},{6,7},{7,6},{8,9},{9,8},{10,11... | collective-permute-start | bytes 49160 | tf_op jit(solution)/shard_map/ppermute | solution.py:399
  2.8 5.7 %collective-permute-start.3 = (f32[32,128]{1,0:T(8,128)S(1)}, f32[32,128]{1,0:T(8,128)S(1)}, u32[]{:S(2)}, u32[]{:S(2)}) collective-permute-start(f32[32,128]{1,0:T(8,128)S(1)} %get-tuple-element.11), channel_id=1, source_target_pairs={{1,2},{2,1},{3,4},{4,3},{5,6},{6,5},{7,8},{8,7},{9,10},{10,9},{11,... | collective-permute-start | bytes 49160 | tf_op jit(solution)/shard_map/ppermute | solution.py:400
  8.5 4.6 %collective-permute-start.1 = (f32[32,4864]{1,0:T(8,128)S(1)}, f32[32,4864]{1,0:T(8,128)S(1)}, u32[]{:S(2)}, u32[]{:S(2)}) collective-permute-start(f32[32,4864]{1,0:T(8,128)S(1)} %get-tuple-element.9.own.even_in.refs_0_), channel_id=1, source_target_pairs={{16,32},{32,16},{48,64},{64,48},{80,96},{96,80},{112,128},{128,112... | collective-permute-start | bytes 1867784 | tf_op jit(solution)/shard_map/ppermute | solution.py:383
  13.1 0.1 collective-permute-start
  13.2 0.0 collective-permute-done.2.first
  13.2 0.0 collective-permute-done.3.second
  13.3 0.6 %collective-permute-start.4 = (f32[32,3456]{1,0:T(8,128)S(1)}, f32[32,3456]{1,0:T(8,128)S(1)}, u32[]{:S(2)}, u32[]{:S(2)}) collective-permute-start(f32[32,3456]{1,0:T(8,128)S(1)} %join.1.own.refs_1_.even_in), channel_id=1, source_target_pairs={{0,16},{16,0},{32,48},{48,32},{64,80},{80,64},{96,112},{112,96},{1... | collective-permute-start | bytes 1327112 | tf_op jit(solution)/shard_map/ppermute | solution.py:380
  13.9 4.5 %collective-permute-start.5 = (f32[32,3456]{1,0:T(8,128)S(1)}, f32[32,3456]{1,0:T(8,128)S(1)}, u32[]{:S(2)}, u32[]{:S(2)}) collective-permute-start(f32[32,3456]{1,0:T(8,128)S(1)} %join.1.own.refs_1_.even_in), channel_id=1, source_target_pairs={{16,32},{32,16},{48,64},{64,48},{80,96},{96,80},{112,128},{128,112... | collective-permute-start | bytes 1327112 | tf_op jit(solution)/shard_map/ppermute | solution.py:383
  18.4 0.0 collective-permute-done.even_in.refs_2_
  18.4 4.6 %collective-permute-start.8 = (f32[32,4864]{1,0:T(8,128)S(1)}, f32[32,4864]{1,0:T(8,128)S(1)}, u32[]{:S(2)}, u32[]{:S(2)}) collective-permute-start(f32[32,4864]{1,0:T(8,128)S(1)} %collective-permute-done.even_in.refs_2_), channel_id=1, source_target_pairs={{16,32},{32,16},{48,64},{64,48},{80,96},{96,80},{112,128},{128,112... | collective-permute-start | bytes 1867784 | tf_op jit(solution)/shard_map/ppermute | solution.py:383
  23.1 0.6 %collective-permute-done.1.odd_in.own.refs_4_ = f32[32,4864]{1,0:T(8,128)S(1)} collective-permute-done((f32[32,4864]{1,0:T(8,128)S(1)}, f32[32,4864]{1,0:T(8,128)S(1)}, u32[]{:S(2)}, u32[]{:S(2)}) %collective-permute-start.1) | collective-permute-done | bytes 622624 | tf_op jit(solution)/shard_map/ppermute | solution.py:383
  23.7 0.0 copy-start.9
  23.7 0.0 copy-start.8
  23.7 1.5 %rows_one.1.refs_6_.own.refs_0_ = f32[32,4864]{1,0:T(8,128)S(1)} custom-call(f32[32,4864]{1,0:T(8,128)S(1)} %get-tuple-element.9.own.even_in.refs_0_, f32[32,4864]{1,0:T(8,128)S(1)} %collective-permute-done.even_in.refs_2_, f32[32,4864]{1,0:T(8,128)S(1)} %collective-permute-done.1.odd_in.own.refs_4_), custom_call_target="tpu_custom_call" | custom-call | tf_op jit(solution)/shard_map/rows_one/pallas_call | solution.py:419
  25.1 0.0 copy-start.3
  25.2 0.0 copy-start.4
  25.2 0.0 copy-start.5
  25.2 0.0 copy-start.6
  25.2 0.0 copy-start.7
  25.2 0.1 collective-permute-start.6
  25.3 0.0 collective-permute-done.4.even_in.refs_3_
  25.3 4.8 %collective-permute-start.9 = (f32[32,3456]{1,0:T(8,128)S(1)}, f32[32,3456]{1,0:T(8,128)S(1)}, u32[]{:S(2)}, u32[]{:S(2)}) collective-permute-start(f32[32,3456]{1,0:T(8,128)S(1)} %collective-permute-done.4.even_in.refs_3_), channel_id=1, source_target_pairs={{16,32},{32,16},{48,64},{64,48},{80,96},{96,80},{112,128},{128,112... | collective-permute-start | bytes 1327112 | tf_op jit(solution)/shard_map/ppermute | solution.py:383
  30.1 0.0 collective-permute-done.5.odd_in.refs_5_.own
  30.1 1.1 %rows_two.1.refs_7_.refs_1_ = f32[32,3456]{1,0:T(8,128)S(1)} custom-call(f32[32,3456]{1,0:T(8,128)S(1)} %join.1.own.refs_1_.even_in, f32[32,3456]{1,0:T(8,128)S(1)} %collective-permute-done.4.even_in.refs_3_, f32[32,3456]{1,0:T(8,128)S(1)} %collective-permute-done.5.odd_in.refs_5_.own), custom_call_target="tpu_custom_call" | custom-call | tf_op jit(solution)/shard_map/rows_two/pallas_call | solution.py:419
  31.2 0.1 collective-permute-start.7
  31.3 0.0 copy-done.9
  31.3 0.1 broadcast_in_dim.2.levels
  31.3 0.0 copy-done.8
  31.3 0.0 copy-done.3
  31.3 0.0 copy-done.4
  31.4 0.0 copy-done.5
  31.4 0.0 copy-done.6
  31.4 0.0 copy-done.7
  31.4 4.9 %details.1 = (f32[32,8192]{1,0:T(8,128)S(1)}, f32[32,8192]{1,0:T(8,128)S(1)}) custom-call(f32[5,256]{1,0:T(8,128)S(1)} %broadcast_in_dim.2.levels, f32[32,4864]{1,0:T(8,128)S(1)} %get-tuple-element.9.own.even_in.refs_0_, f32[32,3456]{1,0:T(8,128)S(1)} %join.1.own.refs_1_.even_in, f32[32,4864]{1,0:T(8,128)S(1)} %collective-permute-done.even_in.refs_2_, ...), custom_call_target="tpu_custom_call" | custom-call | tf_op jit(solution)/shard_map/details/pallas_call | solution.py:436
  36.3 0.0 copy-start
  36.3 0.0 copy-start.2
  36.3 0.0 collective-permute-done.8.odd_in
  36.3 1.4 %far_one.1.odd_in.refs_4_ = f32[32,4864]{1,0:T(8,128)S(1)} custom-call(f32[32,4864]{1,0:T(8,128)S(1)} %collective-permute-done.1.odd_in.own.refs_4_, f32[32,4864]{1,0:T(8,128)S(1)} %get-tuple-element.9.own.even_in.refs_0_, f32[32,4864]{1,0:T(8,128)S(1)} %collective-permute-done.8.odd_in), custom_call_target="tpu_custom_call" | custom-call | tf_op jit(solution)/shard_map/far_one/pallas_call | solution.py:449
  37.8 0.0 collective-permute-done.6.even_in.refs_2_
  37.8 0.0 copy-done
  37.8 0.0 copy-done.2
  37.8 0.9 %coarse_one.1 = (f32[32,4352]{1,0:T(8,128)S(1)}, f32[32,4352]{1,0:T(8,128)S(1)}) custom-call(f32[5,256]{1,0:T(8,128)S(1)} %broadcast_in_dim.2.levels, f32[32,4864]{1,0:T(8,128)S(1)} %rows_one.1.refs_6_.own.refs_0_, f32[32,4864]{1,0:T(8,128)S(1)} %collective-permute-done.6.even_in.refs_2_, f32[32,4864]{1,0:T(8,128)S(1)} %far_one.1.odd_in.refs_4_, ...), custom_call_target="tpu_custom_call" | custom-call | tf_op jit(solution)/shard_map/coarse_one/pallas_call | solution.py:461
  38.7 1.1 %collective-permute-done.9.odd_in = f32[32,3456]{1,0:T(8,128)S(1)} collective-permute-done((f32[32,3456]{1,0:T(8,128)S(1)}, f32[32,3456]{1,0:T(8,128)S(1)}, u32[]{:S(2)}, u32[]{:S(2)}) %collective-permute-start.9) | collective-permute-done | bytes 442400 | tf_op jit(solution)/shard_map/ppermute | solution.py:383
  39.8 1.0 %far_two.1.refs_5_ = f32[32,3456]{1,0:T(8,128)S(1)} custom-call(f32[32,3456]{1,0:T(8,128)S(1)} %collective-permute-done.5.odd_in.refs_5_.own, f32[32,3456]{1,0:T(8,128)S(1)} %join.1.own.refs_1_.even_in, f32[32,3456]{1,0:T(8,128)S(1)} %collective-permute-done.9.odd_in, f32[32,4352]{1,0:T(8,128)S(1)} %get-tuple-element.14.refs_0_.refs_10_), custom_call_target="tpu_custom_call" | custom-call | tf_op jit(solution)/shard_map/far_two/pallas_call | solution.py:449
  40.8 0.0 collective-permute-done.7.refs_3_
  40.8 2.0 %coarse_two.1 = (f32[32,8192]{1,0:T(8,128)}, f32[32,8192]{1,0:T(8,128)}) custom-call(f32[5,256]{1,0:T(8,128)S(1)} %broadcast_in_dim.2.levels, f32[32,4864]{1,0:T(8,128)S(1)} %rows_one.1.refs_6_.own.refs_0_, f32[32,3456]{1,0:T(8,128)S(1)} %rows_two.1.refs_7_.refs_1_, f32[32,4864]{1,0:T(8,128)S(1)} %collective-permute-done.6.even_in.refs_2_, ...), custom_call_target="tpu_custom_call" | custom-call | tf_op jit(solution)/shard_map/coarse_two/pallas_call | solution.py:472
  (2 shorter events, 0.1 us)
Async XLA Ops:
  0.6 1.2 %copy-start.1 = (f32[32,8192]{1,0:T(8,128)S(1)}, f32[32,8192]{1,0:T(8,128)}, u32[]{:S(2)}) copy-start(f32[32,8192]{1,0:T(8,128)} %sky.3) | copy-start | bytes 3145732
  1.9 11.3 %collective-permute-start.2 = (f32[32,128]{1,0:T(8,128)S(1)}, f32[32,128]{1,0:T(8,128)S(1)}, u32[]{:S(2)}, u32[]{:S(2)}) collective-permute-start(f32[32,128]{1,0:T(8,128)S(1)} %get-tuple-element.10), channel_id=1, source_target_pairs={{0,1},{1,0},{2,3},{3,2},{4,5},{5,4},{6,7},{7,6},{8,9},{9,8},{10,11... | collective-permute-start | bytes 49160 | tf_op jit(solution)/shard_map/ppermute | solution.py:399
  2.8 10.4 %collective-permute-start.3 = (f32[32,128]{1,0:T(8,128)S(1)}, f32[32,128]{1,0:T(8,128)S(1)}, u32[]{:S(2)}, u32[]{:S(2)}) collective-permute-start(f32[32,128]{1,0:T(8,128)S(1)} %get-tuple-element.11), channel_id=1, source_target_pairs={{1,2},{2,1},{3,4},{4,3},{5,6},{6,5},{7,8},{8,7},{9,10},{10,9},{11,... | collective-permute-start | bytes 49160 | tf_op jit(solution)/shard_map/ppermute | solution.py:400
  8.5 15.2 %collective-permute-start.1 = (f32[32,4864]{1,0:T(8,128)S(1)}, f32[32,4864]{1,0:T(8,128)S(1)}, u32[]{:S(2)}, u32[]{:S(2)}) collective-permute-start(f32[32,4864]{1,0:T(8,128)S(1)} %get-tuple-element.9.own.even_in.refs_0_), channel_id=1, source_target_pairs={{16,32},{32,16},{48,64},{64,48},{80,96},{96,80},{112,128},{128,112... | collective-permute-start | bytes 1867784 | tf_op jit(solution)/shard_map/ppermute | solution.py:383
  13.1 5.3 %collective-permute-start = (f32[32,4864]{1,0:T(8,128)S(1)}, f32[32,4864]{1,0:T(8,128)S(1)}, u32[]{:S(2)}, u32[]{:S(2)}) collective-permute-start(f32[32,4864]{1,0:T(8,128)S(1)} %get-tuple-element.9.own.even_in.refs_0_), channel_id=1, source_target_pairs={{0,16},{16,0},{32,48},{48,32},{64,80},{80,64},{96,112},{112,96},{1... | collective-permute-start | bytes 1867784 | tf_op jit(solution)/shard_map/ppermute | solution.py:380
  13.3 12.0 %collective-permute-start.4 = (f32[32,3456]{1,0:T(8,128)S(1)}, f32[32,3456]{1,0:T(8,128)S(1)}, u32[]{:S(2)}, u32[]{:S(2)}) collective-permute-start(f32[32,3456]{1,0:T(8,128)S(1)} %join.1.own.refs_1_.even_in), channel_id=1, source_target_pairs={{0,16},{16,0},{32,48},{48,32},{64,80},{80,64},{96,112},{112,96},{1... | collective-permute-start | bytes 1327112 | tf_op jit(solution)/shard_map/ppermute | solution.py:380
  13.9 16.2 %collective-permute-start.5 = (f32[32,3456]{1,0:T(8,128)S(1)}, f32[32,3456]{1,0:T(8,128)S(1)}, u32[]{:S(2)}, u32[]{:S(2)}) collective-permute-start(f32[32,3456]{1,0:T(8,128)S(1)} %join.1.own.refs_1_.even_in), channel_id=1, source_target_pairs={{16,32},{32,16},{48,64},{64,48},{80,96},{96,80},{112,128},{128,112... | collective-permute-start | bytes 1327112 | tf_op jit(solution)/shard_map/ppermute | solution.py:383
  18.4 17.9 %collective-permute-start.8 = (f32[32,4864]{1,0:T(8,128)S(1)}, f32[32,4864]{1,0:T(8,128)S(1)}, u32[]{:S(2)}, u32[]{:S(2)}) collective-permute-start(f32[32,4864]{1,0:T(8,128)S(1)} %collective-permute-done.even_in.refs_2_), channel_id=1, source_target_pairs={{16,32},{32,16},{48,64},{64,48},{80,96},{96,80},{112,128},{128,112... | collective-permute-start | bytes 1867784 | tf_op jit(solution)/shard_map/ppermute | solution.py:383
  23.7 7.6 %copy-start.9 = (f32[5]{0:T(128)S(1)}, f32[5]{0:T(128)}, u32[]{:S(2)}) copy-start(f32[5]{0:T(128)} %param.11) | copy-start | bytes 64
  23.7 7.7 %copy-start.8 = (bf16[384,256]{1,0:T(8,128)(2,1)S(1)}, bf16[384,256]{1,0:T(8,128)(2,1)}, u32[]{:S(2)}) copy-start(bf16[384,256]{1,0:T(8,128)(2,1)} %constant.19.clone.refs_11_) | copy-start | bytes 589828
  25.1 6.2 %copy-start.3 = (bf16[768,256]{1,0:T(8,128)(2,1)S(1)}, bf16[768,256]{1,0:T(8,128)(2,1)}, u32[]{:S(2)}) copy-start(bf16[768,256]{1,0:T(8,128)(2,1)} %constant.20.clone.refs_12_) | copy-start | bytes 1179652
  25.2 6.2 %copy-start.4 = (bf16[768,256]{1,0:T(8,128)(2,1)S(1)}, bf16[768,256]{1,0:T(8,128)(2,1)}, u32[]{:S(2)}) copy-start(bf16[768,256]{1,0:T(8,128)(2,1)} %constant.18.clone.refs_10_) | copy-start | bytes 1179652
  25.2 6.2 %copy-start.5 = (bf16[768,256]{1,0:T(8,128)(2,1)S(1)}, bf16[768,256]{1,0:T(8,128)(2,1)}, u32[]{:S(2)}) copy-start(bf16[768,256]{1,0:T(8,128)(2,1)} %constant.17.clone.refs_9_) | copy-start | bytes 1179652
  25.2 6.2 %copy-start.6 = (bf16[768,256]{1,0:T(8,128)(2,1)S(1)}, bf16[768,256]{1,0:T(8,128)(2,1)}, u32[]{:S(2)}) copy-start(bf16[768,256]{1,0:T(8,128)(2,1)} %constant.16.clone.refs_8_) | copy-start | bytes 1179652
  25.2 6.2 %copy-start.7 = (bf16[384,256]{1,0:T(8,128)(2,1)S(1)}, bf16[384,256]{1,0:T(8,128)(2,1)}, u32[]{:S(2)}) copy-start(bf16[384,256]{1,0:T(8,128)(2,1)} %constant.21.clone.refs_13_) | copy-start | bytes 589828
  25.2 12.6 %collective-permute-start.6 = (f32[32,4864]{1,0:T(8,128)S(1)}, f32[32,4864]{1,0:T(8,128)S(1)}, u32[]{:S(2)}, u32[]{:S(2)}) collective-permute-start(f32[32,4864]{1,0:T(8,128)S(1)} %rows_one.1.refs_6_.own.refs_0_), channel_id=1, source_target_pairs={{0,16},{16,0},{32,48},{48,32},{64,80},{80,64},{96,112},{112,96},{1... | collective-permute-start | bytes 1867784 | tf_op jit(solution)/shard_map/ppermute | solution.py:380
  25.3 14.5 %collective-permute-start.9 = (f32[32,3456]{1,0:T(8,128)S(1)}, f32[32,3456]{1,0:T(8,128)S(1)}, u32[]{:S(2)}, u32[]{:S(2)}) collective-permute-start(f32[32,3456]{1,0:T(8,128)S(1)} %collective-permute-done.4.even_in.refs_3_), channel_id=1, source_target_pairs={{16,32},{32,16},{48,64},{64,48},{80,96},{96,80},{112,128},{128,112... | collective-permute-start | bytes 1327112 | tf_op jit(solution)/shard_map/ppermute | solution.py:383
  31.2 9.7 %collective-permute-start.7 = (f32[32,3456]{1,0:T(8,128)S(1)}, f32[32,3456]{1,0:T(8,128)S(1)}, u32[]{:S(2)}, u32[]{:S(2)}) collective-permute-start(f32[32,3456]{1,0:T(8,128)S(1)} %rows_two.1.refs_7_.refs_1_), channel_id=1, source_target_pairs={{0,16},{16,0},{32,48},{48,32},{64,80},{80,64},{96,112},{112,96},{1... | collective-permute-start | bytes 1327112 | tf_op jit(solution)/shard_map/ppermute | solution.py:380
  36.3 1.5 %copy-start = (bf16[768,256]{1,0:T(8,128)(2,1)S(1)}, bf16[768,256]{1,0:T(8,128)(2,1)}, u32[]{:S(2)}) copy-start(bf16[768,256]{1,0:T(8,128)(2,1)} %constant.22.clone.high.refs_8_) | copy-start | bytes 1179652
  36.3 1.5 %copy-start.2 = (bf16[384,256]{1,0:T(8,128)(2,1)S(1)}, bf16[384,256]{1,0:T(8,128)(2,1)}, u32[]{:S(2)}) copy-start(bf16[384,256]{1,0:T(8,128)(2,1)} %constant.23.clone.low.refs_9_) | copy-start | bytes 589828

commit v6 on v5

--- a/solution.py
+++ b/solution.py
@@ -129,7 +129,7 @@
         rest[:, halo] = jnp.where(in_first, flip(sky[:, columns - LANES : columns]), left)
 
 
-def smooth_tile(group, own, even_in, odd_in, out, buffers):
+def smooth_tile(group, own, even_in, odd_in, out, buffers, kept=None):
     rows = own.shape[0]
 
     def one(block, slot):
@@ -142,13 +142,17 @@
         n = 3 * rows - 32
         three = binomial(two[0:n], twos[4 : n + 4, :], two[8 : n + 8], twos[12 : n + 12, :], two[16 : n + 16])
         out[:, columns] = binomial(*[three[8 * k : 8 * k + rows] for k in range(5)])
+        if kept is not None:
+            kept[0][:, columns] = ones[rows - 4 : 2 * rows - 4, :]
+            kept[1][:, columns] = two[rows - 8 : 2 * rows - 8]
+            kept[2][:, columns] = three[rows - 16 : 2 * rows - 16]
 
     loop(0, own.shape[1] // LANES, one, group)
 
 
-def rows_kernel(group, own, even_in, odd_in, out, flipped, *buffers):
+def rows_kernel(group, own, even_in, odd_in, ones, twos, threes, out, flipped, *buffers):
     def run(odd):
-        smooth_tile(group, own, even_in, odd[0], out, buffers)
+        smooth_tile(group, own, even_in, odd[0], out, buffers, (ones, twos, threes))
 
     with_neighbours((own,), (odd_in,), (flipped,), run)
 
@@ -189,40 +193,25 @@
 
 
 def details_kernel(pairs, weight_counts, levels, *refs):
-    own, even_in, odd_in, four, refs = refs[:2], refs[2:4], refs[4:6], refs[6:8], refs[8:]
+    own, smoothed, refs = refs[:2], (refs[2:6], refs[6:10]), refs[10:]
     weights, refs = refs[: sum(weight_counts)], refs[sum(weight_counts) :]
-    out, plane, refs = refs[0], refs[1], refs[2:]
-    flipped, operands, buffers = refs[:2], refs[2:6], refs[6:]
+    out, plane, *operands = refs
     rows = own[0].shape[0]
     first = own[0].shape[1] // PAIR
 
-    def keep(odd):
-        for source, target in zip(odd, flipped):
-            if source is not target:
-                target[...] = source[...]
-
-    with_neighbours(own, odd_in, flipped, keep)
-
-    def one(span, block, slot):
-        zero, ones, twos = buffers[3 * slot : 3 * slot + 3]
-        columns = columns_of(block)
-        load_block(own[span][:, columns], even_in[span][:, columns], flipped[span][:, columns], zero)
-        ones[...] = binomial(*taps(zero, rows - 12, 1, rows + 24))
-        two = binomial(*taps(ones, 4, 2, rows + 16))
-        twos[...] = two
-        three = binomial(two[0:rows], twos[4 : rows + 4, :], two[8 : rows + 8], twos[12 : rows + 12, :], two[16 : rows + 16])
-        return ones[12 : rows + 12, :], two[8 : rows + 8], three, four[span][:, columns]
-
-    def one_pair(span, begin, pair, slot):
+    def one(span, block):
+        return [values[:, columns_of(block)] for values in smoothed[span]]
+
+    def one_pair(span, begin, pair):
         block = 2 * (pair - begin)
-        left, right = one(span, block, 2 * slot), one(span, block + 1, 2 * slot + 1)
+        left, right = one(span, block), one(span, block + 1)
         for k in range(4):
             put(left[k], operands[k], rows, main=(pair + 1, 0), after=pair)
             put(right[k], operands[k], rows, main=(pair + 1, 1), before=pair + 2)
 
-    for k, value in enumerate(one(1, 2 * (pairs - first), 0)):
+    for k, value in enumerate(one(1, 2 * (pairs - first))):
         put(value, operands[k], rows, after=pairs, before=1)
-    loop(0, first, lambda pair, slot: one_pair(0, 0, pair, slot), 2)
+    loop(0, first, lambda pair, slot: one_pair(0, 0, pair), 2)
     def columns_step(scale, start, count):
         def emit(slot, total):
             pair = slot - 1
@@ -244,10 +233,10 @@
             count = min(BATCH, first - 1 - start)
             columns_step(scale, start, count)
             for pair in waiting[:share]:
-                one_pair(1, first, pair, pair % 4)
+                one_pair(1, first, pair)
             waiting = waiting[share:]
     for pair in waiting:
-        one_pair(1, first, pair, pair % 4)
+        one_pair(1, first, pair)
     for scale in range(4):
         columns_step(scale, first - 1, pairs - first + 1)
 
@@ -418,15 +407,16 @@
         width = widths[which]
         return pl.pallas_call(
             functools.partial(rows_kernel, group),
-            out_shape=array(width),
+            out_shape=(array(width),) * 4,
             in_specs=[in_vmem] * 3,
-            out_specs=in_vmem,
+            out_specs=(in_vmem,) * 4,
             scratch_shapes=[vmem(width)] + row_buffers,
             compiler_params=room(10),
             name=name,
         )(own[which], *near[which])
 
-    four = [smooth_rows(0, "rows_one"), smooth_rows(1, "rows_two")]
+    smoothed = [smooth_rows(0, "rows_one"), smooth_rows(1, "rows_two")]
+    four = [kept[3] for kept in smoothed]
     even_four = [even_swap(values) for values in four]
 
     def columnwise(pairs_of_inputs):
@@ -436,14 +426,12 @@
     part_sum, plane = pl.pallas_call(
         functools.partial(details_kernel, pairs, tuple(len(weights[scale]) for scale in range(4))),
         out_shape=(array(columns), array(columns)),
-        in_specs=[in_vmem] * (9 + len(fine)),
+        in_specs=[in_vmem] * (11 + len(fine)),
         out_specs=(in_vmem, in_vmem),
-        scratch_shapes=[vmem(w) for w in widths]
-        + [operand(pairs + 2)] * 4
-        + [pltpu.VMEM((n, LANES), F32) for _ in range(8) for n in (3 * rows, rows + 24, rows + 16)],
-        compiler_params=room(28),
+        scratch_shapes=[operand(pairs + 2)] * 4,
+        compiler_params=room(22),
         name="details",
-    )(levels, *own, *columnwise(near), *four, *fine)
+    )(levels, *own, *smoothed[0], *smoothed[1], *fine)
 
     def smooth_far(which, name, *after):
         return pl.pallas_call(

time: 43.1 us -> 43.1 us (level)
  Pallas kernels: 12.9 us -> 11.6 us
  waiting for transfers between devices: 1.67 us -> 2.45 us
  local copies, waits for them, and re-layouts: 1.34 us -> 1.88 us
    pallas_call x1, Pallas kernels: 4.93 us -> 3.57 us  [on_device(): pl.pallas_call(functools.partial(details_kernel, pairs, tuple((len(weight...]
    ppermute x4, waiting for transfers between devices: 1.65 us -> 2.44 us  [odd_swap(): return lax.ppermute(values, 'rows', swaps(row_count, 1))]
    unnamed x20, local copies, waits for them, and re-layouts: 1.27 us -> 1.81 us
  transfers between devices with their start and end apart: 10 -> 10, of which waited for: 2 -> 2; matrix products, arithmetic and copies ran while one was open for 0% -> 0% of each run, Pallas kernels for 25% -> 22%
where the time goes in v6:
time: 43.1 us; the launch traced here: 42.9 us
  starting transfers between devices  26 us (60%)
  Pallas kernels  11.6 us (27%)
  waiting for transfers between devices  2.45 us (6%)
  local copies, waits for them, and re-layouts  1.88 us (4%)
  between operations  0.91 us (2%)
    ppermute x4, starting transfers between devices, odd_swap(): return lax.ppermute(values, 'rows', swaps(row_count, 1))  18.6 us
    ppermute x1, starting transfers between devices, on_device(): two = lax.ppermute(two, 'cols', swaps(col_count, 1))  5.66 us
    pallas_call x1, Pallas kernels, on_device(): pl.pallas_call(functools.partial(details_kernel, pairs, tuple((len(weight...  3.57 us
    pallas_call x2, Pallas kernels, smooth_rows(): pl.pallas_call(functools.partial(rows_kernel, group), out_shape=(array(wi...  2.57 us
    ppermute x4, waiting for transfers between devices, odd_swap(): return lax.ppermute(values, 'rows', swaps(row_count, 1))  2.44 us
    pallas_call x2, Pallas kernels, smooth_far(): pl.pallas_call(functools.partial(far_kernel, group, len(after)), out_shap...  2.43 us
    pallas_call x1, Pallas kernels, on_device(): pl.pallas_call(coarse_two_kernel, out_shape=(array(columns), array(column...  2.03 us
    unnamed x20, local copies, waits for them, and re-layouts  1.81 us
  transfers between devices with their start and end apart: 10, of which 2 were waited for; matrix products, arithmetic and copies ran while one was open for 0% of the time, Pallas kernels for 22%

profile of v6, /device:TPU:102, one launch (start us, length us, event | category | flops | bytes accessed | tf_op | source)
XLA Modules:
  0.0 42.9 jit_solution(11895223770628102598)
XLA Ops:
  0.6 0.0 copy-start.1
  0.6 1.2 %copy-done.1 = f32[32,8192]{1,0:T(8,128)S(1)} copy-done((f32[32,8192]{1,0:T(8,128)S(1)}, f32[32,8192]{1,0:T(8,128)}, u32[]{:S(2)}) %copy-start.1) | copy-done | bytes 1048600
  1.9 0.9 %collective-permute-start.2 = (f32[32,128]{1,0:T(8,128)S(1)}, f32[32,128]{1,0:T(8,128)S(1)}, u32[]{:S(2)}, u32[]{:S(2)}) collective-permute-start(f32[32,128]{1,0:T(8,128)S(1)} %get-tuple-element.19), channel_id=1, source_target_pairs={{0,1},{1,0},{2,3},{3,2},{4,5},{5,4},{6,7},{7,6},{8,9},{9,8},{10,11... | collective-permute-start | bytes 49160 | tf_op jit(solution)/shard_map/ppermute | solution.py:388
  2.8 5.7 %collective-permute-start.3 = (f32[32,128]{1,0:T(8,128)S(1)}, f32[32,128]{1,0:T(8,128)S(1)}, u32[]{:S(2)}, u32[]{:S(2)}) collective-permute-start(f32[32,128]{1,0:T(8,128)S(1)} %get-tuple-element.20), channel_id=1, source_target_pairs={{1,2},{2,1},{3,4},{4,3},{5,6},{6,5},{7,8},{8,7},{9,10},{10,9},{11,... | collective-permute-start | bytes 49160 | tf_op jit(solution)/shard_map/ppermute | solution.py:389
  8.5 4.6 %collective-permute-start.1 = (f32[32,4864]{1,0:T(8,128)S(1)}, f32[32,4864]{1,0:T(8,128)S(1)}, u32[]{:S(2)}, u32[]{:S(2)}) collective-permute-start(f32[32,4864]{1,0:T(8,128)S(1)} %get-tuple-element.17.own.even_in.refs_0_), channel_id=1, source_target_pairs={{16,32},{32,16},{48,64},{64,48},{80,96},{96,80},{112,128},{128,112... | collective-permute-start | bytes 1867784 | tf_op jit(solution)/shard_map/ppermute | solution.py:372
  13.1 0.1 collective-permute-start
  13.2 0.0 collective-permute-done.2.first
  13.2 0.0 collective-permute-done.3.second
  13.3 0.6 %collective-permute-start.4 = (f32[32,3456]{1,0:T(8,128)S(1)}, f32[32,3456]{1,0:T(8,128)S(1)}, u32[]{:S(2)}, u32[]{:S(2)}) collective-permute-start(f32[32,3456]{1,0:T(8,128)S(1)} %join.1.own.refs_1_.even_in), channel_id=1, source_target_pairs={{0,16},{16,0},{32,48},{48,32},{64,80},{80,64},{96,112},{112,96},{1... | collective-permute-start | bytes 1327112 | tf_op jit(solution)/shard_map/ppermute | solution.py:369
  13.9 4.5 %collective-permute-start.5 = (f32[32,3456]{1,0:T(8,128)S(1)}, f32[32,3456]{1,0:T(8,128)S(1)}, u32[]{:S(2)}, u32[]{:S(2)}) collective-permute-start(f32[32,3456]{1,0:T(8,128)S(1)} %join.1.own.refs_1_.even_in), channel_id=1, source_target_pairs={{16,32},{32,16},{48,64},{64,48},{80,96},{96,80},{112,128},{128,112... | collective-permute-start | bytes 1327112 | tf_op jit(solution)/shard_map/ppermute | solution.py:372
  18.4 0.0 collective-permute-done.even_in
  18.4 4.6 %collective-permute-start.8 = (f32[32,4864]{1,0:T(8,128)S(1)}, f32[32,4864]{1,0:T(8,128)S(1)}, u32[]{:S(2)}, u32[]{:S(2)}) collective-permute-start(f32[32,4864]{1,0:T(8,128)S(1)} %collective-permute-done.even_in), channel_id=1, source_target_pairs={{16,32},{32,16},{48,64},{64,48},{80,96},{96,80},{112,128},{128,112... | collective-permute-start | bytes 1867784 | tf_op jit(solution)/shard_map/ppermute | solution.py:372
  23.1 0.6 %collective-permute-done.1.odd_in.own = f32[32,4864]{1,0:T(8,128)S(1)} collective-permute-done((f32[32,4864]{1,0:T(8,128)S(1)}, f32[32,4864]{1,0:T(8,128)S(1)}, u32[]{:S(2)}, u32[]{:S(2)}) %collective-permute-start.1) | collective-permute-done | bytes 622624 | tf_op jit(solution)/shard_map/ppermute | solution.py:372
  23.7 0.0 copy-start.6
  23.7 0.0 copy-start.7
  23.7 0.0 copy-start.8
  23.7 1.5 %rows_one.1 = (f32[32,4864]{1,0:T(8,128)S(1)}, f32[32,4864]{1,0:T(8,128)S(1)}, f32[32,4864]{1,0:T(8,128)S(1)}, f32[32,4864]{1,0:T(8,128)S(1)}) custom-call(f32[32,4864]{1,0:T(8,128)S(1)} %get-tuple-element.17.own.even_in.refs_0_, f32[32,4864]{1,0:T(8,128)S(1)} %collective-permute-done.even_in, f32[32,4864]{1,0:T(8,128)S(1)} %collective-permute-done.1.odd_in.own), custom_call_target="tpu_custom_call" | custom-call | tf_op jit(solution)/shard_map/rows_one/pallas_call | solution.py:408
  25.2 0.0 copy-start.3
  25.2 0.0 copy-start.4
  25.2 0.0 copy-start.5
  25.2 0.1 collective-permute-start.6
  25.3 0.0 collective-permute-done.4.even_in
  25.3 4.8 %collective-permute-start.9 = (f32[32,3456]{1,0:T(8,128)S(1)}, f32[32,3456]{1,0:T(8,128)S(1)}, u32[]{:S(2)}, u32[]{:S(2)}) collective-permute-start(f32[32,3456]{1,0:T(8,128)S(1)} %collective-permute-done.4.even_in), channel_id=1, source_target_pairs={{16,32},{32,16},{48,64},{64,48},{80,96},{96,80},{112,128},{128,112... | collective-permute-start | bytes 1327112 | tf_op jit(solution)/shard_map/ppermute | solution.py:372
  30.1 0.0 collective-permute-done.5.odd_in.own
  30.1 1.1 %rows_two.1 = (f32[32,3456]{1,0:T(8,128)S(1)}, f32[32,3456]{1,0:T(8,128)S(1)}, f32[32,3456]{1,0:T(8,128)S(1)}, f32[32,3456]{1,0:T(8,128)S(1)}) custom-call(f32[32,3456]{1,0:T(8,128)S(1)} %join.1.own.refs_1_.even_in, f32[32,3456]{1,0:T(8,128)S(1)} %collective-permute-done.4.even_in, f32[32,3456]{1,0:T(8,128)S(1)} %collective-permute-done.5.odd_in.own), custom_call_target="tpu_custom_call" | custom-call | tf_op jit(solution)/shard_map/rows_two/pallas_call | solution.py:408
  31.2 0.0 copy-start.9
  31.2 0.1 collective-permute-start.7
  31.3 0.5 %copy-done.9 = f32[5]{0:T(128)S(1)} copy-done((f32[5]{0:T(128)S(1)}, f32[5]{0:T(128)}, u32[]{:S(2)}) %copy-start.9) | copy-done | bytes 44
  31.8 0.1 broadcast_in_dim.2.levels
  31.9 0.0 copy-done.6
  31.9 0.0 copy-done.7
  31.9 0.0 copy-done.8
  31.9 0.0 copy-done.3
  31.9 0.0 copy-done.4
  31.9 0.0 copy-done.5
  31.9 3.6 %details.1 = (f32[32,8192]{1,0:T(8,128)S(1)}, f32[32,8192]{1,0:T(8,128)S(1)}) custom-call(f32[5,256]{1,0:T(8,128)S(1)} %broadcast_in_dim.2.levels, f32[32,4864]{1,0:T(8,128)S(1)} %get-tuple-element.17.own.even_in.refs_0_, f32[32,3456]{1,0:T(8,128)S(1)} %join.1.own.refs_1_.even_in, f32[32,4864]{1,0:T(8,128)S(1)} %get-tuple-element.22.refs_2_, ...), custom_call_target="tpu_custom_call" | custom-call | tf_op jit(solution)/shard_map/details/pallas_call | solution.py:426
  35.5 0.0 copy-start
  35.5 0.0 copy-start.2
  35.5 0.0 collective-permute-done.8.odd_in
  35.6 1.4 %far_one.1.odd_in.refs_4_ = f32[32,4864]{1,0:T(8,128)S(1)} custom-call(f32[32,4864]{1,0:T(8,128)S(1)} %collective-permute-done.1.odd_in.own, f32[32,4864]{1,0:T(8,128)S(1)} %get-tuple-element.17.own.even_in.refs_0_, f32[32,4864]{1,0:T(8,128)S(1)} %collective-permute-done.8.odd_in), custom_call_target="tpu_custom_call" | custom-call | tf_op jit(solution)/shard_map/far_one/pallas_call | solution.py:437
  37.0 0.0 collective-permute-done.6.even_in.refs_2_
  37.0 0.0 copy-done
  37.0 0.0 copy-done.2
  37.0 0.9 %coarse_one.1 = (f32[32,4352]{1,0:T(8,128)S(1)}, f32[32,4352]{1,0:T(8,128)S(1)}) custom-call(f32[5,256]{1,0:T(8,128)S(1)} %broadcast_in_dim.2.levels, f32[32,4864]{1,0:T(8,128)S(1)} %get-tuple-element.18.refs_5_.own.refs_0_, f32[32,4864]{1,0:T(8,128)S(1)} %collective-permute-done.6.even_in.refs_2_, f32[32,4864]{1,0:T(8,128)S(1)} %far_one.1.odd_in.refs_4_, ...), custom_call_target="tpu_custom_call" | custom-call | tf_op jit(solution)/shard_map/coarse_one/pallas_call | solution.py:449
  38.0 1.8 %collective-permute-done.9.odd_in = f32[32,3456]{1,0:T(8,128)S(1)} collective-permute-done((f32[32,3456]{1,0:T(8,128)S(1)}, f32[32,3456]{1,0:T(8,128)S(1)}, u32[]{:S(2)}, u32[]{:S(2)}) %collective-permute-start.9) | collective-permute-done | bytes 442400 | tf_op jit(solution)/shard_map/ppermute | solution.py:372
  39.8 1.0 %far_two.1.refs_5_ = f32[32,3456]{1,0:T(8,128)S(1)} custom-call(f32[32,3456]{1,0:T(8,128)S(1)} %collective-permute-done.5.odd_in.own, f32[32,3456]{1,0:T(8,128)S(1)} %join.1.own.refs_1_.even_in, f32[32,3456]{1,0:T(8,128)S(1)} %collective-permute-done.9.odd_in, f32[32,4352]{1,0:T(8,128)S(1)} %get-tuple-element.30.refs_0_.refs_10_), custom_call_target="tpu_custom_call" | custom-call | tf_op jit(solution)/shard_map/far_two/pallas_call | solution.py:437
  40.8 0.0 collective-permute-done.7.refs_3_
  40.8 2.0 %coarse_two.1 = (f32[32,8192]{1,0:T(8,128)}, f32[32,8192]{1,0:T(8,128)}) custom-call(f32[5,256]{1,0:T(8,128)S(1)} %broadcast_in_dim.2.levels, f32[32,4864]{1,0:T(8,128)S(1)} %get-tuple-element.18.refs_5_.own.refs_0_, f32[32,3456]{1,0:T(8,128)S(1)} %get-tuple-element.21.refs_9_.refs_1_, f32[32,4864]{1,0:T(8,128)S(1)} %collective-permute-done.6.even_in.refs_2_, ...), custom_call_target="tpu_custom_call" | custom-call | tf_op jit(solution)/shard_map/coarse_two/pallas_call | solution.py:460
  (2 shorter events, 0.1 us)
Async XLA Ops:
  0.6 1.2 %copy-start.1 = (f32[32,8192]{1,0:T(8,128)S(1)}, f32[32,8192]{1,0:T(8,128)}, u32[]{:S(2)}) copy-start(f32[32,8192]{1,0:T(8,128)} %sky.3) | copy-start | bytes 3145732
  1.9 11.3 %collective-permute-start.2 = (f32[32,128]{1,0:T(8,128)S(1)}, f32[32,128]{1,0:T(8,128)S(1)}, u32[]{:S(2)}, u32[]{:S(2)}) collective-permute-start(f32[32,128]{1,0:T(8,128)S(1)} %get-tuple-element.19), channel_id=1, source_target_pairs={{0,1},{1,0},{2,3},{3,2},{4,5},{5,4},{6,7},{7,6},{8,9},{9,8},{10,11... | collective-permute-start | bytes 49160 | tf_op jit(solution)/shard_map/ppermute | solution.py:388
  2.8 10.4 %collective-permute-start.3 = (f32[32,128]{1,0:T(8,128)S(1)}, f32[32,128]{1,0:T(8,128)S(1)}, u32[]{:S(2)}, u32[]{:S(2)}) collective-permute-start(f32[32,128]{1,0:T(8,128)S(1)} %get-tuple-element.20), channel_id=1, source_target_pairs={{1,2},{2,1},{3,4},{4,3},{5,6},{6,5},{7,8},{8,7},{9,10},{10,9},{11,... | collective-permute-start | bytes 49160 | tf_op jit(solution)/shard_map/ppermute | solution.py:389
  8.5 15.2 %collective-permute-start.1 = (f32[32,4864]{1,0:T(8,128)S(1)}, f32[32,4864]{1,0:T(8,128)S(1)}, u32[]{:S(2)}, u32[]{:S(2)}) collective-permute-start(f32[32,4864]{1,0:T(8,128)S(1)} %get-tuple-element.17.own.even_in.refs_0_), channel_id=1, source_target_pairs={{16,32},{32,16},{48,64},{64,48},{80,96},{96,80},{112,128},{128,112... | collective-permute-start | bytes 1867784 | tf_op jit(solution)/shard_map/ppermute | solution.py:372
  13.1 5.3 %collective-permute-start = (f32[32,4864]{1,0:T(8,128)S(1)}, f32[32,4864]{1,0:T(8,128)S(1)}, u32[]{:S(2)}, u32[]{:S(2)}) collective-permute-start(f32[32,4864]{1,0:T(8,128)S(1)} %get-tuple-element.17.own.even_in.refs_0_), channel_id=1, source_target_pairs={{0,16},{16,0},{32,48},{48,32},{64,80},{80,64},{96,112},{112,96},{1... | collective-permute-start | bytes 1867784 | tf_op jit(solution)/shard_map/ppermute | solution.py:369
  13.3 12.0 %collective-permute-start.4 = (f32[32,3456]{1,0:T(8,128)S(1)}, f32[32,3456]{1,0:T(8,128)S(1)}, u32[]{:S(2)}, u32[]{:S(2)}) collective-permute-start(f32[32,3456]{1,0:T(8,128)S(1)} %join.1.own.refs_1_.even_in), channel_id=1, source_target_pairs={{0,16},{16,0},{32,48},{48,32},{64,80},{80,64},{96,112},{112,96},{1... | collective-permute-start | bytes 1327112 | tf_op jit(solution)/shard_map/ppermute | solution.py:369
  13.9 16.2 %collective-permute-start.5 = (f32[32,3456]{1,0:T(8,128)S(1)}, f32[32,3456]{1,0:T(8,128)S(1)}, u32[]{:S(2)}, u32[]{:S(2)}) collective-permute-start(f32[32,3456]{1,0:T(8,128)S(1)} %join.1.own.refs_1_.even_in), channel_id=1, source_target_pairs={{16,32},{32,16},{48,64},{64,48},{80,96},{96,80},{112,128},{128,112... | collective-permute-start | bytes 1327112 | tf_op jit(solution)/shard_map/ppermute | solution.py:372
  18.4 17.1 %collective-permute-start.8 = (f32[32,4864]{1,0:T(8,128)S(1)}, f32[32,4864]{1,0:T(8,128)S(1)}, u32[]{:S(2)}, u32[]{:S(2)}) collective-permute-start(f32[32,4864]{1,0:T(8,128)S(1)} %collective-permute-done.even_in), channel_id=1, source_target_pairs={{16,32},{32,16},{48,64},{64,48},{80,96},{96,80},{112,128},{128,112... | collective-permute-start | bytes 1867784 | tf_op jit(solution)/shard_map/ppermute | solution.py:372
  23.7 8.3 %copy-start.6 = (bf16[768,256]{1,0:T(8,128)(2,1)S(1)}, bf16[768,256]{1,0:T(8,128)(2,1)}, u32[]{:S(2)}) copy-start(bf16[768,256]{1,0:T(8,128)(2,1)} %constant.16.clone.refs_10_) | copy-start | bytes 1179652
  23.7 8.3 %copy-start.7 = (bf16[384,256]{1,0:T(8,128)(2,1)S(1)}, bf16[384,256]{1,0:T(8,128)(2,1)}, u32[]{:S(2)}) copy-start(bf16[384,256]{1,0:T(8,128)(2,1)} %constant.21.clone.refs_15_) | copy-start | bytes 589828
  23.7 8.3 %copy-start.8 = (bf16[384,256]{1,0:T(8,128)(2,1)S(1)}, bf16[384,256]{1,0:T(8,128)(2,1)}, u32[]{:S(2)}) copy-start(bf16[384,256]{1,0:T(8,128)(2,1)} %constant.19.clone.refs_13_) | copy-start | bytes 589828
  25.2 6.8 %copy-start.3 = (bf16[768,256]{1,0:T(8,128)(2,1)S(1)}, bf16[768,256]{1,0:T(8,128)(2,1)}, u32[]{:S(2)}) copy-start(bf16[768,256]{1,0:T(8,128)(2,1)} %constant.20.clone.refs_14_) | copy-start | bytes 1179652
  25.2 6.8 %copy-start.4 = (bf16[768,256]{1,0:T(8,128)(2,1)S(1)}, bf16[768,256]{1,0:T(8,128)(2,1)}, u32[]{:S(2)}) copy-start(bf16[768,256]{1,0:T(8,128)(2,1)} %constant.18.clone.refs_12_) | copy-start | bytes 1179652
  25.2 6.8 %copy-start.5 = (bf16[768,256]{1,0:T(8,128)(2,1)S(1)}, bf16[768,256]{1,0:T(8,128)(2,1)}, u32[]{:S(2)}) copy-start(bf16[768,256]{1,0:T(8,128)(2,1)} %constant.17.clone.refs_11_) | copy-start | bytes 1179652
  25.2 11.8 %collective-permute-start.6 = (f32[32,4864]{1,0:T(8,128)S(1)}, f32[32,4864]{1,0:T(8,128)S(1)}, u32[]{:S(2)}, u32[]{:S(2)}) collective-permute-start(f32[32,4864]{1,0:T(8,128)S(1)} %get-tuple-element.18.refs_5_.own.refs_0_), channel_id=1, source_target_pairs={{0,16},{16,0},{32,48},{48,32},{64,80},{80,64},{96,112},{112,96},{1... | collective-permute-start | bytes 1867784 | tf_op jit(solution)/shard_map/ppermute | solution.py:369
  25.3 14.5 %collective-permute-start.9 = (f32[32,3456]{1,0:T(8,128)S(1)}, f32[32,3456]{1,0:T(8,128)S(1)}, u32[]{:S(2)}, u32[]{:S(2)}) collective-permute-start(f32[32,3456]{1,0:T(8,128)S(1)} %collective-permute-done.4.even_in), channel_id=1, source_target_pairs={{16,32},{32,16},{48,64},{64,48},{80,96},{96,80},{112,128},{128,112... | collective-permute-start | bytes 1327112 | tf_op jit(solution)/shard_map/ppermute | solution.py:372
  31.2 0.7 %copy-start.9 = (f32[5]{0:T(128)S(1)}, f32[5]{0:T(128)}, u32[]{:S(2)}) copy-start(f32[5]{0:T(128)} %param.11) | copy-start | bytes 64
  31.2 9.6 %collective-permute-start.7 = (f32[32,3456]{1,0:T(8,128)S(1)}, f32[32,3456]{1,0:T(8,128)S(1)}, u32[]{:S(2)}, u32[]{:S(2)}) collective-permute-start(f32[32,3456]{1,0:T(8,128)S(1)} %get-tuple-element.21.refs_9_.refs_1_), channel_id=1, source_target_pairs={{0,16},{16,0},{32,48},{48,32},{64,80},{80,64},{96,112},{112,96},{1... | collective-permute-start | bytes 1327112 | tf_op jit(solution)/shard_map/ppermute | solution.py:369
  35.5 1.5 %copy-start = (bf16[768,256]{1,0:T(8,128)(2,1)S(1)}, bf16[768,256]{1,0:T(8,128)(2,1)}, u32[]{:S(2)}) copy-start(bf16[768,256]{1,0:T(8,128)(2,1)} %constant.22.clone.high.refs_8_) | copy-start | bytes 1179652
  35.5 1.5 %copy-start.2 = (bf16[384,256]{1,0:T(8,128)(2,1)S(1)}, bf16[384,256]{1,0:T(8,128)(2,1)}, u32[]{:S(2)}) copy-start(bf16[384,256]{1,0:T(8,128)(2,1)} %constant.23.clone.low.refs_9_) | copy-start | bytes 589828

commit v7 on v6

--- a/solution.py
+++ b/solution.py
@@ -16,7 +16,7 @@
 TILE = 8
 SCALES = 5
 MEBI = 1024 * 1024
-BATCH = 18
+BATCH = 20
 STEPS = 4
 F32, BF16 = jnp.float32, jnp.bfloat16
 
@@ -342,7 +342,7 @@
     rows, columns = sky.shape
     row_count, col_count = lax.axis_size("rows"), lax.axis_size("cols")
     blocks, pairs = columns // LANES, columns // PAIR
-    first = blocks // 2 + 6
+    first = blocks // 2 + 10
     weights = [
         [jnp.asarray(w if k else np.concatenate([w, w])) for k, w in enumerate(column_weights(scale + 1))]
         for scale in range(SCALES)

time: 43.1 us -> 42.9 us (level)
  transfers between devices with their start and end apart: 10 -> 10, of which waited for: 2 -> 2; matrix products, arithmetic and copies ran while one was open for 0% -> 0% of each run, Pallas kernels for 22% -> 23%
where the time goes in v7:
time: 42.9 us; the launch traced here: 42.6 us
  starting transfers between devices  26 us (61%)
  Pallas kernels  11.7 us (27%)
  waiting for transfers between devices  2.13 us (5%)
  local copies, waits for them, and re-layouts  1.88 us (4%)
  between operations  0.91 us (2%)
    ppermute x4, starting transfers between devices, odd_swap(): return lax.ppermute(values, 'rows', swaps(row_count, 1))  18.6 us
    ppermute x1, starting transfers between devices, on_device(): two = lax.ppermute(two, 'cols', swaps(col_count, 1))  5.66 us
    pallas_call x1, Pallas kernels, on_device(): pl.pallas_call(functools.partial(details_kernel, pairs, tuple((len(weight...  3.68 us
    pallas_call x2, Pallas kernels, smooth_rows(): pl.pallas_call(functools.partial(rows_kernel, group), out_shape=(array(wi...  2.54 us
    pallas_call x2, Pallas kernels, smooth_far(): pl.pallas_call(functools.partial(far_kernel, group, len(after)), out_shap...  2.44 us
    ppermute x4, waiting for transfers between devices, odd_swap(): return lax.ppermute(values, 'rows', swaps(row_count, 1))  2.11 us
    pallas_call x1, Pallas kernels, on_device(): pl.pallas_call(coarse_two_kernel, out_shape=(array(columns), array(column...  1.91 us
    unnamed x20, local copies, waits for them, and re-layouts  1.81 us
  transfers between devices with their start and end apart: 10, of which 2 were waited for; matrix products, arithmetic and copies ran while one was open for 0% of the time, Pallas kernels for 23%

profile of v7, /device:TPU:102, one launch (start us, length us, event | category | flops | bytes accessed | tf_op | source)
XLA Modules:
  0.0 42.6 jit_solution(14507354997903329248)
XLA Ops:
  0.6 0.0 copy-start.1
  0.6 1.2 %copy-done.1 = f32[32,8192]{1,0:T(8,128)S(1)} copy-done((f32[32,8192]{1,0:T(8,128)S(1)}, f32[32,8192]{1,0:T(8,128)}, u32[]{:S(2)}) %copy-start.1) | copy-done | bytes 1048600
  1.9 0.9 %collective-permute-start.2 = (f32[32,128]{1,0:T(8,128)S(1)}, f32[32,128]{1,0:T(8,128)S(1)}, u32[]{:S(2)}, u32[]{:S(2)}) collective-permute-start(f32[32,128]{1,0:T(8,128)S(1)} %get-tuple-element.19), channel_id=1, source_target_pairs={{0,1},{1,0},{2,3},{3,2},{4,5},{5,4},{6,7},{7,6},{8,9},{9,8},{10,11... | collective-permute-start | bytes 49160 | tf_op jit(solution)/shard_map/ppermute | solution.py:388
  2.8 5.7 %collective-permute-start.3 = (f32[32,128]{1,0:T(8,128)S(1)}, f32[32,128]{1,0:T(8,128)S(1)}, u32[]{:S(2)}, u32[]{:S(2)}) collective-permute-start(f32[32,128]{1,0:T(8,128)S(1)} %get-tuple-element.20), channel_id=1, source_target_pairs={{1,2},{2,1},{3,4},{4,3},{5,6},{6,5},{7,8},{8,7},{9,10},{10,9},{11,... | collective-permute-start | bytes 49160 | tf_op jit(solution)/shard_map/ppermute | solution.py:389
  8.5 4.6 %collective-permute-start.1 = (f32[32,5376]{1,0:T(8,128)S(1)}, f32[32,5376]{1,0:T(8,128)S(1)}, u32[]{:S(2)}, u32[]{:S(2)}) collective-permute-start(f32[32,5376]{1,0:T(8,128)S(1)} %get-tuple-element.17.own.even_in.refs_0_), channel_id=1, source_target_pairs={{16,32},{32,16},{48,64},{64,48},{80,96},{96,80},{112,128},{128,112... | collective-permute-start | bytes 2064392 | tf_op jit(solution)/shard_map/ppermute | solution.py:372
  13.1 0.1 collective-permute-start
  13.2 0.0 collective-permute-done.2.first
  13.3 0.0 collective-permute-done.3.second
  13.3 0.6 %collective-permute-start.4 = (f32[32,2944]{1,0:T(8,128)S(1)}, f32[32,2944]{1,0:T(8,128)S(1)}, u32[]{:S(2)}, u32[]{:S(2)}) collective-permute-start(f32[32,2944]{1,0:T(8,128)S(1)} %join.1.own.refs_1_.even_in), channel_id=1, source_target_pairs={{0,16},{16,0},{32,48},{48,32},{64,80},{80,64},{96,112},{112,96},{1... | collective-permute-start | bytes 1130504 | tf_op jit(solution)/shard_map/ppermute | solution.py:369
  13.9 4.5 %collective-permute-start.5 = (f32[32,2944]{1,0:T(8,128)S(1)}, f32[32,2944]{1,0:T(8,128)S(1)}, u32[]{:S(2)}, u32[]{:S(2)}) collective-permute-start(f32[32,2944]{1,0:T(8,128)S(1)} %join.1.own.refs_1_.even_in), channel_id=1, source_target_pairs={{16,32},{32,16},{48,64},{64,48},{80,96},{96,80},{112,128},{128,112... | collective-permute-start | bytes 1130504 | tf_op jit(solution)/shard_map/ppermute | solution.py:372
  18.4 0.0 collective-permute-done.even_in
  18.4 4.6 %collective-permute-start.8 = (f32[32,5376]{1,0:T(8,128)S(1)}, f32[32,5376]{1,0:T(8,128)S(1)}, u32[]{:S(2)}, u32[]{:S(2)}) collective-permute-start(f32[32,5376]{1,0:T(8,128)S(1)} %collective-permute-done.even_in), channel_id=1, source_target_pairs={{16,32},{32,16},{48,64},{64,48},{80,96},{96,80},{112,128},{128,112... | collective-permute-start | bytes 2064392 | tf_op jit(solution)/shard_map/ppermute | solution.py:372
  23.1 1.3 %collective-permute-done.1.odd_in.own = f32[32,5376]{1,0:T(8,128)S(1)} collective-permute-done((f32[32,5376]{1,0:T(8,128)S(1)}, f32[32,5376]{1,0:T(8,128)S(1)}, u32[]{:S(2)}, u32[]{:S(2)}) %collective-permute-start.1) | collective-permute-done | bytes 688160 | tf_op jit(solution)/shard_map/ppermute | solution.py:372
  24.4 0.0 copy-start.5
  24.4 0.0 copy-start.6
  24.4 0.0 copy-start.8
  24.4 1.6 %rows_one.1 = (f32[32,5376]{1,0:T(8,128)S(1)}, f32[32,5376]{1,0:T(8,128)S(1)}, f32[32,5376]{1,0:T(8,128)S(1)}, f32[32,5376]{1,0:T(8,128)S(1)}) custom-call(f32[32,5376]{1,0:T(8,128)S(1)} %get-tuple-element.17.own.even_in.refs_0_, f32[32,5376]{1,0:T(8,128)S(1)} %collective-permute-done.even_in, f32[32,5376]{1,0:T(8,128)S(1)} %collective-permute-done.1.odd_in.own), custom_call_target="tpu_custom_call" | custom-call | tf_op jit(solution)/shard_map/rows_one/pallas_call | solution.py:408
  26.0 0.0 copy-start.3
  26.0 0.0 copy-start.4
  26.0 0.0 copy-start.7
  26.1 0.1 collective-permute-start.6
  26.2 0.0 collective-permute-done.4.even_in
  26.2 4.8 %collective-permute-start.9 = (f32[32,2944]{1,0:T(8,128)S(1)}, f32[32,2944]{1,0:T(8,128)S(1)}, u32[]{:S(2)}, u32[]{:S(2)}) collective-permute-start(f32[32,2944]{1,0:T(8,128)S(1)} %collective-permute-done.4.even_in), channel_id=1, source_target_pairs={{16,32},{32,16},{48,64},{64,48},{80,96},{96,80},{112,128},{128,112... | collective-permute-start | bytes 1130504 | tf_op jit(solution)/shard_map/ppermute | solution.py:372
  30.9 0.0 collective-permute-done.5.odd_in.own
  31.0 0.9 %rows_two.1 = (f32[32,2944]{1,0:T(8,128)S(1)}, f32[32,2944]{1,0:T(8,128)S(1)}, f32[32,2944]{1,0:T(8,128)S(1)}, f32[32,2944]{1,0:T(8,128)S(1)}) custom-call(f32[32,2944]{1,0:T(8,128)S(1)} %join.1.own.refs_1_.even_in, f32[32,2944]{1,0:T(8,128)S(1)} %collective-permute-done.4.even_in, f32[32,2944]{1,0:T(8,128)S(1)} %collective-permute-done.5.odd_in.own), custom_call_target="tpu_custom_call" | custom-call | tf_op jit(solution)/shard_map/rows_two/pallas_call | solution.py:408
  31.9 0.0 copy-start.9
  31.9 0.1 collective-permute-start.7
  32.0 0.5 %copy-done.9 = f32[5]{0:T(128)S(1)} copy-done((f32[5]{0:T(128)S(1)}, f32[5]{0:T(128)}, u32[]{:S(2)}) %copy-start.9) | copy-done | bytes 44
  32.5 0.1 broadcast_in_dim.2.levels
  32.6 0.0 copy-done.5
  32.6 0.0 copy-done.6
  32.6 0.0 copy-done.8
  32.6 0.0 copy-done.3
  32.6 0.0 copy-done.4
  32.6 0.0 copy-done.7
  32.6 3.7 %details.1 = (f32[32,8192]{1,0:T(8,128)S(1)}, f32[32,8192]{1,0:T(8,128)S(1)}) custom-call(f32[5,256]{1,0:T(8,128)S(1)} %broadcast_in_dim.2.levels, f32[32,5376]{1,0:T(8,128)S(1)} %get-tuple-element.17.own.even_in.refs_0_, f32[32,2944]{1,0:T(8,128)S(1)} %join.1.own.refs_1_.even_in, f32[32,5376]{1,0:T(8,128)S(1)} %get-tuple-element.22.refs_2_, ...), custom_call_target="tpu_custom_call" | custom-call | tf_op jit(solution)/shard_map/details/pallas_call | solution.py:426
  36.3 0.0 copy-start
  36.3 0.0 copy-start.2
  36.3 0.0 collective-permute-done.8.odd_in
  36.3 1.6 %far_one.1.odd_in.refs_4_ = f32[32,5376]{1,0:T(8,128)S(1)} custom-call(f32[32,5376]{1,0:T(8,128)S(1)} %collective-permute-done.1.odd_in.own, f32[32,5376]{1,0:T(8,128)S(1)} %get-tuple-element.17.own.even_in.refs_0_, f32[32,5376]{1,0:T(8,128)S(1)} %collective-permute-done.8.odd_in), custom_call_target="tpu_custom_call" | custom-call | tf_op jit(solution)/shard_map/far_one/pallas_call | solution.py:437
  37.9 0.0 collective-permute-done.6.even_in.refs_2_
  37.9 0.0 copy-done
  38.0 0.0 copy-done.2
  38.0 1.0 %coarse_one.1 = (f32[32,4864]{1,0:T(8,128)S(1)}, f32[32,4864]{1,0:T(8,128)S(1)}) custom-call(f32[5,256]{1,0:T(8,128)S(1)} %broadcast_in_dim.2.levels, f32[32,5376]{1,0:T(8,128)S(1)} %get-tuple-element.18.refs_5_.own.refs_0_, f32[32,5376]{1,0:T(8,128)S(1)} %collective-permute-done.6.even_in.refs_2_, f32[32,5376]{1,0:T(8,128)S(1)} %far_one.1.odd_in.refs_4_, ...), custom_call_target="tpu_custom_call" | custom-call | tf_op jit(solution)/shard_map/coarse_one/pallas_call | solution.py:449
  39.0 0.8 %collective-permute-done.9.odd_in = f32[32,2944]{1,0:T(8,128)S(1)} collective-permute-done((f32[32,2944]{1,0:T(8,128)S(1)}, f32[32,2944]{1,0:T(8,128)S(1)}, u32[]{:S(2)}, u32[]{:S(2)}) %collective-permute-start.9) | collective-permute-done | bytes 376864 | tf_op jit(solution)/shard_map/ppermute | solution.py:372
  39.8 0.8 %far_two.1.refs_5_ = f32[32,2944]{1,0:T(8,128)S(1)} custom-call(f32[32,2944]{1,0:T(8,128)S(1)} %collective-permute-done.5.odd_in.own, f32[32,2944]{1,0:T(8,128)S(1)} %join.1.own.refs_1_.even_in, f32[32,2944]{1,0:T(8,128)S(1)} %collective-permute-done.9.odd_in, f32[32,4864]{1,0:T(8,128)S(1)} %get-tuple-element.30.refs_0_.refs_10_), custom_call_target="tpu_custom_call" | custom-call | tf_op jit(solution)/shard_map/far_two/pallas_call | solution.py:437
  40.7 0.0 collective-permute-done.7.refs_3_
  40.7 1.9 %coarse_two.1 = (f32[32,8192]{1,0:T(8,128)}, f32[32,8192]{1,0:T(8,128)}) custom-call(f32[5,256]{1,0:T(8,128)S(1)} %broadcast_in_dim.2.levels, f32[32,5376]{1,0:T(8,128)S(1)} %get-tuple-element.18.refs_5_.own.refs_0_, f32[32,2944]{1,0:T(8,128)S(1)} %get-tuple-element.21.refs_9_.refs_1_, f32[32,5376]{1,0:T(8,128)S(1)} %collective-permute-done.6.even_in.refs_2_, ...), custom_call_target="tpu_custom_call" | custom-call | tf_op jit(solution)/shard_map/coarse_two/pallas_call | solution.py:460
  (2 shorter events, 0.1 us)
Async XLA Ops:
  0.6 1.2 %copy-start.1 = (f32[32,8192]{1,0:T(8,128)S(1)}, f32[32,8192]{1,0:T(8,128)}, u32[]{:S(2)}) copy-start(f32[32,8192]{1,0:T(8,128)} %sky.3) | copy-start | bytes 3145732
  1.9 11.3 %collective-permute-start.2 = (f32[32,128]{1,0:T(8,128)S(1)}, f32[32,128]{1,0:T(8,128)S(1)}, u32[]{:S(2)}, u32[]{:S(2)}) collective-permute-start(f32[32,128]{1,0:T(8,128)S(1)} %get-tuple-element.19), channel_id=1, source_target_pairs={{0,1},{1,0},{2,3},{3,2},{4,5},{5,4},{6,7},{7,6},{8,9},{9,8},{10,11... | collective-permute-start | bytes 49160 | tf_op jit(solution)/shard_map/ppermute | solution.py:388
  2.8 10.4 %collective-permute-start.3 = (f32[32,128]{1,0:T(8,128)S(1)}, f32[32,128]{1,0:T(8,128)S(1)}, u32[]{:S(2)}, u32[]{:S(2)}) collective-permute-start(f32[32,128]{1,0:T(8,128)S(1)} %get-tuple-element.20), channel_id=1, source_target_pairs={{1,2},{2,1},{3,4},{4,3},{5,6},{6,5},{7,8},{8,7},{9,10},{10,9},{11,... | collective-permute-start | bytes 49160 | tf_op jit(solution)/shard_map/ppermute | solution.py:389
  8.5 15.9 %collective-permute-start.1 = (f32[32,5376]{1,0:T(8,128)S(1)}, f32[32,5376]{1,0:T(8,128)S(1)}, u32[]{:S(2)}, u32[]{:S(2)}) collective-permute-start(f32[32,5376]{1,0:T(8,128)S(1)} %get-tuple-element.17.own.even_in.refs_0_), channel_id=1, source_target_pairs={{16,32},{32,16},{48,64},{64,48},{80,96},{96,80},{112,128},{128,112... | collective-permute-start | bytes 2064392 | tf_op jit(solution)/shard_map/ppermute | solution.py:372
  13.1 5.3 %collective-permute-start = (f32[32,5376]{1,0:T(8,128)S(1)}, f32[32,5376]{1,0:T(8,128)S(1)}, u32[]{:S(2)}, u32[]{:S(2)}) collective-permute-start(f32[32,5376]{1,0:T(8,128)S(1)} %get-tuple-element.17.own.even_in.refs_0_), channel_id=1, source_target_pairs={{0,16},{16,0},{32,48},{48,32},{64,80},{80,64},{96,112},{112,96},{1... | collective-permute-start | bytes 2064392 | tf_op jit(solution)/shard_map/ppermute | solution.py:369
  13.3 12.9 %collective-permute-start.4 = (f32[32,2944]{1,0:T(8,128)S(1)}, f32[32,2944]{1,0:T(8,128)S(1)}, u32[]{:S(2)}, u32[]{:S(2)}) collective-permute-start(f32[32,2944]{1,0:T(8,128)S(1)} %join.1.own.refs_1_.even_in), channel_id=1, source_target_pairs={{0,16},{16,0},{32,48},{48,32},{64,80},{80,64},{96,112},{112,96},{1... | collective-permute-start | bytes 1130504 | tf_op jit(solution)/shard_map/ppermute | solution.py:369
  13.9 17.1 %collective-permute-start.5 = (f32[32,2944]{1,0:T(8,128)S(1)}, f32[32,2944]{1,0:T(8,128)S(1)}, u32[]{:S(2)}, u32[]{:S(2)}) collective-permute-start(f32[32,2944]{1,0:T(8,128)S(1)} %join.1.own.refs_1_.even_in), channel_id=1, source_target_pairs={{16,32},{32,16},{48,64},{64,48},{80,96},{96,80},{112,128},{128,112... | collective-permute-start | bytes 1130504 | tf_op jit(solution)/shard_map/ppermute | solution.py:372
  18.4 17.9 %collective-permute-start.8 = (f32[32,5376]{1,0:T(8,128)S(1)}, f32[32,5376]{1,0:T(8,128)S(1)}, u32[]{:S(2)}, u32[]{:S(2)}) collective-permute-start(f32[32,5376]{1,0:T(8,128)S(1)} %collective-permute-done.even_in), channel_id=1, source_target_pairs={{16,32},{32,16},{48,64},{64,48},{80,96},{96,80},{112,128},{128,112... | collective-permute-start | bytes 2064392 | tf_op jit(solution)/shard_map/ppermute | solution.py:372
  24.4 8.2 %copy-start.5 = (bf16[768,256]{1,0:T(8,128)(2,1)S(1)}, bf16[768,256]{1,0:T(8,128)(2,1)}, u32[]{:S(2)}) copy-start(bf16[768,256]{1,0:T(8,128)(2,1)} %constant.17.clone.refs_11_) | copy-start | bytes 1179652
  24.4 8.2 %copy-start.6 = (bf16[768,256]{1,0:T(8,128)(2,1)S(1)}, bf16[768,256]{1,0:T(8,128)(2,1)}, u32[]{:S(2)}) copy-start(bf16[768,256]{1,0:T(8,128)(2,1)} %constant.16.clone.refs_10_) | copy-start | bytes 1179652
  24.4 8.2 %copy-start.8 = (bf16[384,256]{1,0:T(8,128)(2,1)S(1)}, bf16[384,256]{1,0:T(8,128)(2,1)}, u32[]{:S(2)}) copy-start(bf16[384,256]{1,0:T(8,128)(2,1)} %constant.19.clone.refs_13_) | copy-start | bytes 589828
  26.0 6.6 %copy-start.3 = (bf16[768,256]{1,0:T(8,128)(2,1)S(1)}, bf16[768,256]{1,0:T(8,128)(2,1)}, u32[]{:S(2)}) copy-start(bf16[768,256]{1,0:T(8,128)(2,1)} %constant.20.clone.refs_14_) | copy-start | bytes 1179652
  26.0 6.6 %copy-start.4 = (bf16[768,256]{1,0:T(8,128)(2,1)S(1)}, bf16[768,256]{1,0:T(8,128)(2,1)}, u32[]{:S(2)}) copy-start(bf16[768,256]{1,0:T(8,128)(2,1)} %constant.18.clone.refs_12_) | copy-start | bytes 1179652
  26.0 6.6 %copy-start.7 = (bf16[384,256]{1,0:T(8,128)(2,1)S(1)}, bf16[384,256]{1,0:T(8,128)(2,1)}, u32[]{:S(2)}) copy-start(bf16[384,256]{1,0:T(8,128)(2,1)} %constant.21.clone.refs_15_) | copy-start | bytes 589828
  26.1 11.9 %collective-permute-start.6 = (f32[32,5376]{1,0:T(8,128)S(1)}, f32[32,5376]{1,0:T(8,128)S(1)}, u32[]{:S(2)}, u32[]{:S(2)}) collective-permute-start(f32[32,5376]{1,0:T(8,128)S(1)} %get-tuple-element.18.refs_5_.own.refs_0_), channel_id=1, source_target_pairs={{0,16},{16,0},{32,48},{48,32},{64,80},{80,64},{96,112},{112,96},{1... | collective-permute-start | bytes 2064392 | tf_op jit(solution)/shard_map/ppermute | solution.py:369
  26.2 13.6 %collective-permute-start.9 = (f32[32,2944]{1,0:T(8,128)S(1)}, f32[32,2944]{1,0:T(8,128)S(1)}, u32[]{:S(2)}, u32[]{:S(2)}) collective-permute-start(f32[32,2944]{1,0:T(8,128)S(1)} %collective-permute-done.4.even_in), channel_id=1, source_target_pairs={{16,32},{32,16},{48,64},{64,48},{80,96},{96,80},{112,128},{128,112... | collective-permute-start | bytes 1130504 | tf_op jit(solution)/shard_map/ppermute | solution.py:372
  31.9 0.7 %copy-start.9 = (f32[5]{0:T(128)S(1)}, f32[5]{0:T(128)}, u32[]{:S(2)}) copy-start(f32[5]{0:T(128)} %param.11) | copy-start | bytes 64
  31.9 8.8 %collective-permute-start.7 = (f32[32,2944]{1,0:T(8,128)S(1)}, f32[32,2944]{1,0:T(8,128)S(1)}, u32[]{:S(2)}, u32[]{:S(2)}) collective-permute-start(f32[32,2944]{1,0:T(8,128)S(1)} %get-tuple-element.21.refs_9_.refs_1_), channel_id=1, source_target_pairs={{0,16},{16,0},{32,48},{48,32},{64,80},{80,64},{96,112},{112,96},{1... | collective-permute-start | bytes 1130504 | tf_op jit(solution)/shard_map/ppermute | solution.py:369
  36.3 1.6 %copy-start = (bf16[768,256]{1,0:T(8,128)(2,1)S(1)}, bf16[768,256]{1,0:T(8,128)(2,1)}, u32[]{:S(2)}) copy-start(bf16[768,256]{1,0:T(8,128)(2,1)} %constant.22.clone.high.refs_8_) | copy-start | bytes 1179652
  36.3 1.6 %copy-start.2 = (bf16[384,256]{1,0:T(8,128)(2,1)S(1)}, bf16[384,256]{1,0:T(8,128)(2,1)}, u32[]{:S(2)}) copy-start(bf16[384,256]{1,0:T(8,128)(2,1)} %constant.23.clone.low.refs_9_) | copy-start | bytes 589828

commit v8 on v7

--- a/solution.py
+++ b/solution.py
@@ -321,7 +321,7 @@
 
     with_neighbours(own, far, flipped, lambda odd: last_rows(own, even_in, odd, blocks))
     count = pairs - begin + 1
-    half = count // 2
+    half = 4
     pair_of = lambda slot: slot + begin - 1 if slot else 0
     for start, size, den, coa, at in ((0, half, den_two, coa_two, 0), (half, count - half, den_three, coa_three, 4)):
         finish(operand, (high, low), rows, start, size, levels[4:5, :], pair_of, part_sum, plane, den, coa)
@@ -464,7 +464,7 @@
         out_specs=(in_hbm,) * 2,
         scratch_shapes=[vmem(w) for w in widths]
         + [operand(count + 2)]
-        + [vmem(n * PAIR) for n in (count // 2, count // 2, count - count // 2, count - count // 2)]
+        + [vmem(n * PAIR) for n in (4, 4, count - 4, count - 4)]
         + [dma((8, rows // TILE))],
         compiler_params=room(16),
         name="coarse_two",

time: 42.9 us -> 42.8 us (level)
  no operation moved by 1% of the time
where the time goes in v8:
time: 42.8 us; the launch traced here: 42.5 us
  starting transfers between devices  26 us (61%)
  Pallas kernels  11.6 us (27%)
  waiting for transfers between devices  2.13 us (5%)
  local copies, waits for them, and re-layouts  1.88 us (4%)
  between operations  0.91 us (2%)
    ppermute x4, starting transfers between devices, odd_swap(): return lax.ppermute(values, 'rows', swaps(row_count, 1))  18.6 us
    ppermute x1, starting transfers between devices, on_device(): two = lax.ppermute(two, 'cols', swaps(col_count, 1))  5.66 us
    pallas_call x1, Pallas kernels, on_device(): pl.pallas_call(functools.partial(details_kernel, pairs, tuple((len(weight...  3.68 us
    pallas_call x2, Pallas kernels, smooth_rows(): pl.pallas_call(functools.partial(rows_kernel, group), out_shape=(array(wi...  2.54 us
    pallas_call x2, Pallas kernels, smooth_far(): pl.pallas_call(functools.partial(far_kernel, group, len(after)), out_shap...  2.44 us
    ppermute x4, waiting for transfers between devices, odd_swap(): return lax.ppermute(values, 'rows', swaps(row_count, 1))  2.11 us
    pallas_call x1, Pallas kernels, on_device(): pl.pallas_call(coarse_two_kernel, out_shape=(array(columns), array(column...  1.84 us
    unnamed x20, local copies, waits for them, and re-layouts  1.81 us
  transfers between devices with their start and end apart: 10, of which 2 were waited for; matrix products, arithmetic and copies ran while one was open for 0% of the time, Pallas kernels for 23%

profile of v8, /device:TPU:102, one launch (start us, length us, event | category | flops | bytes accessed | tf_op | source)
XLA Modules:
  0.0 42.5 jit_solution(12436065447725592255)
XLA Ops:
  0.6 0.0 copy-start.1
  0.6 1.2 %copy-done.1 = f32[32,8192]{1,0:T(8,128)S(1)} copy-done((f32[32,8192]{1,0:T(8,128)S(1)}, f32[32,8192]{1,0:T(8,128)}, u32[]{:S(2)}) %copy-start.1) | copy-done | bytes 1048600
  1.9 0.9 %collective-permute-start.2 = (f32[32,128]{1,0:T(8,128)S(1)}, f32[32,128]{1,0:T(8,128)S(1)}, u32[]{:S(2)}, u32[]{:S(2)}) collective-permute-start(f32[32,128]{1,0:T(8,128)S(1)} %get-tuple-element.19), channel_id=1, source_target_pairs={{0,1},{1,0},{2,3},{3,2},{4,5},{5,4},{6,7},{7,6},{8,9},{9,8},{10,11... | collective-permute-start | bytes 49160 | tf_op jit(solution)/shard_map/ppermute | solution.py:388
  2.8 5.7 %collective-permute-start.3 = (f32[32,128]{1,0:T(8,128)S(1)}, f32[32,128]{1,0:T(8,128)S(1)}, u32[]{:S(2)}, u32[]{:S(2)}) collective-permute-start(f32[32,128]{1,0:T(8,128)S(1)} %get-tuple-element.20), channel_id=1, source_target_pairs={{1,2},{2,1},{3,4},{4,3},{5,6},{6,5},{7,8},{8,7},{9,10},{10,9},{11,... | collective-permute-start | bytes 49160 | tf_op jit(solution)/shard_map/ppermute | solution.py:389
  8.5 4.6 %collective-permute-start.1 = (f32[32,5376]{1,0:T(8,128)S(1)}, f32[32,5376]{1,0:T(8,128)S(1)}, u32[]{:S(2)}, u32[]{:S(2)}) collective-permute-start(f32[32,5376]{1,0:T(8,128)S(1)} %get-tuple-element.17.own.even_in.refs_0_), channel_id=1, source_target_pairs={{16,32},{32,16},{48,64},{64,48},{80,96},{96,80},{112,128},{128,112... | collective-permute-start | bytes 2064392 | tf_op jit(solution)/shard_map/ppermute | solution.py:372
  13.1 0.1 collective-permute-start
  13.2 0.0 collective-permute-done.2.first
  13.3 0.0 collective-permute-done.3.second
  13.3 0.6 %collective-permute-start.4 = (f32[32,2944]{1,0:T(8,128)S(1)}, f32[32,2944]{1,0:T(8,128)S(1)}, u32[]{:S(2)}, u32[]{:S(2)}) collective-permute-start(f32[32,2944]{1,0:T(8,128)S(1)} %join.1.own.refs_1_.even_in), channel_id=1, source_target_pairs={{0,16},{16,0},{32,48},{48,32},{64,80},{80,64},{96,112},{112,96},{1... | collective-permute-start | bytes 1130504 | tf_op jit(solution)/shard_map/ppermute | solution.py:369
  13.9 4.5 %collective-permute-start.5 = (f32[32,2944]{1,0:T(8,128)S(1)}, f32[32,2944]{1,0:T(8,128)S(1)}, u32[]{:S(2)}, u32[]{:S(2)}) collective-permute-start(f32[32,2944]{1,0:T(8,128)S(1)} %join.1.own.refs_1_.even_in), channel_id=1, source_target_pairs={{16,32},{32,16},{48,64},{64,48},{80,96},{96,80},{112,128},{128,112... | collective-permute-start | bytes 1130504 | tf_op jit(solution)/shard_map/ppermute | solution.py:372
  18.4 0.0 collective-permute-done.even_in
  18.4 4.6 %collective-permute-start.8 = (f32[32,5376]{1,0:T(8,128)S(1)}, f32[32,5376]{1,0:T(8,128)S(1)}, u32[]{:S(2)}, u32[]{:S(2)}) collective-permute-start(f32[32,5376]{1,0:T(8,128)S(1)} %collective-permute-done.even_in), channel_id=1, source_target_pairs={{16,32},{32,16},{48,64},{64,48},{80,96},{96,80},{112,128},{128,112... | collective-permute-start | bytes 2064392 | tf_op jit(solution)/shard_map/ppermute | solution.py:372
  23.1 1.3 %collective-permute-done.1.odd_in.own = f32[32,5376]{1,0:T(8,128)S(1)} collective-permute-done((f32[32,5376]{1,0:T(8,128)S(1)}, f32[32,5376]{1,0:T(8,128)S(1)}, u32[]{:S(2)}, u32[]{:S(2)}) %collective-permute-start.1) | collective-permute-done | bytes 688160 | tf_op jit(solution)/shard_map/ppermute | solution.py:372
  24.4 0.0 copy-start.5
  24.4 0.0 copy-start.6
  24.4 0.0 copy-start.8
  24.4 1.6 %rows_one.1 = (f32[32,5376]{1,0:T(8,128)S(1)}, f32[32,5376]{1,0:T(8,128)S(1)}, f32[32,5376]{1,0:T(8,128)S(1)}, f32[32,5376]{1,0:T(8,128)S(1)}) custom-call(f32[32,5376]{1,0:T(8,128)S(1)} %get-tuple-element.17.own.even_in.refs_0_, f32[32,5376]{1,0:T(8,128)S(1)} %collective-permute-done.even_in, f32[32,5376]{1,0:T(8,128)S(1)} %collective-permute-done.1.odd_in.own), custom_call_target="tpu_custom_call" | custom-call | tf_op jit(solution)/shard_map/rows_one/pallas_call | solution.py:408
  26.0 0.0 copy-start.3
  26.0 0.0 copy-start.4
  26.0 0.0 copy-start.7
  26.1 0.1 collective-permute-start.6
  26.2 0.0 collective-permute-done.4.even_in
  26.2 4.8 %collective-permute-start.9 = (f32[32,2944]{1,0:T(8,128)S(1)}, f32[32,2944]{1,0:T(8,128)S(1)}, u32[]{:S(2)}, u32[]{:S(2)}) collective-permute-start(f32[32,2944]{1,0:T(8,128)S(1)} %collective-permute-done.4.even_in), channel_id=1, source_target_pairs={{16,32},{32,16},{48,64},{64,48},{80,96},{96,80},{112,128},{128,112... | collective-permute-start | bytes 1130504 | tf_op jit(solution)/shard_map/ppermute | solution.py:372
  30.9 0.0 collective-permute-done.5.odd_in.own
  31.0 0.9 %rows_two.1 = (f32[32,2944]{1,0:T(8,128)S(1)}, f32[32,2944]{1,0:T(8,128)S(1)}, f32[32,2944]{1,0:T(8,128)S(1)}, f32[32,2944]{1,0:T(8,128)S(1)}) custom-call(f32[32,2944]{1,0:T(8,128)S(1)} %join.1.own.refs_1_.even_in, f32[32,2944]{1,0:T(8,128)S(1)} %collective-permute-done.4.even_in, f32[32,2944]{1,0:T(8,128)S(1)} %collective-permute-done.5.odd_in.own), custom_call_target="tpu_custom_call" | custom-call | tf_op jit(solution)/shard_map/rows_two/pallas_call | solution.py:408
  31.9 0.0 copy-start.9
  31.9 0.1 collective-permute-start.7
  32.0 0.5 %copy-done.9 = f32[5]{0:T(128)S(1)} copy-done((f32[5]{0:T(128)S(1)}, f32[5]{0:T(128)}, u32[]{:S(2)}) %copy-start.9) | copy-done | bytes 44
  32.5 0.1 broadcast_in_dim.2.levels
  32.6 0.0 copy-done.5
  32.6 0.0 copy-done.6
  32.6 0.0 copy-done.8
  32.6 0.0 copy-done.3
  32.6 0.0 copy-done.4
  32.6 0.0 copy-done.7
  32.6 3.7 %details.1 = (f32[32,8192]{1,0:T(8,128)S(1)}, f32[32,8192]{1,0:T(8,128)S(1)}) custom-call(f32[5,256]{1,0:T(8,128)S(1)} %broadcast_in_dim.2.levels, f32[32,5376]{1,0:T(8,128)S(1)} %get-tuple-element.17.own.even_in.refs_0_, f32[32,2944]{1,0:T(8,128)S(1)} %join.1.own.refs_1_.even_in, f32[32,5376]{1,0:T(8,128)S(1)} %get-tuple-element.22.refs_2_, ...), custom_call_target="tpu_custom_call" | custom-call | tf_op jit(solution)/shard_map/details/pallas_call | solution.py:426
  36.3 0.0 copy-start
  36.3 0.0 copy-start.2
  36.3 0.0 collective-permute-done.8.odd_in
  36.3 1.6 %far_one.1.odd_in.refs_4_ = f32[32,5376]{1,0:T(8,128)S(1)} custom-call(f32[32,5376]{1,0:T(8,128)S(1)} %collective-permute-done.1.odd_in.own, f32[32,5376]{1,0:T(8,128)S(1)} %get-tuple-element.17.own.even_in.refs_0_, f32[32,5376]{1,0:T(8,128)S(1)} %collective-permute-done.8.odd_in), custom_call_target="tpu_custom_call" | custom-call | tf_op jit(solution)/shard_map/far_one/pallas_call | solution.py:437
  37.9 0.0 collective-permute-done.6.even_in.refs_2_
  37.9 0.0 copy-done
  38.0 0.0 copy-done.2
  38.0 1.0 %coarse_one.1 = (f32[32,4864]{1,0:T(8,128)S(1)}, f32[32,4864]{1,0:T(8,128)S(1)}) custom-call(f32[5,256]{1,0:T(8,128)S(1)} %broadcast_in_dim.2.levels, f32[32,5376]{1,0:T(8,128)S(1)} %get-tuple-element.18.refs_5_.own.refs_0_, f32[32,5376]{1,0:T(8,128)S(1)} %collective-permute-done.6.even_in.refs_2_, f32[32,5376]{1,0:T(8,128)S(1)} %far_one.1.odd_in.refs_4_, ...), custom_call_target="tpu_custom_call" | custom-call | tf_op jit(solution)/shard_map/coarse_one/pallas_call | solution.py:449
  39.0 0.8 %collective-permute-done.9.odd_in = f32[32,2944]{1,0:T(8,128)S(1)} collective-permute-done((f32[32,2944]{1,0:T(8,128)S(1)}, f32[32,2944]{1,0:T(8,128)S(1)}, u32[]{:S(2)}, u32[]{:S(2)}) %collective-permute-start.9) | collective-permute-done | bytes 376864 | tf_op jit(solution)/shard_map/ppermute | solution.py:372
  39.8 0.8 %far_two.1.refs_5_ = f32[32,2944]{1,0:T(8,128)S(1)} custom-call(f32[32,2944]{1,0:T(8,128)S(1)} %collective-permute-done.5.odd_in.own, f32[32,2944]{1,0:T(8,128)S(1)} %join.1.own.refs_1_.even_in, f32[32,2944]{1,0:T(8,128)S(1)} %collective-permute-done.9.odd_in, f32[32,4864]{1,0:T(8,128)S(1)} %get-tuple-element.30.refs_0_.refs_10_), custom_call_target="tpu_custom_call" | custom-call | tf_op jit(solution)/shard_map/far_two/pallas_call | solution.py:437
  40.7 0.0 collective-permute-done.7.refs_3_
  40.7 1.8 %coarse_two.1 = (f32[32,8192]{1,0:T(8,128)}, f32[32,8192]{1,0:T(8,128)}) custom-call(f32[5,256]{1,0:T(8,128)S(1)} %broadcast_in_dim.2.levels, f32[32,5376]{1,0:T(8,128)S(1)} %get-tuple-element.18.refs_5_.own.refs_0_, f32[32,2944]{1,0:T(8,128)S(1)} %get-tuple-element.21.refs_9_.refs_1_, f32[32,5376]{1,0:T(8,128)S(1)} %collective-permute-done.6.even_in.refs_2_, ...), custom_call_target="tpu_custom_call" | custom-call | tf_op jit(solution)/shard_map/coarse_two/pallas_call | solution.py:460
  (2 shorter events, 0.1 us)
Async XLA Ops:
  0.6 1.2 %copy-start.1 = (f32[32,8192]{1,0:T(8,128)S(1)}, f32[32,8192]{1,0:T(8,128)}, u32[]{:S(2)}) copy-start(f32[32,8192]{1,0:T(8,128)} %sky.3) | copy-start | bytes 3145732
  1.9 11.3 %collective-permute-start.2 = (f32[32,128]{1,0:T(8,128)S(1)}, f32[32,128]{1,0:T(8,128)S(1)}, u32[]{:S(2)}, u32[]{:S(2)}) collective-permute-start(f32[32,128]{1,0:T(8,128)S(1)} %get-tuple-element.19), channel_id=1, source_target_pairs={{0,1},{1,0},{2,3},{3,2},{4,5},{5,4},{6,7},{7,6},{8,9},{9,8},{10,11... | collective-permute-start | bytes 49160 | tf_op jit(solution)/shard_map/ppermute | solution.py:388
  2.8 10.4 %collective-permute-start.3 = (f32[32,128]{1,0:T(8,128)S(1)}, f32[32,128]{1,0:T(8,128)S(1)}, u32[]{:S(2)}, u32[]{:S(2)}) collective-permute-start(f32[32,128]{1,0:T(8,128)S(1)} %get-tuple-element.20), channel_id=1, source_target_pairs={{1,2},{2,1},{3,4},{4,3},{5,6},{6,5},{7,8},{8,7},{9,10},{10,9},{11,... | collective-permute-start | bytes 49160 | tf_op jit(solution)/shard_map/ppermute | solution.py:389
  8.5 15.9 %collective-permute-start.1 = (f32[32,5376]{1,0:T(8,128)S(1)}, f32[32,5376]{1,0:T(8,128)S(1)}, u32[]{:S(2)}, u32[]{:S(2)}) collective-permute-start(f32[32,5376]{1,0:T(8,128)S(1)} %get-tuple-element.17.own.even_in.refs_0_), channel_id=1, source_target_pairs={{16,32},{32,16},{48,64},{64,48},{80,96},{96,80},{112,128},{128,112... | collective-permute-start | bytes 2064392 | tf_op jit(solution)/shard_map/ppermute | solution.py:372
  13.1 5.3 %collective-permute-start = (f32[32,5376]{1,0:T(8,128)S(1)}, f32[32,5376]{1,0:T(8,128)S(1)}, u32[]{:S(2)}, u32[]{:S(2)}) collective-permute-start(f32[32,5376]{1,0:T(8,128)S(1)} %get-tuple-element.17.own.even_in.refs_0_), channel_id=1, source_target_pairs={{0,16},{16,0},{32,48},{48,32},{64,80},{80,64},{96,112},{112,96},{1... | collective-permute-start | bytes 2064392 | tf_op jit(solution)/shard_map/ppermute | solution.py:369
  13.3 12.9 %collective-permute-start.4 = (f32[32,2944]{1,0:T(8,128)S(1)}, f32[32,2944]{1,0:T(8,128)S(1)}, u32[]{:S(2)}, u32[]{:S(2)}) collective-permute-start(f32[32,2944]{1,0:T(8,128)S(1)} %join.1.own.refs_1_.even_in), channel_id=1, source_target_pairs={{0,16},{16,0},{32,48},{48,32},{64,80},{80,64},{96,112},{112,96},{1... | collective-permute-start | bytes 1130504 | tf_op jit(solution)/shard_map/ppermute | solution.py:369
  13.9 17.1 %collective-permute-start.5 = (f32[32,2944]{1,0:T(8,128)S(1)}, f32[32,2944]{1,0:T(8,128)S(1)}, u32[]{:S(2)}, u32[]{:S(2)}) collective-permute-start(f32[32,2944]{1,0:T(8,128)S(1)} %join.1.own.refs_1_.even_in), channel_id=1, source_target_pairs={{16,32},{32,16},{48,64},{64,48},{80,96},{96,80},{112,128},{128,112... | collective-permute-start | bytes 1130504 | tf_op jit(solution)/shard_map/ppermute | solution.py:372
  18.4 17.9 %collective-permute-start.8 = (f32[32,5376]{1,0:T(8,128)S(1)}, f32[32,5376]{1,0:T(8,128)S(1)}, u32[]{:S(2)}, u32[]{:S(2)}) collective-permute-start(f32[32,5376]{1,0:T(8,128)S(1)} %collective-permute-done.even_in), channel_id=1, source_target_pairs={{16,32},{32,16},{48,64},{64,48},{80,96},{96,80},{112,128},{128,112... | collective-permute-start | bytes 2064392 | tf_op jit(solution)/shard_map/ppermute | solution.py:372
  24.4 8.2 %copy-start.5 = (bf16[768,256]{1,0:T(8,128)(2,1)S(1)}, bf16[768,256]{1,0:T(8,128)(2,1)}, u32[]{:S(2)}) copy-start(bf16[768,256]{1,0:T(8,128)(2,1)} %constant.17.clone.refs_11_) | copy-start | bytes 1179652
  24.4 8.2 %copy-start.6 = (bf16[768,256]{1,0:T(8,128)(2,1)S(1)}, bf16[768,256]{1,0:T(8,128)(2,1)}, u32[]{:S(2)}) copy-start(bf16[768,256]{1,0:T(8,128)(2,1)} %constant.16.clone.refs_10_) | copy-start | bytes 1179652
  24.4 8.2 %copy-start.8 = (bf16[384,256]{1,0:T(8,128)(2,1)S(1)}, bf16[384,256]{1,0:T(8,128)(2,1)}, u32[]{:S(2)}) copy-start(bf16[384,256]{1,0:T(8,128)(2,1)} %constant.19.clone.refs_13_) | copy-start | bytes 589828
  26.0 6.6 %copy-start.3 = (bf16[768,256]{1,0:T(8,128)(2,1)S(1)}, bf16[768,256]{1,0:T(8,128)(2,1)}, u32[]{:S(2)}) copy-start(bf16[768,256]{1,0:T(8,128)(2,1)} %constant.20.clone.refs_14_) | copy-start | bytes 1179652
  26.0 6.6 %copy-start.4 = (bf16[768,256]{1,0:T(8,128)(2,1)S(1)}, bf16[768,256]{1,0:T(8,128)(2,1)}, u32[]{:S(2)}) copy-start(bf16[768,256]{1,0:T(8,128)(2,1)} %constant.18.clone.refs_12_) | copy-start | bytes 1179652
  26.0 6.6 %copy-start.7 = (bf16[384,256]{1,0:T(8,128)(2,1)S(1)}, bf16[384,256]{1,0:T(8,128)(2,1)}, u32[]{:S(2)}) copy-start(bf16[384,256]{1,0:T(8,128)(2,1)} %constant.21.clone.refs_15_) | copy-start | bytes 589828
  26.1 11.9 %collective-permute-start.6 = (f32[32,5376]{1,0:T(8,128)S(1)}, f32[32,5376]{1,0:T(8,128)S(1)}, u32[]{:S(2)}, u32[]{:S(2)}) collective-permute-start(f32[32,5376]{1,0:T(8,128)S(1)} %get-tuple-element.18.refs_5_.own.refs_0_), channel_id=1, source_target_pairs={{0,16},{16,0},{32,48},{48,32},{64,80},{80,64},{96,112},{112,96},{1... | collective-permute-start | bytes 2064392 | tf_op jit(solution)/shard_map/ppermute | solution.py:369
  26.2 13.6 %collective-permute-start.9 = (f32[32,2944]{1,0:T(8,128)S(1)}, f32[32,2944]{1,0:T(8,128)S(1)}, u32[]{:S(2)}, u32[]{:S(2)}) collective-permute-start(f32[32,2944]{1,0:T(8,128)S(1)} %collective-permute-done.4.even_in), channel_id=1, source_target_pairs={{16,32},{32,16},{48,64},{64,48},{80,96},{96,80},{112,128},{128,112... | collective-permute-start | bytes 1130504 | tf_op jit(solution)/shard_map/ppermute | solution.py:372
  31.9 0.7 %copy-start.9 = (f32[5]{0:T(128)S(1)}, f32[5]{0:T(128)}, u32[]{:S(2)}) copy-start(f32[5]{0:T(128)} %param.11) | copy-start | bytes 64
  31.9 8.8 %collective-permute-start.7 = (f32[32,2944]{1,0:T(8,128)S(1)}, f32[32,2944]{1,0:T(8,128)S(1)}, u32[]{:S(2)}, u32[]{:S(2)}) collective-permute-start(f32[32,2944]{1,0:T(8,128)S(1)} %get-tuple-element.21.refs_9_.refs_1_), channel_id=1, source_target_pairs={{0,16},{16,0},{32,48},{48,32},{64,80},{80,64},{96,112},{112,96},{1... | collective-permute-start | bytes 1130504 | tf_op jit(solution)/shard_map/ppermute | solution.py:369
  36.3 1.6 %copy-start = (bf16[768,256]{1,0:T(8,128)(2,1)S(1)}, bf16[768,256]{1,0:T(8,128)(2,1)}, u32[]{:S(2)}) copy-start(bf16[768,256]{1,0:T(8,128)(2,1)} %constant.22.clone.high.refs_8_) | copy-start | bytes 1179652
  36.3 1.6 %copy-start.2 = (bf16[384,256]{1,0:T(8,128)(2,1)S(1)}, bf16[384,256]{1,0:T(8,128)(2,1)}, u32[]{:S(2)}) copy-start(bf16[384,256]{1,0:T(8,128)(2,1)} %constant.23.clone.low.refs_9_) | copy-start | bytes 589828
